TPU v7x, 32 devices: a whole 2x2x4 slice. The times are simulated.
32 devices in a mesh: shift: 4 (over z), leaf: 8 (over y, x, core).
Axes of the slice: x: 2, y: 2, z: 4, core: 2. Of those that a mesh axis runs over, the one named last changes fastest.
Arguments:
- leaf_rhs: bfloat16 [8, 1024, 1024], P('leaf'), may hold values from -6 to 6
- leaf_inverse: bfloat16 [4, 8, 1024, 1024], P('shift', 'leaf')
- leaf_coupling: bfloat16 [4, 8, 1024, 384], P('shift', 'leaf'), may hold values from -0.1875 to 0.1875
- leaf_rows: int32 [8, 384], P('leaf'), may hold values from 0 to 767, as said below
- front_sizes: int32 [3], replicated, may hold values from 384 to 768, as said below
- front_inverse: bfloat16 [4, 3, 8, 768, 768], P('shift', None, 'leaf'), as said below
- front_coupling: bfloat16 [4, 2, 8, 768, 768], P('shift', None, 'leaf'), as said below
- shift_weight: float32 [4], P('shift'), may hold values from -1 to 1
Outputs:
- filtered: float32 [8, 1024, 1024], P('leaf', 'shift')
Inputs may be any that keep to these rules, and one draw needn't show every extreme that they name: `leaf_rows`: the 384 entries of one leaf are distinct. `front_sizes`: the front of at least one level is full. `front_inverse`: all leaves below one separator hold the same front inverse for it. `front_coupling`: all leaves below one separator hold the same coupling for it.
All inputs are finite; a program needn't handle non-finite values.
Results may differ from a plain program's by a relative error of at most 0.01.
Values may be sent and summed in bfloat16 or wider, within the bound.
No kernel may reach another device: no remote copies, remote signals or barrier semaphores. Data moves between devices by JAX's collectives and lax.ppermute only.
A program may use at most 128 MiB of HBM per device.

v0:
```python
import jax
import jax.numpy as jnp
from jax import lax
from jax.sharding import PartitionSpec as P


def partner_2(value, axis, stride):
    mask = 2**stride
    pairs = [(source, source ^ mask) for source in range(lax.axis_size(axis))]
    return lax.ppermute(value, axis, pairs)


def transposed(left_matrix, right_matrix):
    return lax.dot_general(
        left_matrix, right_matrix, (((0,), (0,)), ((), ())), preferred_element_type=jnp.float32
    )


def widen(solved, bit_index, position):
    partner = partner_2(solved, "leaf", bit_index)
    own_bit = position >> bit_index & 1
    lower = jnp.where(own_bit == 0, solved, partner)
    upper = jnp.where(own_bit == 0, partner, solved)
    return jnp.concatenate([lower, upper], axis=1)


def body(
    leaf_rhs,
    leaf_inverse,
    leaf_coupling,
    leaf_rows,
    front_sizes,
    front_inverse,
    front_coupling,
    shift_weight,
):
    levels = lax.axis_size("leaf").bit_length() - 1
    position = lax.axis_index("leaf")
    inverse = leaf_inverse[0, 0]
    coupling = leaf_coupling[0, 0]
    front = front_inverse.shape[-1]
    selector = (leaf_rows[0][:, None] == jnp.arange(front, dtype=jnp.int32)[None, :]).astype(
        jnp.bfloat16
    )
    spread = jnp.dot(coupling, selector, preferred_element_type=jnp.float32).astype(jnp.bfloat16)
    front_index = jnp.arange(front, dtype=jnp.int32)[:, None]
    leaf_half = jnp.dot(inverse, leaf_rhs[0], preferred_element_type=jnp.float32).astype(
        jnp.bfloat16
    )
    carried = transposed(spread, leaf_half)
    solved_list = []
    halving_list = []
    for level_index in range(levels):
        columns = carried.shape[1]
        own_bit = position >> level_index & 1
        retained = lax.dynamic_slice_in_dim(carried, own_bit * (columns // 2), columns // 2, 1)
        outgoing = lax.dynamic_slice_in_dim(
            carried, (1 - own_bit) * (columns // 2), columns // 2, 1
        )
        summed = retained + partner_2(outgoing, "leaf", level_index)
        live_rows = front_index < front_sizes[level_index]
        operand = jnp.where(live_rows, summed, 0.0).astype(jnp.bfloat16)
        solved = jnp.where(
            live_rows,
            jnp.dot(front_inverse[0, level_index, 0], operand, preferred_element_type=jnp.float32),
            0.0,
        ).astype(jnp.bfloat16)
        solved_list.append(solved)
        halving_list.append(True)
        if level_index < levels - 1:
            carried = transposed(front_coupling[0, level_index, 0], solved)
    current = solved_list[-1]
    for level_index in range(levels - 2, -1, -1):
        current = widen(current, level_index + 1, position)
        lifted_up = jnp.dot(
            front_coupling[0, level_index, 0], current, preferred_element_type=jnp.float32
        ).astype(jnp.bfloat16)
        correction = jnp.dot(
            front_inverse[0, level_index, 0], lifted_up, preferred_element_type=jnp.float32
        )
        live_rows = front_index < front_sizes[level_index]
        current = jnp.where(
            live_rows, solved_list[level_index].astype(jnp.float32) - correction, 0.0
        ).astype(jnp.bfloat16)
    current = widen(current, 0, position)
    lifted = jnp.dot(spread, current, preferred_element_type=jnp.float32).astype(jnp.bfloat16)
    weight = shift_weight[0]
    weighted = weight * (
        leaf_half.astype(jnp.float32) - jnp.dot(inverse, lifted, preferred_element_type=jnp.float32)
    )
    result = lax.psum_scatter(weighted, "shift", scatter_dimension=0, tiled=True)
    return result[None]


def solution(mesh):
    in_specs = (
        P("leaf", None, None),
        P("shift", "leaf", None, None),
        P("shift", "leaf", None, None),
        P("leaf", None),
        P(),
        P("shift", None, "leaf", None, None),
        P("shift", None, "leaf", None, None),
        P("shift"),
    )
    out_specs = P("leaf", "shift", None)
    return jax.shard_map(body, mesh=mesh, in_specs=in_specs, out_specs=out_specs, check_vma=False)
```

profile of v0, /device:TPU:0, one launch (start us, length us, event | category | flops | bytes accessed | tf_op | source)
XLA Modules:
  0.0 183.3 jit_solution(15963516456378621519)
XLA Ops:
  6.5 0.8 reduce
  7.4 0.8 copy-done
  8.1 4.0 %fusion.6 = bf16[1024,1024]{1,0:T(8,128)(2,1)S(1)} fusion(bf16[1,1024,1024]{2,1,0:T(8,128)(2,1)} %param.8, bf16[1,1,1024,1024]{3,2,1,0:T(8,128)(2,1)S(1)} %copy-done), kind=kOutput, calls=%fused_computation.7 | convolution fusion | flops 2148532224 | bytes 6291456 | tf_op jit(solution)/shard_map/dot_general | solution.py:47
  12.2 1.2 convolution_convert_fusion
  13.3 1.8 fusion.95
  15.2 1.6 constant_dynamic-slice_fusion
  16.8 0.7 copy-done.1
  17.9 0.6 fusion.94
  18.5 0.6 iota_compare_fusion.3
  19.2 2.1 %collective-permute-done = f32[768,512]{1,0:T(8,128)} collective-permute-done((f32[768,512]{1,0:T(8,128)}, f32[768,512]{1,0:T(8,128)}, u32[]{:S(2)}, u32[]{:S(2)}) %collective-permute-start) | collective-permute-done | bytes 1572896 | tf_op jit(solution)/shard_map/ppermute | solution.py:10
  21.3 3.2 %select_convert_fusion.1 = bf16[512,768]{1,0:T(8,128)(2,1)S(1)} fusion(bf16[1,3,1,768,768]{4,3,2,1,0:T(8,128)(2,1)} %param.13, f32[768,512]{1,0:T(8,128)} %collective-permute-done, f32[768,1024]{1,0:T(8,128)} %copy-done.1, s32[]{:T(128)S(6)} %select_n.85, pred[768]{0:T(1024)(128)(4,1)S(1)} %iota_compare_fusion.3), kind=kOutput, calls=%fused_computation.14 | convolution fusion | flops 605945856 | bytes 5113860 | tf_op jit(solution)/shard_map/dot_general | solution.py:65
  24.5 0.8 fusion.28
  25.4 1.2 copy-done.4
  26.6 2.9 %collective-permute-start.1 = (f32[768,256]{0,1:T(8,128)S(1)}, f32[768,256]{0,1:T(8,128)}, u32[]{:S(2)}, u32[]{:S(2)}) collective-permute-start(f32[768,256]{0,1:T(8,128)S(1)} %dynamic-slice_bitcast_fusion), channel_id=1, source_target_pairs={{0,2},{1,3},{2,0},{3,1},{4,6},{5,7},{6,4},{7,5},{8,10},{9,11},{10,... | collective-permute-start | bytes 2359304 | tf_op jit(solution)/shard_map/ppermute | solution.py:10
  30.2 17.3 %collective-permute-done.1 = f32[768,256]{0,1:T(8,128)} collective-permute-done((f32[768,256]{0,1:T(8,128)S(1)}, f32[768,256]{0,1:T(8,128)}, u32[]{:S(2)}, u32[]{:S(2)}) %collective-permute-start.1) | collective-permute-done | bytes 786464 | tf_op jit(solution)/shard_map/ppermute | solution.py:10
  47.5 2.3 %fusion.17 = bf16[256,768]{1,0:T(8,128)(2,1)S(1)} fusion(bf16[1,3,1,768,768]{4,3,2,1,0:T(8,128)(2,1)} %param.13, f32[768,256]{0,1:T(8,128)} %collective-permute-done.1, f32[512,768]{1,0:T(8,128)} %copy-done.4, s32[]{:T(128)S(6)} %select_n.90, pred[768]{0:T(1024)(128)(4,1)S(1)} %iota_compare_fusion.2), kind=kOutput, calls=%fused_computation.21 | convolution fusion | flops 302972928 | bytes 3147780 | tf_op jit(solution)/shard_map/dot_general | solution.py:65
  50.3 0.8 dynamic-slice_bitcast_fusion.1
  51.1 1.8 collective-permute-start.2
  52.8 0.6 iota_compare_fusion.1
  53.5 8.6 %collective-permute-done.2 = f32[768,128]{0,1:T(8,128)} collective-permute-done((f32[768,128]{0,1:T(8,128)}, f32[768,128]{0,1:T(8,128)}, u32[]{:S(2)}, u32[]{:S(2)}) %collective-permute-start.2) | collective-permute-done | bytes 393248 | tf_op jit(solution)/shard_map/ppermute | solution.py:10
  62.0 1.9 %fusion.37 = bf16[768,128]{0,1:T(8,128)(2,1)S(1)} fusion(bf16[1,3,1,768,768]{4,3,2,1,0:T(8,128)(2,1)} %param.13, f32[768,128]{0,1:T(8,128)} %collective-permute-done.2, f32[256,768]{1,0:T(8,128)S(1)} %fusion.23, s32[]{:T(128)S(6)} %select_n.95, pred[768]{0:T(1024)(128)(4,1)S(1)} %iota_compare_fusion.1), kind=kOutput, calls=%fused_computation.41 | convolution fusion | flops 151486464 | bytes 2164740 | tf_op jit(solution)/shard_map/dot_general | solution.py:65
  64.0 1.5 collective-permute-start.3
  65.5 4.2 %collective-permute-done.3 = bf16[768,128]{0,1:T(8,128)(2,1)S(1)} collective-permute-done((bf16[768,128]{0,1:T(8,128)(2,1)S(1)}, bf16[768,128]{0,1:T(8,128)(2,1)S(1)}, u32[]{:S(2)}, u32[]{:S(2)}) %collective-permute-start.3) | collective-permute-done | bytes 196640 | tf_op jit(solution)/shard_map/ppermute | solution.py:10
  69.7 2.6 %fusion.19 = bf16[768,256]{0,1:T(8,128)(2,1)S(1)} fusion(bf16[1,2,1,768,768]{4,3,2,1,0:T(8,128)(2,1)} %param.14, bf16[1,3,1,768,768]{4,3,2,1,0:T(8,128)(2,1)} %param.13, bf16[256,768]{1,0:T(8,128)(2,1)S(1)} %fusion.17, bf16[768,128]{0,1:T(8,128)(2,1)S(1)} %get-tuple-element.10, bf16[768,128]{0,1:T(8,128)(2,1)S(1)} %get-tuple-element.9, ...), kind=kOutput, calls=%fused_computation.25 | convolution fusion | flops 605749248 | bytes 3539712 | tf_op jit(solution)/shard_map/dot_general | solution.py:78
  72.3 1.5 collective-permute-start.4
  73.8 7.2 %collective-permute-done.4 = bf16[768,256]{0,1:T(8,128)(2,1)S(1)} collective-permute-done((bf16[768,256]{0,1:T(8,128)(2,1)S(1)}, bf16[768,256]{0,1:T(8,128)(2,1)S(1)}, u32[]{:S(2)}, u32[]{:S(2)}) %collective-permute-start.4) | collective-permute-done | bytes 393248 | tf_op jit(solution)/shard_map/ppermute | solution.py:10
  81.0 0.8 broadcast_select_fusion.3
  81.8 3.5 %fusion.15 = bf16[768,512]{0,1:T(8,128)(2,1)S(1)} fusion(bf16[512,768]{1,0:T(8,128)(2,1)} %copy-done.7, bf16[1,3,1,768,768]{4,3,2,1,0:T(8,128)(2,1)} %param.13, bf16[1,2,1,768,768]{4,3,2,1,0:T(8,128)(2,1)} %param.14, bf16[768,256]{0,1:T(8,128)(2,1)} %get-tuple-element.8, bf16[768,256]{0,1:T(8,128)(2,1)S(1)} %get-tuple-element.7, ...), kind=kOutput, calls=%fused_computation.17 | convolution fusion | flops 1211498496 | bytes 4719360 | tf_op jit(solution)/shard_map/dot_general | solution.py:78
  86.0 1.8 collective-permute-done.5
  87.8 2.4 %broadcast_select_fusion.1 = (bf16[768,512]{0,1:T(8,128)(2,1)}, bf16[768,512]{0,1:T(8,128)(2,1)}) fusion(bf16[768,512]{0,1:T(8,128)(2,1)S(1)} %fusion.15, bf16[768,512]{0,1:T(8,128)(2,1)} %collective-permute-done.5, pred[]{:T(512)S(6)} %eq.31), kind=kLoop, calls=%fused_computation.61 | loop fusion | flops 786432 | bytes 3145729 | tf_op jit(solution)/shard_map/jit(_where)/select_n | solution.py:22
  90.1 8.6 %fusion = f32[1024,1024]{1,0:T(8,128)} fusion(bf16[1024,1024]{1,0:T(8,128)(2,1)} %copy-done.9, bf16[1,1,1024,1024]{3,2,1,0:T(8,128)(2,1)S(1)} %copy-done, f32[]{:T(128)} %bitcast.83, bf16[768,1024]{1,0:T(8,128)(2,1)} %copy-done.8, bf16[768,512]{0,1:T(8,128)(2,1)} %get-tuple-element.6, bf16[768,512]{0,1:T(8,128)(2,1)} %get-tuple-element.5), kind=kOutput, calls=%fused_computation.1 | convolution fusion | flops 3765436416 | bytes 11534340 | tf_op jit(solution)/shard_map/dot_general | solution.py:89
  98.7 77.8 %reduce-scatter.2.cloned.1.call-done = f32[256,1024]{1,0:T(8,128)} async-done(((f32[1024,1024]{1,0:T(8,128)}), f32[256,1024]{1,0:T(8,128)}) %reduce-scatter.2.cloned.1.call-update) | async-done | bytes 1048592 | tf_op jit(solution)/shard_map/reduce_scatter | solution.py:91
  (25 shorter events, 1.8 us)
Async XLA Ops:
  6.5 1.6 copy-start
  6.5 170.0 %reduce-scatter.2.cloned.1.call-start = ((), (), s32[]{:S(2)}) async-start(), calls=%async_computation.1 | async-start | bytes 5242880 | tf_op jit(solution)/shard_map/reduce_scatter | solution.py:91
  8.1 4.0 %copy-start.6 = (bf16[1,1,1024,384]{3,2,1,0:T(8,128)(2,1)S(1)}, bf16[1,1,1024,384]{3,2,1,0:T(8,128)(2,1)}, u32[]{:S(2)}) copy-start(bf16[1,1,1024,384]{3,2,1,0:T(8,128)(2,1)} %param.10) | copy-start | bytes 2359300
  12.2 3.0 %copy-start.9 = (bf16[1024,1024]{1,0:T(8,128)(2,1)}, bf16[1024,1024]{1,0:T(8,128)(2,1)S(1)}, u32[]{:S(2)}) copy-start(bf16[1024,1024]{1,0:T(8,128)(2,1)S(1)} %fusion.6) | copy-start | bytes 6291460
  13.3 1.8 %copy-start.8 = (bf16[768,1024]{1,0:T(8,128)(2,1)}, bf16[768,1024]{1,0:T(8,128)(2,1)S(1)}, u32[]{:S(2)}) copy-start(bf16[768,1024]{1,0:T(8,128)(2,1)S(1)} %convolution_convert_fusion) | copy-start | bytes 4718596
  15.2 2.3 %copy-start.1 = (f32[768,1024]{1,0:T(8,128)}, f32[768,1024]{1,0:T(8,128)S(1)}, u32[]{:S(2)}) copy-start(f32[768,1024]{1,0:T(8,128)S(1)} %fusion.95) | copy-start | bytes 9437188
  15.2 2.7 %copy-start.5 = (s32[3]{0:T(128)S(1)}, s32[3]{0:T(128)}, u32[]{:S(2)}) copy-start(s32[3]{0:T(128)} %param.12) | copy-start | bytes 40
  17.5 3.8 %collective-permute-start = (f32[768,512]{1,0:T(8,128)}, f32[768,512]{1,0:T(8,128)}, u32[]{:S(2)}, u32[]{:S(2)}) collective-permute-start(f32[768,512]{1,0:T(8,128)} %constant_dynamic-slice_fusion), channel_id=1, source_target_pairs={{0,1},{1,0},{2,3},{3,2},{4,5},{5,4},{6,7},{7,6},{8,9},{9,8},{10,11... | collective-permute-start | bytes 4718600 | tf_op jit(solution)/shard_map/ppermute | solution.py:10
  19.2 5.3 %copy-start.2 = (bf16[1,2,1,768,768]{4,3,2,1,0:T(8,128)(2,1)S(1)}, bf16[1,2,1,768,768]{4,3,2,1,0:T(8,128)(2,1)}, u32[]{:S(2)}) copy-start(bf16[1,2,1,768,768]{4,3,2,1,0:T(8,128)(2,1)} %param.14) | copy-start | bytes 7077892
  24.5 0.9 copy-start.7
  25.4 1.2 copy-start.4
  26.6 20.9 %collective-permute-start.1 = (f32[768,256]{0,1:T(8,128)S(1)}, f32[768,256]{0,1:T(8,128)}, u32[]{:S(2)}, u32[]{:S(2)}) collective-permute-start(f32[768,256]{0,1:T(8,128)S(1)} %dynamic-slice_bitcast_fusion), channel_id=1, source_target_pairs={{0,2},{1,3},{2,0},{3,1},{4,6},{5,7},{6,4},{7,5},{8,10},{9,11},{10,... | collective-permute-start | bytes 2359304 | tf_op jit(solution)/shard_map/ppermute | solution.py:10
  30.2 19.6 %copy-start.3 = (bf16[1,2,1,768,768]{4,3,2,1,0:T(8,128)(2,1)S(1)}, bf16[1,2,1,768,768]{4,3,2,1,0:T(8,128)(2,1)}, u32[]{:S(2)}) copy-start(bf16[1,2,1,768,768]{4,3,2,1,0:T(8,128)(2,1)} %param.14) | copy-start | bytes 7077892
  51.1 11.0 %collective-permute-start.2 = (f32[768,128]{0,1:T(8,128)}, f32[768,128]{0,1:T(8,128)}, u32[]{:S(2)}, u32[]{:S(2)}) collective-permute-start(f32[768,128]{0,1:T(8,128)} %dynamic-slice_bitcast_fusion.1), channel_id=1, source_target_pairs={{0,4},{1,5},{2,6},{3,7},{4,0},{5,1},{6,2},{7,3},{8,12},{9,13},{10,... | collective-permute-start | bytes 1179656 | tf_op jit(solution)/shard_map/ppermute | solution.py:10
  64.0 5.7 %collective-permute-start.3 = (bf16[768,128]{0,1:T(8,128)(2,1)S(1)}, bf16[768,128]{0,1:T(8,128)(2,1)S(1)}, u32[]{:S(2)}, u32[]{:S(2)}) collective-permute-start(bf16[768,128]{0,1:T(8,128)(2,1)S(1)} %fusion.37), channel_id=1, source_target_pairs={{0,4},{1,5},{2,6},{3,7},{4,0},{5,1},{6,2},{7,3},{8,12},{9,13},{10,... | collective-permute-start | bytes 589832 | tf_op jit(solution)/shard_map/ppermute | solution.py:10
  72.3 8.7 %collective-permute-start.4 = (bf16[768,256]{0,1:T(8,128)(2,1)S(1)}, bf16[768,256]{0,1:T(8,128)(2,1)S(1)}, u32[]{:S(2)}, u32[]{:S(2)}) collective-permute-start(bf16[768,256]{0,1:T(8,128)(2,1)S(1)} %fusion.19), channel_id=1, source_target_pairs={{0,2},{1,3},{2,0},{3,1},{4,6},{5,7},{6,4},{7,5},{8,10},{9,11},{10,... | collective-permute-start | bytes 1179656 | tf_op jit(solution)/shard_map/ppermute | solution.py:10
  85.3 2.5 %collective-permute-start.5 = (bf16[768,512]{0,1:T(8,128)(2,1)S(1)}, bf16[768,512]{0,1:T(8,128)(2,1)}, u32[]{:S(2)}, u32[]{:S(2)}) collective-permute-start(bf16[768,512]{0,1:T(8,128)(2,1)S(1)} %fusion.15), channel_id=1, source_target_pairs={{0,1},{1,0},{2,3},{3,2},{4,5},{5,4},{6,7},{7,6},{8,9},{9,8},{10,11... | collective-permute-start | bytes 2359304 | tf_op jit(solution)/shard_map/ppermute | solution.py:10
Sparse Core Ops, SparseCore 0:
  98.9 77.5 reduce-scatter.1
where the time goes:
time: 184 us; the launch traced here: 183 us
  waiting for transfers between devices  119 us (65%)
  matrix products  30.3 us (16%)
  between operations  14.2 us (8%)
  starting transfers between devices  8.23 us (4%)
  other arithmetic  5.95 us (3%)
  local copies, waits for them, and re-layouts  5.73 us (3%)
    reduce_scatter x1, waiting for transfers between devices, body(): lax.psum_scatter(weighted, 'shift', scatter_dimension=0, tiled=True)  77.8 us
    ppermute x6, waiting for transfers between devices, partner_2(): return lax.ppermute(value, axis, pairs)  41.1 us
    dot_general x1, matrix products, body(): jnp.dot(inverse, lifted, preferred_element_type=jnp.float32)  8.59 us
    ppermute x6, starting transfers between devices, partner_2(): return lax.ppermute(value, axis, pairs)  8.22 us
    dot_general x3, matrix products, body(): jnp.dot(front_inverse[0, level_index, 0], operand, preferred_element_type...  7.43 us
    dot_general x2, matrix products, body(): jnp.dot(front_inverse[0, level_index, 0], lifted_up, preferred_element_ty...  6.07 us
    dot_general x1, matrix products, body(): jnp.dot(inverse, leaf_rhs[0], preferred_element_type=jnp.float32)  3.99 us
  transfers between devices with their start and end apart: 7, of which 7 were waited for; matrix products, arithmetic and copies ran while one was open for 1% of the time, Pallas kernels for 0%

commit v1 on v0

v1 whole, which is shorter than its diff:
```python
import functools

import jax
import jax.numpy as jnp
from jax import lax
from jax.experimental import pallas as pl
from jax.experimental.pallas import tpu as pltpu
from jax.sharding import PartitionSpec as P

WIDE = jnp.float32
NARROW = jnp.bfloat16
VMEM_LIMIT = 24 * 1024 * 1024
SHARES = (4, 4)
PARTS = ((4, 4), (4, 4))


COST = 0.01
TILES = 2


def exchange(value, axis, bit):
    mask = 2**bit
    pairs = [(source, source ^ mask) for source in range(lax.axis_size(axis))]
    return lax.ppermute(value, axis, pairs)


def dot(left, right, left_dim=1, right_dim=0):
    return lax.dot_general(
        left, right, (((left_dim,), (right_dim,)), ((), ())), preferred_element_type=WIDE
    )


class Chain:
    def __init__(self):
        self.last = None
        self.tag = None
        self.cost = COST

    def __call__(self, kernel, outs, scalars, arrays, name, far=(), out_space=pltpu.VMEM, scratch=()):
        after = [] if self.last is None else [self.last]

        def run(*refs):
            kernel(*refs[len(after) :])

        results = pl.pallas_call(
            run,
            out_shape=[jax.ShapeDtypeStruct(shape, kind) for shape, kind in outs],
            in_specs=[pl.BlockSpec(memory_space=pl.ANY)] * len(after)
            + [pl.BlockSpec(memory_space=pltpu.SMEM)] * len(scalars)
            + [pl.BlockSpec(memory_space=pltpu.VMEM)] * len(arrays)
            + [pl.BlockSpec(memory_space=pl.ANY)] * len(far),
            out_specs=[pl.BlockSpec(memory_space=out_space)] * len(outs),
            scratch_shapes=scratch,
            cost_estimate=pl.CostEstimate(
                flops=int(self.cost * 1.15e9), bytes_accessed=1, transcendentals=0
            ),
            compiler_params=pltpu.CompilerParams(vmem_limit_bytes=VMEM_LIMIT),
            name=self.tag + "_" + name,
        )(*after, *scalars, *arrays, *[pltpu.with_memory_space_constraint(a, pltpu.HBM) for a in far])
        self.last = results[0]
        return results


def live(value, size):
    unknowns = lax.broadcasted_iota(jnp.int32, value.shape, 1)
    return jnp.where(unknowns < size, value, 0.0)


def selector(rows, front):
    at = lax.broadcasted_iota(jnp.int32, (front, rows.shape[1]), 0)
    return (at == rows[...]).astype(WIDE).astype(NARROW)


def load_kernel(width, place, rhs_in, inverse_in, coupling_in, rows_in, fronts_in, links_in, *refs):
    front_in, link_in = fronts_in.at[0], links_in.at[0]
    own, other, half, chosen, inverse, coupling, rhs, front, link, rows, sems = refs
    count = rhs.shape[1] // 2
    tile = inverse.shape[0] // TILES
    mine = place[0]
    copies = []

    def columns(side, start, size):
        return pl.ds(pl.multiple_of(side * count + start, 128), size)

    def load(source, target):
        copies.append(pltpu.make_async_copy(source, target, sems.at[len(copies)]))
        copies[-1].start()

    for side in (mine, 1 - mine):
        load(rhs_in.at[:, columns(side, 0, width)], rhs.at[:, columns(side, 0, width)])
    for number in range(TILES):
        block = pl.ds(number * tile, tile)
        load(inverse_in.at[block], inverse.at[block])
    load(rows_in, rows)
    load(coupling_in, coupling)
    load(front_in, front)
    load(link_in, link)
    if width < count:
        for side in (mine, 1 - mine):
            load(rhs_in.at[:, columns(side, width, count - width)], rhs.at[:, columns(side, width, count - width)])

    copies[0].wait()
    copies[1].wait()
    both = jnp.concatenate([rhs[:, columns(mine, 0, width)], rhs[:, columns(1 - mine, 0, width)]], axis=1)
    for number in range(TILES):
        copies[2 + number].wait()
        block = pl.ds(number * tile, tile)
        half[block, :] = dot(inverse[block, :], both).astype(NARROW)
    copies[2 + TILES].wait()
    selected = selector(rows, own.shape[1])
    chosen[...] = selected
    copies[3 + TILES].wait()
    boundary = dot(half[...], coupling[...], 0, 0).astype(NARROW)
    placed = dot(boundary, selected, 1, 1).astype(NARROW)
    own[...] = placed[:width]
    other[...] = placed[width:]
    for copy in copies[4 + TILES :]:
        copy.wait()


def leaf_up_kernel(offset, width, place, inverse, rhs, coupling, chosen, *refs):
    if len(refs) > 3:
        fronts_in, links_in, own, other, half, fronts, links, sems = refs
        copies = [
            pltpu.make_async_copy(source.at[pl.ds(1, target.shape[0])], target, sems.at[number])
            for number, (source, target) in enumerate(((fronts_in, fronts), (links_in, links)))
        ]
    else:
        own, other, half = refs
        copies = []
    for copy in copies:
        copy.start()
    count = rhs.shape[1] // 2
    mine = place[0]

    def columns(side):
        return rhs[:, pl.ds(pl.multiple_of(side * count + offset, 128), width)]

    both = jnp.concatenate([columns(mine), columns(1 - mine)], axis=1)
    product = dot(inverse[...], both).astype(NARROW)
    half[...] = product
    boundary = dot(product, coupling[...], 0, 0).astype(NARROW)
    placed = dot(boundary, chosen[...], 1, 1).astype(NARROW)
    own[...] = placed[:width]
    other[...] = placed[width:]
    for copy in copies:
        copy.wait()


def front_up_kernel(sizes, mine, received, front, link, carried, solved):
    gathered = mine[...].astype(WIDE) + received[...].astype(WIDE)
    operand = live(gathered, sizes[0]).astype(NARROW)
    result = live(dot(operand, front[...], 1, 1), sizes[0]).astype(NARROW)
    solved[...] = result
    carried[...] = dot(result, link[...]).astype(NARROW)


def product_kernel(sizes, front, link, fronts, links, downs, ups):
    downs[0] = dot(front[...], link[...]).astype(NARROW)
    for level in range(links.shape[0]):
        coupling = links[level]
        downs[level + 1] = dot(fronts[level], coupling).astype(NARROW)
        alive = lax.broadcasted_iota(jnp.int32, coupling.shape, 0) < sizes[level + 1]
        masked = jnp.where(alive, coupling, jnp.zeros_like(coupling))
        ups[level] = dot(fronts[level], masked, 0, 0).astype(NARROW)


def front_pass_kernel(level, sizes, mine, received, ups, carried, operand):
    gathered = mine[...].astype(WIDE) + received[...].astype(WIDE)
    value = live(gathered, sizes[level]).astype(NARROW)
    operand[...] = value
    carried[...] = dot(value, ups[level - 1]).astype(NARROW)


def front_solve_kernel(level, sizes, operand, fronts, solved):
    solved[...] = live(dot(operand[...], fronts[level - 1], 1, 1), sizes[level]).astype(NARROW)


def top_kernel(levels, sizes, mine, received, fronts, downs, *refs):
    *solved, back = refs
    gathered = mine[...].astype(WIDE) + received[...].astype(WIDE)
    operand = live(gathered, sizes[levels - 1]).astype(NARROW)
    current = live(dot(operand, fronts[levels - 2], 1, 1), sizes[levels - 1]).astype(NARROW)
    for level in range(levels - 2, -1, -1):
        correction = dot(current, downs[level], 1, 1)
        current = live(solved[level][...].astype(WIDE) - correction, sizes[level]).astype(NARROW)
    back[...] = current


def lift_kernel(inverse, coupling, lift):
    lift[...] = dot(inverse[...], coupling[...]).astype(NARROW)


def down(masks, place, weight, lift, picked, half, columns, out):
    block = out.shape[0] // len(masks)
    for number, mask in enumerate(masks):
        source = pl.ds(pl.multiple_of((place[1] ^ mask) * block, block), block)
        correction = dot(lift[source, :], picked, 1, 1)
        result = weight[0] * (half[source, columns].astype(WIDE) - correction)
        out[number * block : (number + 1) * block, :] = result.astype(out.dtype)


def down_first_kernel(masks, start, at, place, weight, lift, chosen, half, *refs):
    *backs, out, picked = refs
    width = out.shape[1]
    back = jnp.concatenate([ref[...] for ref in backs], axis=0)[at : at + width]
    values = dot(back, chosen[...]).astype(NARROW)
    picked[...] = values
    down(masks, place, weight, lift, values, half, pl.ds(start, width), out)


def down_second_kernel(masks, start, place, weight, lift, half, picked, out):
    down(masks, place, weight, lift, picked[...], half, pl.ds(start, out.shape[1]), out)


def add_kernel(kept, came, sent, rest):
    total = kept[...] + came[...].astype(WIDE)
    rows = sent.shape[0]
    sent[...] = total[:rows].astype(NARROW)
    rest[...] = total[rows:]


def last_add_kernel(kept, came, total):
    total[...] = kept[...] + came[...].astype(WIDE)


def body(
    leaf_rhs,
    leaf_inverse,
    leaf_coupling,
    leaf_rows,
    front_sizes,
    front_inverse,
    front_coupling,
    shift_weight,
):
    levels = lax.axis_size("leaf").bit_length() - 1
    shifts = lax.axis_size("shift")
    steps = shifts.bit_length() - 1
    core = lax.axis_index("leaf") & 1
    place = jnp.stack([core, lax.axis_index("shift")]).astype(jnp.int32)
    inverse_in, coupling_in, rhs_in = leaf_inverse[0, 0], leaf_coupling[0, 0], leaf_rhs[0]
    fronts_in, links_in = front_inverse[0, :, 0], front_coupling[0, :, 0]
    order, columns = rhs_in.shape
    front, boundary = fronts_in.shape[-1], coupling_in.shape[1]
    block = order // shifts
    unit = columns // (2 * sum(SHARES))
    widths = [share * unit for share in SHARES]
    offsets = [sum(widths[:n]) for n in range(len(widths))]
    def masks_of(step):
        if step == steps:
            return [0]
        stay = masks_of(step + 1)
        return [m | 1 << step for m in stay] + stay
    stay = masks_of(1)
    leave = [m | 1 for m in stay]

    chain = Chain()
    state = [dict() for _ in widths]
    final = [None for _ in widths]

    held = {}

    held = {}

    held = {}

    def leaf(n):
        width = widths[n]
        s = state[n]
        outs = [((width, front), NARROW)] * 2 + [((order, 2 * width), NARROW)]
        if n == 0:
            kept = {"inverse": inverse_in, "coupling": coupling_in, "rhs": rhs_in}
            shapes = [a.shape for a in kept.values()] + [(front, front)] * 2
            s["mine"], other, s["half"], held["chosen"], *loaded = chain(
                functools.partial(load_kernel, width),
                [*outs, ((front, boundary), NARROW), *[(shape, NARROW) for shape in shapes]],
                [place], [], "leaf_up", far=[rhs_in, inverse_in, coupling_in, leaf_rows, fronts_in, links_in],
                scratch=[pltpu.VMEM(leaf_rows.shape, jnp.int32), pltpu.SemaphoreType.DMA((8 + TILES,))],
            )
            held.update(zip([*kept, "front", "link"], loaded))
        else:
            far = [fronts_in, links_in] if n == 1 else []
            outs += [((a.shape[0] - 1, front, front), NARROW) for a in far]
            s["mine"], other, s["half"], *loaded = chain(
                functools.partial(leaf_up_kernel, offsets[n], width), outs, [place],
                [held[k] for k in ("inverse", "rhs", "coupling", "chosen")], "leaf_up",
                far=far, scratch=[pltpu.SemaphoreType.DMA((2,))] if far else [],
            )
            held.update(zip(("fronts", "links"), loaded))
        s["came"] = exchange(other, "leaf", 0)
        s["solved"] = []

    def up(n):
        width = widths[n]
        s = state[n]
        s["mine"], solved = chain(
            front_up_kernel, [((width, front), NARROW)] * 2, [front_sizes],
            [s["mine"], s["came"], held["front"], held["link"]], "front_up",
        )
        s["solved"].append(solved)
        s["came"] = exchange(s["mine"], "leaf", 1)

    def products():
        held["downs"], held["ups"] = chain(
            product_kernel,
            [((levels - 1, front, front), NARROW), ((levels - 2, front, front), NARROW)],
            [front_sizes], [held[k] for k in ("front", "link", "fronts", "links")], "products",
        )

    def middle(n):
        s = state[n]
        s["operands"] = []
        for level in range(1, levels - 1):
            s["mine"], operand = chain(
                functools.partial(front_pass_kernel, level), [((widths[n], front), NARROW)] * 2, [front_sizes],
                [s["mine"], s["came"], held["ups"]], "front_pass",
            )
            s["operands"].append(operand)
            s["came"] = exchange(s["mine"], "leaf", level + 1)

    def solve(n):
        s = state[n]
        for level in range(1, levels - 1):
            s["solved"] += chain(
                functools.partial(front_solve_kernel, level), [((widths[n], front), NARROW)], [front_sizes],
                [s["operands"][level - 1], held["fronts"]], "front_solve",
            )

    def top(n):
        s = state[n]
        (s["back"],) = chain(
            functools.partial(top_kernel, levels), [((widths[n], front), NARROW)], [front_sizes],
            [s["mine"], s["came"], held["fronts"], held["downs"], *s["solved"]], "top",
        )
        s["back_came"] = exchange(s["back"], "leaf", 0)

    def lift():
        (held["lift"],) = chain(
            lift_kernel, [((order, boundary), NARROW)], [], [held["inverse"], held["coupling"]], "lift"
        )

    def parts(n):
        sizes = [share * unit for share in PARTS[n]]
        return [(sum(sizes[:p]), size) for p, size in enumerate(sizes)]

    def first(n, part):
        s = state[n]
        start, width = parts(n)[part]
        backs, at = [s["back"], s["back_came"]], start
        if start + width <= widths[n]:
            backs = backs[:1]
        elif start >= widths[n]:
            backs, at = backs[1:], start - widths[n]
        sent, s["picked", part] = chain(
            functools.partial(down_first_kernel, leave, start, at),
            [((len(leave) * block, width), NARROW), ((width, boundary), NARROW)],
            [place, shift_weight],
            [held["lift"], held["chosen"], s["half"], *backs],
            "down_first",
        )
        s["sum_came", part] = exchange(sent, "shift", 0)

    def second(n, part):
        s = state[n]
        start, width = parts(n)[part]
        (s["kept", part],) = chain(
            functools.partial(down_second_kernel, stay, start),
            [((len(stay) * block, width), WIDE)],
            [place, shift_weight],
            [held["lift"], s["half"], s["picked", part]],
            "down_second",
        )

    def add(n, part):
        s = state[n]
        width = parts(n)[part][1]
        for step in range(1, steps):
            rows = block * (shifts >> step + 1)
            sent, s["kept", part] = chain(
                add_kernel, [((rows, width), NARROW), ((rows, width), WIDE)], [],
                [s["kept", part], s["sum_came", part]], "add",
            )
            s["sum_came", part] = exchange(sent, "shift", step)

    def last(n, part):
        s = state[n]
        (s["total", part],) = chain(
            last_add_kernel, [((block, parts(n)[part][1]), WIDE)], [],
            [s["kept", part], s["sum_came", part]], "last_add",
        )

    run = {
        "A": leaf,
        "B": up,
        "C": middle,
        "T": solve,
        "Q": lambda n: products(),
        "D": top,
        "G": lambda n: lift(),
        "E": first,
        "S": second,
        "F": add,
        "Z": last,
    }
    for step in ORDER:
        chain.tag, _, cost = step.partition(":")
        chain.cost = float(cost or COST)
        run[step[0]](*[int(digit) for digit in chain.tag[1:] or "0"])

    owned, others = [], []
    for n, width in enumerate(widths):
        whole = jnp.concatenate([state[n]["total", part] for part in range(len(PARTS[n]))], axis=1)
        owned.append(whole[:, :width])
        others.append(whole[:, width:])
    low = jnp.concatenate(owned + others, axis=1)
    high = jnp.concatenate(others + owned, axis=1)
    return jnp.where(core == 0, low, high)[None]


ORDER = ("A0", "A1", "B0", "G", "Q", "B1", "C0", "T0", "D0", "E00", "C1", "E01", "S00", "F00", "T1", "S01:2", "D1", "E10", "F01", "Z00", "S10:3", "E11", "F10", "S11", "Z01:2", "F11", "Z10", "Z11")


def solution(mesh):
    in_specs = (
        P("leaf", None, None),
        P("shift", "leaf", None, None),
        P("shift", "leaf", None, None),
        P("leaf", None),
        P(),
        P("shift", None, "leaf", None, None),
        P("shift", None, "leaf", None, None),
        P("shift"),
    )
    out_specs = P("leaf", "shift", None)
    return jax.shard_map(body, mesh=mesh, in_specs=in_specs, out_specs=out_specs, check_vma=False)
```

time: 184 us -> 85.1 us (0.46)
  waiting for transfers between devices: 119 us -> 31.4 us
  Pallas kernels: 0 us -> 32 us
  matrix products: 30.3 us -> 0 us
  between operations: 14.2 us -> 0.88 us
  starting transfers between devices: 8.23 us -> 19.4 us
  local copies, waits for them, and re-layouts: 5.73 us -> 0.01 us
  other arithmetic: 5.95 us -> 1.22 us
    reduce_scatter x1 -> x0, waiting for transfers between devices: 77.8 us -> none  [body(): lax.psum_scatter(weighted, 'shift', scatter_dimension=0, tiled=True)]
    pallas_call x0 -> x28, Pallas kernels: none -> 32 us  [__call__(): pl.pallas_call(run, out_shape=[jax.ShapeDtypeStruct(shape, kind) for shap...]
    dot_general x11 -> x0, matrix products: 30.3 us -> none  [the longest x1 8.59 us: body(): jnp.dot(inverse, lifted, preferred_element_type=jnp.float32)]
    ppermute x6 -> x16, starting transfers between devices: 8.22 us -> 19.4 us  [exchange(): return lax.ppermute(value, axis, pairs)]
    ppermute x6 -> x16, waiting for transfers between devices: 41.1 us -> 31.4 us  [exchange(): return lax.ppermute(value, axis, pairs)]
    unnamed x20 -> x2, local copies, waits for them, and re-layouts: 2.7 us -> 0.01 us
    dynamic_slice x3 -> x0, local copies, waits for them, and re-layouts: 2.41 us -> none  [body(): lax.dynamic_slice_in_dim(carried, (1 - own_bit) * (columns // 2), columns...]
    select_n x3 -> x1, other arithmetic: 3.21 us -> 1.14 us  [body(): return jnp.where(core == 0, low, high)[None]]
  transfers between devices with their start and end apart: 7 -> 16, of which waited for: 7 -> 7; matrix products, arithmetic and copies ran while one was open for 1% -> 0% of each run, Pallas kernels for 0% -> 30%
where the time goes in v1:
time: 85.1 us; the launch traced here: 84.9 us
  Pallas kernels  32 us (38%)
  waiting for transfers between devices  31.4 us (37%)
  starting transfers between devices  19.4 us (23%)
  other arithmetic  1.22 us (1%)
  between operations  0.88 us (1%)
    pallas_call x28, Pallas kernels, __call__(): pl.pallas_call(run, out_shape=[jax.ShapeDtypeStruct(shape, kind) for shap...  32 us
    ppermute x16, waiting for transfers between devices, exchange(): return lax.ppermute(value, axis, pairs)  31.4 us
    ppermute x16, starting transfers between devices, exchange(): return lax.ppermute(value, axis, pairs)  19.4 us
  transfers between devices with their start and end apart: 16, of which 7 were waited for; matrix products, arithmetic and copies ran while one was open for 0% of the time, Pallas kernels for 30%

profile of v1, /device:TPU:0, one launch (start us, length us, event | category | flops | bytes accessed | tf_op | source)
XLA Modules:
  0.0 84.9 jit_solution(3126819707015705427)
XLA Ops:
  0.1 5.3 %A0_leaf_up.1 = (bf16[256,768]{1,0:T(8,128)(2,1)S(1)}, bf16[256,768]{1,0:T(8,128)(2,1)S(1)}, bf16[1024,512]{1,0:T(8,128)(2,1)S(1)}, bf16[768,384]{1,0:T(8,128)(2...) custom-call(s32[2]{0:T(128)S(1)} %pad_add_fusion.refs_0_.refs_1_, ...), custom_call_target="tpu_custom_call" | custom-call | flops 11500000 | bytes 1 | tf_op jit(solution)/shard_map/A0_leaf_up/pallas_call | solution.py:45
  5.9 3.0 %A1_leaf_up.1 = (bf16[256,768]{1,0:T(8,128)(2,1)S(1)}, bf16[256,768]{1,0:T(8,128)(2,1)S(1)}, bf16[1024,512]{1,0:T(8,128)(2,1)S(1)}, bf16[2,768,768]{2,1,0:T(8,128)(2,1)S(1)}, bf16[1,768,768]{2,1,0:T(8,128)(2,1)S(1)}) custom-call(bf16[256,768]{1,0:T(8,128)(2,1)S(1)} %get-tuple-element.45.refs_0_.refs_2_, s32[2]{0:T(128)S(1)} %pad_add_fusion.refs_0_.refs_1_, ...), custom_call_target="tpu_custom_call" | custom-call | flops 11500000 | bytes 1 | tf_op jit(solution)/shard_map/A1_leaf_up/pallas_call | solution.py:45
  8.9 1.5 %B0_front_up.1 = (bf16[256,768]{1,0:T(8,128)(2,1)S(1)}, bf16[256,768]{1,0:T(8,128)(2,1)S(1)}) custom-call(bf16[256,768]{1,0:T(8,128)(2,1)S(1)} %get-tuple-element.50.refs_0_.refs_2_, s32[3]{0:T(128)S(1)} %copy-done, bf16[256,768]{1,0:T(8,128)(2,1)S(1)} %get-tuple-element.45.refs_0_.refs_2_, bf16[256,768]{1,0:T(8,128)(2,1)S(1)} %collective-permute-done.refs_3_, ...), custom_call_target="tpu_custom_call" | custom-call | flops 11500000 | bytes 1 | tf_op jit(solution)/shard_map/B0_front_up/pallas_call | solution.py:45
  10.4 3.0 %collective-permute-start.2 = (bf16[256,768]{1,0:T(8,128)(2,1)S(1)}, bf16[256,768]{1,0:T(8,128)(2,1)S(1)}, u32[]{:S(2)}, u32[]{:S(2)}) collective-permute-start(bf16[256,768]{1,0:T(8,128)(2,1)S(1)} %get-tuple-element.54.refs_0_.refs_2_), channel_id=1, source_target_pairs={{0,2},{1,3},{2,0},{3,1},{4,6},{5,7},{6,4},{7,5},{8,10},{9,11},{10,... | collective-permute-start | bytes 1179656 | tf_op jit(solution)/shard_map/ppermute | solution.py:24
  13.4 1.2 %G_lift.1.refs_0_.refs_3_ = bf16[1024,384]{1,0:T(8,128)(2,1)S(1)} custom-call(bf16[256,768]{1,0:T(8,128)(2,1)S(1)} %get-tuple-element.54.refs_0_.refs_2_, bf16[1024,1024]{1,0:T(8,128)(2,1)S(1)} %get-tuple-element.46.refs_2_.refs_1_, bf16[1024,384]{1,0:T(8,128)(2,1)S(1)} %get-tuple-element.48.refs_4_.refs_2_), custom_call_target="tpu_custom_call" | custom-call | flops 11500000 | bytes 1 | tf_op jit(solution)/shard_map/G_lift/pallas_call | solution.py:45
  14.7 3.5 %Q_products.1 = (bf16[2,768,768]{2,1,0:T(8,128)(2,1)S(1)}, bf16[1,768,768]{2,1,0:T(8,128)(2,1)S(1)}) custom-call(bf16[1024,384]{1,0:T(8,128)(2,1)S(1)} %G_lift.1.refs_0_.refs_3_, s32[3]{0:T(128)S(1)} %copy-done, bf16[768,768]{1,0:T(8,128)(2,1)S(1)} %get-tuple-element.52.refs_4_.refs_2_, bf16[768,768]{1,0:T(8,128)(2,1)S(1)} %get-tuple-element.53.refs_5_.refs_3_, ...), custom_call_target="tpu_custom_call" | custom-call | flops 11500000 | bytes 1 | tf_op jit(solution)/shard_map/Q_products/pallas_call | solution.py:45
  18.2 1.5 %B1_front_up.1 = (bf16[256,768]{1,0:T(8,128)(2,1)S(1)}, bf16[256,768]{1,0:T(8,128)(2,1)S(1)}) custom-call(bf16[2,768,768]{2,1,0:T(8,128)(2,1)S(1)} %get-tuple-element.57.refs_0_.refs_5_, s32[3]{0:T(128)S(1)} %copy-done, bf16[256,768]{1,0:T(8,128)(2,1)S(1)} %get-tuple-element.50.refs_0_.refs_2_, bf16[256,768]{1,0:T(8,128)(2,1)S(1)} %collective-permute-done.1.refs_3_, ...), custom_call_target="tpu_custom_call" | custom-call | flops 11500000 | bytes 1 | tf_op jit(solution)/shard_map/B1_front_up/pallas_call | solution.py:45
  19.7 3.1 %collective-permute-done.2.refs_3_ = bf16[256,768]{1,0:T(8,128)(2,1)S(1)} collective-permute-done((bf16[256,768]{1,0:T(8,128)(2,1)S(1)}, bf16[256,768]{1,0:T(8,128)(2,1)S(1)}, u32[]{:S(2)}, u32[]{:S(2)}) %collective-permute-start.2) | collective-permute-done | bytes 393248 | tf_op jit(solution)/shard_map/ppermute | solution.py:24
  22.8 1.0 %C0_front_pass.1 = (bf16[256,768]{1,0:T(8,128)(2,1)S(1)}, bf16[256,768]{1,0:T(8,128)(2,1)S(1)}) custom-call(bf16[256,768]{1,0:T(8,128)(2,1)S(1)} %get-tuple-element.59.refs_0_.refs_2_, s32[3]{0:T(128)S(1)} %copy-done, bf16[256,768]{1,0:T(8,128)(2,1)S(1)} %get-tuple-element.54.refs_0_.refs_2_, bf16[256,768]{1,0:T(8,128)(2,1)S(1)} %collective-permute-done.2.refs_3_, ...), custom_call_target="tpu_custom_call" | custom-call | flops 11500000 | bytes 1 | tf_op jit(solution)/shard_map/C0_front_pass/pallas_call | solution.py:45
  23.8 1.8 %collective-permute-start.3 = (bf16[256,768]{1,0:T(8,128)(2,1)S(1)}, bf16[256,768]{1,0:T(8,128)(2,1)S(1)}, u32[]{:S(2)}, u32[]{:S(2)}) collective-permute-start(bf16[256,768]{1,0:T(8,128)(2,1)S(1)} %get-tuple-element.61.refs_0_.refs_2_), channel_id=1, source_target_pairs={{0,4},{1,5},{2,6},{3,7},{4,0},{5,1},{6,2},{7,3},{8,12},{9,13},{10,... | collective-permute-start | bytes 1179656 | tf_op jit(solution)/shard_map/ppermute | solution.py:24
  25.6 1.5 %collective-permute-start.4 = (bf16[256,768]{1,0:T(8,128)(2,1)S(1)}, bf16[256,768]{1,0:T(8,128)(2,1)S(1)}, u32[]{:S(2)}, u32[]{:S(2)}) collective-permute-start(bf16[256,768]{1,0:T(8,128)(2,1)S(1)} %get-tuple-element.59.refs_0_.refs_2_), channel_id=1, source_target_pairs={{0,2},{1,3},{2,0},{3,1},{4,6},{5,7},{6,4},{7,5},{8,10},{9,11},{10,... | collective-permute-start | bytes 1179656 | tf_op jit(solution)/shard_map/ppermute | solution.py:24
  27.1 1.0 %T0_front_solve.1.refs_0_.refs_7_ = bf16[256,768]{1,0:T(8,128)(2,1)S(1)} custom-call(bf16[256,768]{1,0:T(8,128)(2,1)S(1)} %get-tuple-element.61.refs_0_.refs_2_, s32[3]{0:T(128)S(1)} %copy-done, bf16[256,768]{1,0:T(8,128)(2,1)S(1)} %get-tuple-element.62.refs_2_, bf16[2,768,768]{2,1,0:T(8,128)(2,1)S(1)} %get-tuple-element.55.refs_4_.refs_3_), custom_call_target="tpu_custom_call" | custom-call | flops 11500000 | bytes 1 | tf_op jit(solution)/shard_map/T0_front_solve/pallas_call | solution.py:45
  28.2 6.2 %collective-permute-done.3.refs_3_ = bf16[256,768]{1,0:T(8,128)(2,1)S(1)} collective-permute-done((bf16[256,768]{1,0:T(8,128)(2,1)S(1)}, bf16[256,768]{1,0:T(8,128)(2,1)S(1)}, u32[]{:S(2)}, u32[]{:S(2)}) %collective-permute-start.3) | collective-permute-done | bytes 393248 | tf_op jit(solution)/shard_map/ppermute | solution.py:24
  34.4 1.7 %D0_top.1.refs_0_.refs_6_ = bf16[256,768]{1,0:T(8,128)(2,1)S(1)} custom-call(bf16[256,768]{1,0:T(8,128)(2,1)S(1)} %T0_front_solve.1.refs_0_.refs_7_, s32[3]{0:T(128)S(1)} %copy-done, bf16[256,768]{1,0:T(8,128)(2,1)S(1)} %get-tuple-element.61.refs_0_.refs_2_, bf16[256,768]{1,0:T(8,128)(2,1)S(1)} %collective-permute-done.3.refs_3_, ...), custom_call_target="tpu_custom_call" | custom-call | flops 11500000 | bytes 1 | tf_op jit(solution)/shard_map/D0_top/pallas_call | solution.py:45
  36.8 1.2 %E00_down_first.1 = (bf16[512,256]{1,0:T(8,128)(2,1)S(1)}, bf16[256,384]{1,0:T(8,128)(2,1)S(1)}) custom-call(bf16[256,768]{1,0:T(8,128)(2,1)S(1)} %D0_top.1.refs_0_.refs_6_, s32[2]{0:T(128)S(1)} %pad_add_fusion.refs_0_.refs_1_, f32[1]{0:T(128)S(6)} %copy.9.refs_2_, bf16[1024,384]{1,0:T(8,128)(2,1)S(1)} %G_lift.1.refs_0_.refs_3_, ...), custom_call_target="tpu_custom_call" | custom-call | flops 11500000 | bytes 1 | tf_op jit(solution)/shard_map/E00_down_first/pallas_call | solution.py:45
  38.0 1.6 %collective-permute-start.6 = (bf16[512,256]{1,0:T(8,128)(2,1)S(1)}, bf16[512,256]{1,0:T(8,128)(2,1)S(1)}, u32[]{:S(2)}, u32[]{:S(2)}) collective-permute-start(bf16[512,256]{1,0:T(8,128)(2,1)S(1)} %get-tuple-element.65.refs_0_), channel_id=1, source_target_pairs={{0,8},{8,0},{16,24},{24,16},{1,9},{9,1},{17,25},{25,17},{2,10},{10... | collective-permute-start | bytes 786440 | tf_op jit(solution)/shard_map/ppermute | solution.py:24
  39.6 1.0 %C1_front_pass.1 = (bf16[256,768]{1,0:T(8,128)(2,1)S(1)}, bf16[256,768]{1,0:T(8,128)(2,1)S(1)}) custom-call(bf16[512,256]{1,0:T(8,128)(2,1)S(1)} %get-tuple-element.65.refs_0_, s32[3]{0:T(128)S(1)} %copy-done, bf16[256,768]{1,0:T(8,128)(2,1)S(1)} %get-tuple-element.59.refs_0_.refs_2_, bf16[256,768]{1,0:T(8,128)(2,1)S(1)} %collective-permute-done.4.refs_3_, ...), custom_call_target="tpu_custom_call" | custom-call | flops 11500000 | bytes 1 | tf_op jit(solution)/shard_map/C1_front_pass/pallas_call | solution.py:45
  40.6 1.6 %collective-permute-start.7 = (bf16[256,768]{1,0:T(8,128)(2,1)S(1)}, bf16[256,768]{1,0:T(8,128)(2,1)S(1)}, u32[]{:S(2)}, u32[]{:S(2)}) collective-permute-start(bf16[256,768]{1,0:T(8,128)(2,1)S(1)} %get-tuple-element.66.refs_0_.refs_2_), channel_id=1, source_target_pairs={{0,4},{1,5},{2,6},{3,7},{4,0},{5,1},{6,2},{7,3},{8,12},{9,13},{10,... | collective-permute-start | bytes 1179656 | tf_op jit(solution)/shard_map/ppermute | solution.py:24
  42.2 1.2 %E01_down_first.1 = (bf16[512,256]{1,0:T(8,128)(2,1)S(1)}, bf16[256,384]{1,0:T(8,128)(2,1)S(1)}) custom-call(bf16[256,768]{1,0:T(8,128)(2,1)S(1)} %get-tuple-element.66.refs_0_.refs_2_, s32[2]{0:T(128)S(1)} %pad_add_fusion.refs_0_.refs_1_, f32[1]{0:T(128)S(6)} %copy.9.refs_2_, bf16[1024,384]{1,0:T(8,128)(2,1)S(1)} %G_lift.1.refs_0_.refs_3_, ...), custom_call_target="tpu_custom_call" | custom-call | flops 11500000 | bytes 1 | tf_op jit(solution)/shard_map/E01_down_first/pallas_call | solution.py:45
  44.8 2.4 %collective-permute-done.6.refs_2_ = bf16[512,256]{1,0:T(8,128)(2,1)S(1)} collective-permute-done((bf16[512,256]{1,0:T(8,128)(2,1)S(1)}, bf16[512,256]{1,0:T(8,128)(2,1)S(1)}, u32[]{:S(2)}, u32[]{:S(2)}) %collective-permute-start.6) | collective-permute-done | bytes 262176 | tf_op jit(solution)/shard_map/ppermute | solution.py:24
  47.2 2.6 %collective-permute-start.9 = (bf16[256,256]{1,0:T(8,128)(2,1)S(1)}, bf16[256,256]{1,0:T(8,128)(2,1)S(1)}, u32[]{:S(2)}, u32[]{:S(2)}) collective-permute-start(bf16[256,256]{1,0:T(8,128)(2,1)S(1)} %get-tuple-element.69.refs_0_), channel_id=1, source_target_pairs={{0,16},{8,24},{16,0},{24,8},{1,17},{9,25},{17,1},{25,9},{2,18},{10... | collective-permute-start | bytes 393224 | tf_op jit(solution)/shard_map/ppermute | solution.py:24
  49.8 1.0 %T1_front_solve.1.refs_0_.refs_7_ = bf16[256,768]{1,0:T(8,128)(2,1)S(1)} custom-call(bf16[256,256]{1,0:T(8,128)(2,1)S(1)} %get-tuple-element.69.refs_0_, s32[3]{0:T(128)S(1)} %copy-done, bf16[256,768]{1,0:T(8,128)(2,1)S(1)} %get-tuple-element.70.refs_2_, bf16[2,768,768]{2,1,0:T(8,128)(2,1)S(1)} %get-tuple-element.55.refs_4_.refs_3_), custom_call_target="tpu_custom_call" | custom-call | flops 11500000 | bytes 1 | tf_op jit(solution)/shard_map/T1_front_solve/pallas_call | solution.py:45
  51.9 1.7 %D1_top.1.refs_0_.refs_6_ = bf16[256,768]{1,0:T(8,128)(2,1)S(1)} custom-call(f32[512,256]{1,0:T(8,128)S(1)} %S01_down_second.1.refs_0_.refs_1_, s32[3]{0:T(128)S(1)} %copy-done, bf16[256,768]{1,0:T(8,128)(2,1)S(1)} %get-tuple-element.66.refs_0_.refs_2_, bf16[256,768]{1,0:T(8,128)(2,1)S(1)} %collective-permute-done.7.refs_3_, ...), custom_call_target="tpu_custom_call" | custom-call | flops 11500000 | bytes 1 | tf_op jit(solution)/shard_map/D1_top/pallas_call | solution.py:45
  53.8 1.2 %E10_down_first.1 = (bf16[512,256]{1,0:T(8,128)(2,1)S(1)}, bf16[256,384]{1,0:T(8,128)(2,1)S(1)}) custom-call(bf16[256,768]{1,0:T(8,128)(2,1)S(1)} %D1_top.1.refs_0_.refs_6_, s32[2]{0:T(128)S(1)} %pad_add_fusion.refs_0_.refs_1_, f32[1]{0:T(128)S(6)} %copy.9.refs_2_, bf16[1024,384]{1,0:T(8,128)(2,1)S(1)} %G_lift.1.refs_0_.refs_3_, ...), custom_call_target="tpu_custom_call" | custom-call | flops 11500000 | bytes 1 | tf_op jit(solution)/shard_map/E10_down_first/pallas_call | solution.py:45
  55.0 1.5 %collective-permute-start.11 = (bf16[512,256]{1,0:T(8,128)(2,1)S(1)}, bf16[512,256]{1,0:T(8,128)(2,1)S(1)}, u32[]{:S(2)}, u32[]{:S(2)}) collective-permute-start(bf16[512,256]{1,0:T(8,128)(2,1)S(1)} %get-tuple-element.74.refs_0_), channel_id=1, source_target_pairs={{0,8},{8,0},{16,24},{24,16},{1,9},{9,1},{17,25},{25,17},{2,10},{10... | collective-permute-start | bytes 786440 | tf_op jit(solution)/shard_map/ppermute | solution.py:24
  56.5 1.7 %collective-permute-start.12 = (bf16[256,256]{1,0:T(8,128)(2,1)S(1)}, bf16[256,256]{1,0:T(8,128)(2,1)S(1)}, u32[]{:S(2)}, u32[]{:S(2)}) collective-permute-start(bf16[256,256]{1,0:T(8,128)(2,1)S(1)} %get-tuple-element.75.refs_0_), channel_id=1, source_target_pairs={{0,16},{8,24},{16,0},{24,8},{1,17},{9,25},{17,1},{25,9},{2,18},{10... | collective-permute-start | bytes 393224 | tf_op jit(solution)/shard_map/ppermute | solution.py:24
  59.1 1.2 %E11_down_first.1 = (bf16[512,256]{1,0:T(8,128)(2,1)S(1)}, bf16[256,384]{1,0:T(8,128)(2,1)S(1)}) custom-call(f32[512,256]{1,0:T(8,128)S(1)} %S10_down_second.1.refs_0_.refs_1_, s32[2]{0:T(128)S(1)} %pad_add_fusion.refs_0_.refs_1_, f32[1]{0:T(128)S(6)} %copy.9.refs_2_, bf16[1024,384]{1,0:T(8,128)(2,1)S(1)} %G_lift.1.refs_0_.refs_3_, ...), custom_call_target="tpu_custom_call" | custom-call | flops 11500000 | bytes 1 | tf_op jit(solution)/shard_map/E11_down_first/pallas_call | solution.py:45
  60.3 1.6 %collective-permute-start.13 = (bf16[512,256]{1,0:T(8,128)(2,1)S(1)}, bf16[512,256]{1,0:T(8,128)(2,1)S(1)}, u32[]{:S(2)}, u32[]{:S(2)}) collective-permute-start(bf16[512,256]{1,0:T(8,128)(2,1)S(1)} %get-tuple-element.78.refs_0_), channel_id=1, source_target_pairs={{0,8},{8,0},{16,24},{24,16},{1,9},{9,1},{17,25},{25,17},{2,10},{10... | collective-permute-start | bytes 786440 | tf_op jit(solution)/shard_map/ppermute | solution.py:24
  61.9 5.0 %collective-permute-done.11.refs_2_ = bf16[512,256]{1,0:T(8,128)(2,1)S(1)} collective-permute-done((bf16[512,256]{1,0:T(8,128)(2,1)S(1)}, bf16[512,256]{1,0:T(8,128)(2,1)S(1)}, u32[]{:S(2)}, u32[]{:S(2)}) %collective-permute-start.11) | collective-permute-done | bytes 262176 | tf_op jit(solution)/shard_map/ppermute | solution.py:24
  68.5 6.4 %collective-permute-done.13.refs_2_ = bf16[512,256]{1,0:T(8,128)(2,1)S(1)} collective-permute-done((bf16[512,256]{1,0:T(8,128)(2,1)S(1)}, bf16[512,256]{1,0:T(8,128)(2,1)S(1)}, u32[]{:S(2)}, u32[]{:S(2)}) %collective-permute-start.13) | collective-permute-done | bytes 262176 | tf_op jit(solution)/shard_map/ppermute | solution.py:24
  75.7 8.1 %collective-permute-done.15.refs_2_ = bf16[256,256]{1,0:T(8,128)(2,1)S(1)} collective-permute-done((bf16[256,256]{1,0:T(8,128)(2,1)S(1)}, bf16[256,256]{1,0:T(8,128)(2,1)S(1)}, u32[]{:S(2)}, u32[]{:S(2)}) %collective-permute-start.15) | collective-permute-done | bytes 131104 | tf_op jit(solution)/shard_map/ppermute | solution.py:24
  83.8 1.1 %maximum_select_fusion = f32[1,256,1024]{2,1,0:T(8,128)} fusion(f32[1,256,256]{2,1,0:T(8,128)S(1)} %bitcast.13, f32[1,256,256]{2,1,0:T(8,128)S(1)} %bitcast.14, f32[1,256,256]{2,1,0:T(8,128)S(1)} %bitcast.11, f32[1,256,256]{2,1,0:T(8,128)S(1)} %bitcast.12, pred[]{:T(512)S(6)} %eq.3), kind=kLoop, calls=%fused_computation | loop fusion | flops 1835008 | bytes 2097153 | tf_op jit(solution)/shard_map/jit(_where)/select_n | solution.py:418
  (32 shorter events, 6.6 us)
Async XLA Ops:
  5.3 3.6 %collective-permute-start = (bf16[256,768]{1,0:T(8,128)(2,1)S(1)}, bf16[256,768]{1,0:T(8,128)(2,1)S(1)}, u32[]{:S(2)}, u32[]{:S(2)}) collective-permute-start(bf16[256,768]{1,0:T(8,128)(2,1)S(1)} %get-tuple-element.51), channel_id=1, source_target_pairs={{0,1},{1,0},{2,3},{3,2},{4,5},{5,4},{6,7},{7,6},{8,9},{9,8},{10,11... | collective-permute-start | bytes 1179656 | tf_op jit(solution)/shard_map/ppermute | solution.py:24
  5.9 3.1 %copy-start = (s32[3]{0:T(128)S(1)}, s32[3]{0:T(128)}, u32[]{:S(2)}) copy-start(s32[3]{0:T(128)} %refs_1_.17) | copy-start | bytes 40
  8.8 9.3 %collective-permute-start.1 = (bf16[256,768]{1,0:T(8,128)(2,1)S(1)}, bf16[256,768]{1,0:T(8,128)(2,1)S(1)}, u32[]{:S(2)}, u32[]{:S(2)}) collective-permute-start(bf16[256,768]{1,0:T(8,128)(2,1)S(1)} %get-tuple-element.58), channel_id=1, source_target_pairs={{0,1},{1,0},{2,3},{3,2},{4,5},{5,4},{6,7},{7,6},{8,9},{9,8},{10,11... | collective-permute-start | bytes 1179656 | tf_op jit(solution)/shard_map/ppermute | solution.py:24
  10.4 12.3 %collective-permute-start.2 = (bf16[256,768]{1,0:T(8,128)(2,1)S(1)}, bf16[256,768]{1,0:T(8,128)(2,1)S(1)}, u32[]{:S(2)}, u32[]{:S(2)}) collective-permute-start(bf16[256,768]{1,0:T(8,128)(2,1)S(1)} %get-tuple-element.54.refs_0_.refs_2_), channel_id=1, source_target_pairs={{0,2},{1,3},{2,0},{3,1},{4,6},{5,7},{6,4},{7,5},{8,10},{9,11},{10,... | collective-permute-start | bytes 1179656 | tf_op jit(solution)/shard_map/ppermute | solution.py:24
  23.8 10.6 %collective-permute-start.3 = (bf16[256,768]{1,0:T(8,128)(2,1)S(1)}, bf16[256,768]{1,0:T(8,128)(2,1)S(1)}, u32[]{:S(2)}, u32[]{:S(2)}) collective-permute-start(bf16[256,768]{1,0:T(8,128)(2,1)S(1)} %get-tuple-element.61.refs_0_.refs_2_), channel_id=1, source_target_pairs={{0,4},{1,5},{2,6},{3,7},{4,0},{5,1},{6,2},{7,3},{8,12},{9,13},{10,... | collective-permute-start | bytes 1179656 | tf_op jit(solution)/shard_map/ppermute | solution.py:24
  25.6 14.0 %collective-permute-start.4 = (bf16[256,768]{1,0:T(8,128)(2,1)S(1)}, bf16[256,768]{1,0:T(8,128)(2,1)S(1)}, u32[]{:S(2)}, u32[]{:S(2)}) collective-permute-start(bf16[256,768]{1,0:T(8,128)(2,1)S(1)} %get-tuple-element.59.refs_0_.refs_2_), channel_id=1, source_target_pairs={{0,2},{1,3},{2,0},{3,1},{4,6},{5,7},{6,4},{7,5},{8,10},{9,11},{10,... | collective-permute-start | bytes 1179656 | tf_op jit(solution)/shard_map/ppermute | solution.py:24
  36.1 6.1 %collective-permute-start.5 = (bf16[256,768]{1,0:T(8,128)(2,1)S(1)}, bf16[256,768]{1,0:T(8,128)(2,1)S(1)}, u32[]{:S(2)}, u32[]{:S(2)}) collective-permute-start(bf16[256,768]{1,0:T(8,128)(2,1)S(1)} %D0_top.1.refs_0_.refs_6_), channel_id=1, source_target_pairs={{0,1},{1,0},{2,3},{3,2},{4,5},{5,4},{6,7},{7,6},{8,9},{9,8},{10,11... | collective-permute-start | bytes 1179656 | tf_op jit(solution)/shard_map/ppermute | solution.py:24
  38.0 9.2 %collective-permute-start.6 = (bf16[512,256]{1,0:T(8,128)(2,1)S(1)}, bf16[512,256]{1,0:T(8,128)(2,1)S(1)}, u32[]{:S(2)}, u32[]{:S(2)}) collective-permute-start(bf16[512,256]{1,0:T(8,128)(2,1)S(1)} %get-tuple-element.65.refs_0_), channel_id=1, source_target_pairs={{0,8},{8,0},{16,24},{24,16},{1,9},{9,1},{17,25},{25,17},{2,10},{10... | collective-permute-start | bytes 786440 | tf_op jit(solution)/shard_map/ppermute | solution.py:24
  40.6 11.3 %collective-permute-start.7 = (bf16[256,768]{1,0:T(8,128)(2,1)S(1)}, bf16[256,768]{1,0:T(8,128)(2,1)S(1)}, u32[]{:S(2)}, u32[]{:S(2)}) collective-permute-start(bf16[256,768]{1,0:T(8,128)(2,1)S(1)} %get-tuple-element.66.refs_0_.refs_2_), channel_id=1, source_target_pairs={{0,4},{1,5},{2,6},{3,7},{4,0},{5,1},{6,2},{7,3},{8,12},{9,13},{10,... | collective-permute-start | bytes 1179656 | tf_op jit(solution)/shard_map/ppermute | solution.py:24
  43.4 13.0 %collective-permute-start.8 = (bf16[512,256]{1,0:T(8,128)(2,1)S(1)}, bf16[512,256]{1,0:T(8,128)(2,1)S(1)}, u32[]{:S(2)}, u32[]{:S(2)}) collective-permute-start(bf16[512,256]{1,0:T(8,128)(2,1)S(1)} %get-tuple-element.67.refs_0_), channel_id=1, source_target_pairs={{0,8},{8,0},{16,24},{24,16},{1,9},{9,1},{17,25},{25,17},{2,10},{10... | collective-permute-start | bytes 786440 | tf_op jit(solution)/shard_map/ppermute | solution.py:24
  47.2 10.9 %collective-permute-start.9 = (bf16[256,256]{1,0:T(8,128)(2,1)S(1)}, bf16[256,256]{1,0:T(8,128)(2,1)S(1)}, u32[]{:S(2)}, u32[]{:S(2)}) collective-permute-start(bf16[256,256]{1,0:T(8,128)(2,1)S(1)} %get-tuple-element.69.refs_0_), channel_id=1, source_target_pairs={{0,16},{8,24},{16,0},{24,8},{1,17},{9,25},{17,1},{25,9},{2,18},{10... | collective-permute-start | bytes 393224 | tf_op jit(solution)/shard_map/ppermute | solution.py:24
  53.7 5.4 %collective-permute-start.10 = (bf16[256,768]{1,0:T(8,128)(2,1)S(1)}, bf16[256,768]{1,0:T(8,128)(2,1)S(1)}, u32[]{:S(2)}, u32[]{:S(2)}) collective-permute-start(bf16[256,768]{1,0:T(8,128)(2,1)S(1)} %D1_top.1.refs_0_.refs_6_), channel_id=1, source_target_pairs={{0,1},{1,0},{2,3},{3,2},{4,5},{5,4},{6,7},{7,6},{8,9},{9,8},{10,11... | collective-permute-start | bytes 1179656 | tf_op jit(solution)/shard_map/ppermute | solution.py:24
  55.0 12.0 %collective-permute-start.11 = (bf16[512,256]{1,0:T(8,128)(2,1)S(1)}, bf16[512,256]{1,0:T(8,128)(2,1)S(1)}, u32[]{:S(2)}, u32[]{:S(2)}) collective-permute-start(bf16[512,256]{1,0:T(8,128)(2,1)S(1)} %get-tuple-element.74.refs_0_), channel_id=1, source_target_pairs={{0,8},{8,0},{16,24},{24,16},{1,9},{9,1},{17,25},{25,17},{2,10},{10... | collective-permute-start | bytes 786440 | tf_op jit(solution)/shard_map/ppermute | solution.py:24
  56.5 12.0 %collective-permute-start.12 = (bf16[256,256]{1,0:T(8,128)(2,1)S(1)}, bf16[256,256]{1,0:T(8,128)(2,1)S(1)}, u32[]{:S(2)}, u32[]{:S(2)}) collective-permute-start(bf16[256,256]{1,0:T(8,128)(2,1)S(1)} %get-tuple-element.75.refs_0_), channel_id=1, source_target_pairs={{0,16},{8,24},{16,0},{24,8},{1,17},{9,25},{17,1},{25,9},{2,18},{10... | collective-permute-start | bytes 393224 | tf_op jit(solution)/shard_map/ppermute | solution.py:24
  60.3 14.7 %collective-permute-start.13 = (bf16[512,256]{1,0:T(8,128)(2,1)S(1)}, bf16[512,256]{1,0:T(8,128)(2,1)S(1)}, u32[]{:S(2)}, u32[]{:S(2)}) collective-permute-start(bf16[512,256]{1,0:T(8,128)(2,1)S(1)} %get-tuple-element.78.refs_0_), channel_id=1, source_target_pairs={{0,8},{8,0},{16,24},{24,16},{1,9},{9,1},{17,25},{25,17},{2,10},{10... | collective-permute-start | bytes 786440 | tf_op jit(solution)/shard_map/ppermute | solution.py:24
  67.0 8.7 %collective-permute-start.14 = (bf16[256,256]{1,0:T(8,128)(2,1)S(1)}, bf16[256,256]{1,0:T(8,128)(2,1)S(1)}, u32[]{:S(2)}, u32[]{:S(2)}) collective-permute-start(bf16[256,256]{1,0:T(8,128)(2,1)S(1)} %get-tuple-element.79.refs_0_), channel_id=1, source_target_pairs={{0,16},{8,24},{16,0},{24,8},{1,17},{9,25},{17,1},{25,9},{2,18},{10... | collective-permute-start | bytes 393224 | tf_op jit(solution)/shard_map/ppermute | solution.py:24
  75.0 8.7 %collective-permute-start.15 = (bf16[256,256]{1,0:T(8,128)(2,1)S(1)}, bf16[256,256]{1,0:T(8,128)(2,1)S(1)}, u32[]{:S(2)}, u32[]{:S(2)}) collective-permute-start(bf16[256,256]{1,0:T(8,128)(2,1)S(1)} %get-tuple-element.82.refs_0_), channel_id=1, source_target_pairs={{0,16},{8,24},{16,0},{24,8},{1,17},{9,25},{17,1},{25,9},{2,18},{10... | collective-permute-start | bytes 393224 | tf_op jit(solution)/shard_map/ppermute | solution.py:24

commit v2 on v1

v2 whole, which is shorter than its diff:
```python
import functools

import jax
import jax.numpy as jnp
from jax import lax
from jax.experimental import pallas as pl
from jax.experimental.pallas import tpu as pltpu
from jax.sharding import PartitionSpec as P

WIDE = jnp.float32
NARROW = jnp.bfloat16
VMEM_LIMIT = 24 * 1024 * 1024
SHARES = (1, 1, 2)
GROUPS = ((0, 1), (2,))
PARTS = ((((0, 0, 1), (1, 0, 1)),), (((0, 0, 1), (1, 0, 1)),), (((0, 0, 2),), ((1, 0, 2),)))
COST = 0.01
TILES = 2


def exchange(value, axis, bit):
    mask = 2**bit
    pairs = [(source, source ^ mask) for source in range(lax.axis_size(axis))]
    return lax.ppermute(value, axis, pairs)


def dot(left, right, left_dim=1, right_dim=0):
    return lax.dot_general(
        left, right, (((left_dim,), (right_dim,)), ((), ())), preferred_element_type=WIDE
    )


class Chain:
    def __init__(self):
        self.last = None
        self.tag = None
        self.cost = COST

    def __call__(self, kernel, outs, scalars, arrays, name, far=(), out_space=pltpu.VMEM, scratch=()):
        after = [] if self.last is None else [self.last]

        def run(*refs):
            kernel(*refs[len(after) :])

        results = pl.pallas_call(
            run,
            out_shape=[jax.ShapeDtypeStruct(shape, kind) for shape, kind in outs],
            in_specs=[pl.BlockSpec(memory_space=pl.ANY)] * len(after)
            + [pl.BlockSpec(memory_space=pltpu.SMEM)] * len(scalars)
            + [pl.BlockSpec(memory_space=pltpu.VMEM)] * len(arrays)
            + [pl.BlockSpec(memory_space=pl.ANY)] * len(far),
            out_specs=[pl.BlockSpec(memory_space=out_space)] * len(outs),
            scratch_shapes=scratch,
            cost_estimate=pl.CostEstimate(
                flops=int(self.cost * 1.15e9), bytes_accessed=1, transcendentals=0
            ),
            compiler_params=pltpu.CompilerParams(vmem_limit_bytes=VMEM_LIMIT),
            name=self.tag + "_" + name,
        )(*after, *scalars, *arrays, *[pltpu.with_memory_space_constraint(a, pltpu.HBM) for a in far])
        self.last = results[0]
        return results


def selector(rows, front):
    at = lax.broadcasted_iota(jnp.int32, (front, rows.shape[1]), 0)
    return (at == rows[...]).astype(WIDE).astype(NARROW)


def load_kernel(masks, width, rhs_in, inverse_in, coupling_in, rows_in, fronts_in, links_in, *refs):
    own, other, half, chosen, inverse, mixed, coupling, rhs, front, link, rows, sems = refs
    count = rhs.shape[1] // 2
    block = inverse.shape[0] // len(masks)
    core = lax.axis_index("leaf") & 1
    shift = lax.axis_index("shift")
    copies = []

    def load(source, target):
        copies.append(pltpu.make_async_copy(source, target, sems.at[len(copies)]))
        copies[-1].start()
        return copies[-1]

    def load_columns(start, size):
        return [
            load(
                rhs_in.at[:, pl.ds(pl.multiple_of(side * count + start, 128), size)],
                rhs.at[:, pl.ds(number * count + start, size)],
            )
            for number, side in enumerate((core, 1 - core))
        ]

    def load_blocks(source, target):
        return [
            load(
                source.at[pl.ds(pl.multiple_of((shift ^ mask) * block, block), block)],
                target.at[pl.ds(number * block, block)],
            )
            for number, mask in enumerate(masks)
        ]

    first = load_columns(0, width)
    blocks = load_blocks(inverse_in, inverse)
    small = [load(rows_in, rows)]
    small += load_blocks(coupling_in, mixed)

    for copy in first:
        copy.wait()
    both = jnp.concatenate([rhs[:, :width], rhs[:, count : count + width]], axis=1)
    parts = TILES
    for part in range(parts):
        for copy in blocks[part * len(blocks) // parts : (part + 1) * len(blocks) // parts]:
            copy.wait()
        if part == parts - 1:
            later = [load(fronts_in.at[0], front), load(links_in.at[0], link), load(coupling_in, coupling)]
            if width < count:
                later += load_columns(width, count - width)
        tile = pl.ds(part * (inverse.shape[0] // parts), inverse.shape[0] // parts)
        half[tile, :] = dot(inverse[tile, :], both).astype(NARROW)
    for copy in small:
        copy.wait()
    selected = selector(rows, own.shape[1])
    chosen[...] = selected
    boundary = dot(half[...], mixed[...], 0, 0).astype(NARROW)
    placed = dot(boundary, selected, 1, 1).astype(NARROW)
    own[...] = placed[:width]
    other[...] = placed[width:]
    for copy in later:
        copy.wait()


def leaf_up_kernel(offset, width, inverse, rhs, mixed, chosen, *refs):
    if len(refs) > 3:
        fronts_in, links_in, own, other, half, fronts, links, sems = refs
        copies = [
            pltpu.make_async_copy(source.at[pl.ds(1, target.shape[0])], target, sems.at[number])
            for number, (source, target) in enumerate(((fronts_in, fronts), (links_in, links)))
        ]
    else:
        own, other, half = refs
        copies = []
    for copy in copies:
        copy.start()
    count = rhs.shape[1] // 2
    both = jnp.concatenate(
        [rhs[:, offset : offset + width], rhs[:, count + offset : count + offset + width]], axis=1
    )
    product = dot(inverse[...], both).astype(NARROW)
    half[...] = product
    boundary = dot(product, mixed[...], 0, 0).astype(NARROW)
    placed = dot(boundary, chosen[...], 1, 1).astype(NARROW)
    own[...] = placed[:width]
    other[...] = placed[width:]
    for copy in copies:
        copy.wait()


def gather(level, mine, received, alive):
    total = mine.astype(WIDE) + received.astype(WIDE)
    return (total * alive[level : level + 1, :]).astype(NARROW)


def front_up_kernel(at, alive, mine, received, front, link, carried, solved):
    rows = pl.ds(at, carried.shape[0])
    operand = gather(0, mine[rows], received[rows], alive)
    result = (dot(operand, front[...], 1, 1) * alive[0:1, :]).astype(NARROW)
    solved[...] = result
    carried[...] = dot(result, link[...]).astype(NARROW)


def product_kernel(alive, front, link, fronts, links, downs, ups):
    across = alive[...].T
    for level in range(links.shape[0]):
        coupling = links[level]
        masked = (coupling.astype(WIDE) * across[:, level + 1 : level + 2]).astype(NARROW)
        ups[level] = dot(fronts[level], masked, 0, 0).astype(NARROW)
        downs[level + 1] = dot(fronts[level], coupling).astype(NARROW)
    downs[0] = dot(front[...], link[...]).astype(NARROW)


def front_pass_kernel(level, alive, mine, received, ups, carried, operand):
    value = gather(level, mine[...], received[...], alive)
    operand[...] = value
    carried[...] = dot(value, ups[level - 1]).astype(NARROW)


def front_solve_kernel(level, alive, operand, fronts, solved):
    solved[...] = (dot(operand[...], fronts[level - 1], 1, 1) * alive[level : level + 1, :]).astype(NARROW)


def top_kernel(levels, alive, mine, received, fronts, downs, *refs):
    *solved, back = refs
    operand = gather(levels - 1, mine[...], received[...], alive)
    current = (dot(operand, fronts[levels - 2], 1, 1) * alive[levels - 1 : levels, :]).astype(NARROW)
    for level in range(levels - 2, -1, -1):
        correction = dot(current, downs[level], 1, 1)
        value = solved[level][...].astype(WIDE) - correction
        current = (value * alive[level : level + 1, :]).astype(NARROW)
    back[...] = current


def lift_kernel(inverse, coupling, scale, lift):
    lift[...] = (dot(inverse[...], coupling[...]) * scale[0:1, 0:1]).astype(NARROW)


def down(first, spans, scale, lift, picked, half, out):
    size = out.shape[0]
    rows = pl.ds(0 if first else half.shape[0] - size, size)
    halves = jnp.concatenate([half[rows, pl.ds(at, width)] for at, width in spans], axis=1)
    result = halves.astype(WIDE) * scale[0:1, 0:1] - dot(lift[rows, :], picked, 1, 1)
    out[...] = result.astype(out.dtype)


def down_first_kernel(spans, rows, scale, lift, chosen, half, *refs):
    *backs, out, picked = refs
    back = jnp.concatenate([ref[pl.ds(at, width)] for ref, (at, width) in zip(backs, rows)], axis=0)
    values = dot(back, chosen[...]).astype(NARROW)
    picked[...] = values
    down(True, spans, scale, lift, values, half, out)


def down_second_kernel(spans, scale, lift, half, picked, out):
    down(False, spans, scale, lift, picked[...], half, out)


def add_kernel(kept, came, sent, rest):
    total = kept[...] + came[...].astype(WIDE)
    rows = sent.shape[0]
    sent[...] = total[:rows].astype(NARROW)
    rest[...] = total[rows:]


def last_add_kernel(kept, came, total):
    total[...] = kept[...] + came[...].astype(WIDE)


def body(
    leaf_rhs,
    leaf_inverse,
    leaf_coupling,
    leaf_rows,
    front_sizes,
    front_inverse,
    front_coupling,
    shift_weight,
):
    levels = lax.axis_size("leaf").bit_length() - 1
    shifts = lax.axis_size("shift")
    steps = shifts.bit_length() - 1
    core = lax.axis_index("leaf") & 1
    inverse_in, coupling_in, rhs_in = leaf_inverse[0, 0], leaf_coupling[0, 0], leaf_rhs[0]
    fronts_in, links_in = front_inverse[0, :, 0], front_coupling[0, :, 0]
    order, columns = rhs_in.shape
    front, boundary = fronts_in.shape[-1], coupling_in.shape[1]
    block = order // shifts
    unit = columns // (2 * sum(SHARES))
    widths = [share * unit for share in SHARES]
    offsets = [sum(widths[:n]) for n in range(len(widths))]
    def masks_of(step):
        if step == steps:
            return [0]
        stay = masks_of(step + 1)
        return [m | 1 << step for m in stay] + stay
    stay = masks_of(1)
    leave = [m | 1 for m in stay]

    chain = Chain()
    state = [dict() for _ in widths]
    final = [None for _ in widths]

    unknowns = jnp.arange(front, dtype=jnp.int32)[None, :]
    sizes = jnp.pad(front_sizes, (0, 8 - levels % 8))[:, None]
    held = {
        "alive": (unknowns < sizes).astype(WIDE),
        "scale": jnp.broadcast_to(shift_weight, (8, 128)).astype(WIDE),
    }

    unknowns = jnp.arange(front, dtype=jnp.int32)[None, :]
    sizes = jnp.pad(front_sizes, (0, 8 - levels % 8))[:, None]
    held = {
        "alive": (unknowns < sizes).astype(WIDE),
        "scale": jnp.broadcast_to(shift_weight, (8, 128)).astype(WIDE),
    }

    unknowns = jnp.arange(front, dtype=jnp.int32)[None, :]
    sizes = jnp.pad(front_sizes, (0, 8 - levels % 8))[:, None]
    held = {
        "alive": (unknowns < sizes).astype(WIDE),
        "scale": jnp.broadcast_to(shift_weight, (8, 128)).astype(WIDE),
    }

    def leaf(group):
        chunks = GROUPS[group]
        offset, width = offsets[chunks[0]], sum(widths[n] for n in chunks)
        outs = [((width, front), NARROW)] * 2 + [((order, 2 * width), NARROW)]
        if group == 0:
            shapes = [inverse_in.shape, coupling_in.shape, coupling_in.shape, rhs_in.shape, (front, front), (front, front)]
            names = ["chosen", "inverse", "mixed", "coupling", "rhs", "front", "link"]
            own, other, half, *loaded = chain(
                functools.partial(load_kernel, (*leave, *stay), width),
                [*outs, ((front, boundary), NARROW), *[(shape, NARROW) for shape in shapes]],
                [], [], "leaf_up",
                far=[rhs_in, inverse_in, coupling_in, leaf_rows, fronts_in, links_in],
                scratch=[
                    pltpu.VMEM(leaf_rows.shape, jnp.int32),
                    pltpu.SemaphoreType.DMA((10 + 2 * shifts,)),
                ],
            )
            held.update(zip(names, loaded))
        else:
            far = [fronts_in, links_in] if group == 1 else []
            outs += [((a.shape[0] - 1, front, front), NARROW) for a in far]
            own, other, half, *loaded = chain(
                functools.partial(leaf_up_kernel, offset, width), outs, [],
                [held[k] for k in ("inverse", "rhs", "mixed", "chosen")], "leaf_up",
                far=far, scratch=[pltpu.SemaphoreType.DMA((2,))] if far else [],
            )
            held.update(zip(("fronts", "links"), loaded))
        came = exchange(other, "leaf", 0)
        for n in chunks:
            at = offsets[n] - offset
            state[n].update(mine=own, came=came, half=half, solved=[], at=at, spans=(at, width + at))

    def up(n):
        width = widths[n]
        s = state[n]
        s["mine"], solved = chain(
            functools.partial(front_up_kernel, s["at"]), [((width, front), NARROW)] * 2, [],
            [held["alive"], s["mine"], s["came"], held["front"], held["link"]], "front_up",
        )
        s["solved"].append(solved)
        s["came"] = exchange(s["mine"], "leaf", 1)

    def products():
        held["downs"], held["ups"] = chain(
            product_kernel,
            [((levels - 1, front, front), NARROW), ((levels - 2, front, front), NARROW)],
            [], [held[k] for k in ("alive", "front", "link", "fronts", "links")], "products",
        )

    def middle(n):
        s = state[n]
        s["operands"] = []
        for level in range(1, levels - 1):
            s["mine"], operand = chain(
                functools.partial(front_pass_kernel, level), [((widths[n], front), NARROW)] * 2, [],
                [held["alive"], s["mine"], s["came"], held["ups"]], "front_pass",
            )
            s["operands"].append(operand)
            s["came"] = exchange(s["mine"], "leaf", level + 1)

    def solve(n):
        s = state[n]
        for level in range(1, levels - 1):
            s["solved"] += chain(
                functools.partial(front_solve_kernel, level), [((widths[n], front), NARROW)], [],
                [held["alive"], s["operands"][level - 1], held["fronts"]], "front_solve",
            )

    def top(n):
        s = state[n]
        (s["back"],) = chain(
            functools.partial(top_kernel, levels), [((widths[n], front), NARROW)], [],
            [held["alive"], s["mine"], s["came"], held["fronts"], held["downs"], *s["solved"]], "top",
        )
        s["back_came"] = exchange(s["back"], "leaf", 0)

    def lift():
        (held["lift"],) = chain(
            lift_kernel, [((order, boundary), NARROW)], [],
            [held["inverse"], held["coupling"], held["scale"]], "lift",
        )

    def pieces(n, part=0):
        spans = [(side, start * unit, width * unit) for side, start, width in PARTS[n][part]]
        return spans, sum(width for _, _, width in spans)

    def first(n, part=0):
        s = state[n]
        spans, width = pieces(n, part)
        inside = tuple((s["spans"][side] + start, size) for side, start, size in spans)
        sent, s["picked", part] = chain(
            functools.partial(down_first_kernel, inside, tuple(span[1:] for span in spans)),
            [((len(leave) * block, width), NARROW), ((width, boundary), NARROW)],
            [],
            [held["scale"], held["lift"], held["chosen"], s["half"], *[s["back_came" if side else "back"] for side, _, _ in spans]],
            "down_first",
        )
        s["sum_came", part] = exchange(sent, "shift", 0)

    def second(n, part=0):
        s = state[n]
        spans, width = pieces(n, part)
        inside = tuple((s["spans"][side] + start, size) for side, start, size in spans)
        (s["kept", part],) = chain(
            functools.partial(down_second_kernel, inside),
            [((len(stay) * block, width), WIDE)],
            [],
            [held["scale"], held["lift"], s["half"], s["picked", part]],
            "down_second",
        )

    def add(n, part=0):
        s = state[n]
        _, width = pieces(n, part)
        for step in range(1, steps):
            rows = block * (shifts >> step + 1)
            sent, s["kept", part] = chain(
                add_kernel, [((rows, width), NARROW), ((rows, width), WIDE)], [],
                [s["kept", part], s["sum_came", part]], "add",
            )
            s["sum_came", part] = exchange(sent, "shift", step)

    def last(n, part=0):
        s = state[n]
        (s["total", part],) = chain(
            last_add_kernel, [((block, pieces(n, part)[1]), WIDE)], [],
            [s["kept", part], s["sum_came", part]], "last_add",
        )

    run = {
        "A": leaf,
        "B": up,
        "C": middle,
        "T": solve,
        "Q": lambda n: products(),
        "D": top,
        "G": lambda n: lift(),
        "E": first,
        "S": second,
        "F": add,
        "Z": last,
    }
    for step in ORDER:
        chain.tag, _, cost = step.partition(":")
        chain.cost = float(cost or COST)
        run[step[0]](*[int(digit) for digit in chain.tag[1:] or "0"])

    sides = {}
    for n, chunk in enumerate(PARTS):
        for part in range(len(chunk)):
            at = 0
            for side, start, width in pieces(n, part)[0]:
                sides[side, offsets[n] + start] = state[n]["total", part][:, at : at + width]
                at += width
    owned = [sides[key] for key in sorted(sides) if not key[0]]
    others = [sides[key] for key in sorted(sides) if key[0]]
    low = jnp.concatenate(owned + others, axis=1)
    high = jnp.concatenate(others + owned, axis=1)
    return jnp.where(core == 0, low, high)[None]


ORDER = ("A0", "A1", "B0", "Q", "B1", "C0", "B2", "T0", "G", "C1", "T1", "D0", "E0", "C2", "T2", "D1", "S0", "F0", "E1", "D2", "E20", "Z0", "S20", "S1", "F1:3", "E21", "F20", "S21", "F21", "Z1", "Z20", "Z21")


def solution(mesh):
    in_specs = (
        P("leaf", None, None),
        P("shift", "leaf", None, None),
        P("shift", "leaf", None, None),
        P("leaf", None),
        P(),
        P("shift", None, "leaf", None, None),
        P("shift", None, "leaf", None, None),
        P("shift"),
    )
    out_specs = P("leaf", "shift", None)
    return jax.shard_map(body, mesh=mesh, in_specs=in_specs, out_specs=out_specs, check_vma=False)
```

time: 85.1 us -> 75.3 us (0.88)
  waiting for transfers between devices: 31.4 us -> 18.7 us
  starting transfers between devices: 19.4 us -> 25.4 us
  Pallas kernels: 32 us -> 27 us
  local copies, waits for them, and re-layouts: 0.01 us -> 1.82 us
    ppermute x16 -> x19, waiting for transfers between devices: 31.4 us -> 18.7 us  [exchange(): return lax.ppermute(value, axis, pairs)]
    ppermute x16 -> x19, starting transfers between devices: 19.4 us -> 25.4 us  [exchange(): return lax.ppermute(value, axis, pairs)]
    pallas_call x28 -> x32, Pallas kernels: 32 us -> 27 us  [__call__(): pl.pallas_call(run, out_shape=[jax.ShapeDtypeStruct(shape, kind) for shap...]
    unnamed x2 -> x13, local copies, waits for them, and re-layouts: 0.01 us -> 1.73 us
  transfers between devices with their start and end apart: 16 -> 19, of which waited for: 7 -> 11; matrix products, arithmetic and copies ran while one was open for 0% -> 0% of each run, Pallas kernels for 30% -> 29%
where the time goes in v2:
time: 75.3 us; the launch traced here: 75.1 us
  Pallas kernels  27 us (36%)
  starting transfers between devices  25.4 us (34%)
  waiting for transfers between devices  18.7 us (25%)
  local copies, waits for them, and re-layouts  1.82 us (2%)
  other arithmetic  1.19 us (2%)
  between operations  0.96 us (1%)
    pallas_call x32, Pallas kernels, __call__(): pl.pallas_call(run, out_shape=[jax.ShapeDtypeStruct(shape, kind) for shap...  27 us
    ppermute x19, starting transfers between devices, exchange(): return lax.ppermute(value, axis, pairs)  25.4 us
    ppermute x19, waiting for transfers between devices, exchange(): return lax.ppermute(value, axis, pairs)  18.7 us
    unnamed x13, local copies, waits for them, and re-layouts  1.73 us
  transfers between devices with their start and end apart: 19, of which 11 were waited for; matrix products, arithmetic and copies ran while one was open for 0% of the time, Pallas kernels for 29%

profile of v2, /device:TPU:0, one launch (start us, length us, event | category | flops | bytes accessed | tf_op | source)
XLA Modules:
  0.0 75.1 jit_solution(531216958775195720)
XLA Ops:
  0.0 4.8 %A0_leaf_up.1 = (bf16[256,768]{1,0:T(8,128)(2,1)S(1)}, bf16[256,768]{1,0:T(8,128)(2,1)S(1)}, bf16[1024,512]{1,0:T(8,128)(2,1)S(1)}, bf16[768,384]{1,0:T(8,128)(2...) custom-call(bf16[1024,1024]{1,0:T(8,128)(2,1)} %bitcast.41, ...), custom_call_target="tpu_custom_call" | custom-call | flops 11500000 | bytes 1 | tf_op jit(solution)/shard_map/A0_leaf_up/pallas_call | solution.py:44
  5.3 2.4 %A1_leaf_up.1 = (bf16[256,768]{1,0:T(8,128)(2,1)S(1)}, bf16[256,768]{1,0:T(8,128)(2,1)S(1)}, bf16[1024,512]{1,0:T(8,128)(2,1)S(1)}, bf16[2,768,768]{2,1,0:T(8,128)(2,1)S(1)}, bf16[1,768,768]{2,1,0:T(8,128)(2,1)S(1)}) custom-call(bf16[256,768]{1,0:T(8,128)(2,1)S(1)} %get-tuple-element.50.refs_0_.refs_2_, bf16[1024,1024]{1,0:T(8,128)(2,1)S(1)} %get-tuple-element.51.refs_1_, ...), custom_call_target="tpu_custom_call" | custom-call | flops 11500000 | bytes 1 | tf_op jit(solution)/shard_map/A1_leaf_up/pallas_call | solution.py:44
  8.7 3.0 %collective-permute-start.1 = (bf16[128,768]{1,0:T(8,128)(2,1)S(1)}, bf16[128,768]{1,0:T(8,128)(2,1)S(1)}, u32[]{:S(2)}, u32[]{:S(2)}) collective-permute-start(bf16[128,768]{1,0:T(8,128)(2,1)S(1)} %get-tuple-element.59.refs_0_.refs_2_), channel_id=1, source_target_pairs={{0,2},{1,3},{2,0},{3,1},{4,6},{5,7},{6,4},{7,5},{8,10},{9,11},{10,... | collective-permute-start | bytes 589832 | tf_op jit(solution)/shard_map/ppermute | solution.py:23
  11.7 3.4 %Q_products.1 = (bf16[2,768,768]{2,1,0:T(8,128)(2,1)S(1)}, bf16[1,768,768]{2,1,0:T(8,128)(2,1)S(1)}) custom-call(bf16[128,768]{1,0:T(8,128)(2,1)S(1)} %get-tuple-element.59.refs_0_.refs_2_, f32[8,768]{1,0:T(8,128)S(1)} %fusion.8.refs_1_, bf16[768,768]{1,0:T(8,128)(2,1)S(1)} %get-tuple-element.57.refs_4_.refs_2_, ...), custom_call_target="tpu_custom_call" | custom-call | flops 11500000 | bytes 1 | tf_op jit(solution)/shard_map/Q_products/pallas_call | solution.py:44
  16.0 0.9 %collective-permute-done.1.refs_3_ = bf16[128,768]{1,0:T(8,128)(2,1)S(1)} collective-permute-done((bf16[128,768]{1,0:T(8,128)(2,1)S(1)}, bf16[128,768]{1,0:T(8,128)(2,1)S(1)}, u32[]{:S(2)}, u32[]{:S(2)}) %collective-permute-start.1) | collective-permute-done | bytes 196640 | tf_op jit(solution)/shard_map/ppermute | solution.py:23
  17.2 1.8 %collective-permute-start.4 = (bf16[128,768]{1,0:T(8,128)(2,1)S(1)}, bf16[128,768]{1,0:T(8,128)(2,1)S(1)}, u32[]{:S(2)}, u32[]{:S(2)}) collective-permute-start(bf16[128,768]{1,0:T(8,128)(2,1)S(1)} %get-tuple-element.65.refs_0_.refs_2_), channel_id=1, source_target_pairs={{0,4},{1,5},{2,6},{3,7},{4,0},{5,1},{6,2},{7,3},{8,12},{9,13},{10,... | collective-permute-start | bytes 589832 | tf_op jit(solution)/shard_map/ppermute | solution.py:23
  19.0 1.0 %B2_front_up.1 = (bf16[256,768]{1,0:T(8,128)(2,1)S(1)}, bf16[256,768]{1,0:T(8,128)(2,1)S(1)}) custom-call(bf16[128,768]{1,0:T(8,128)(2,1)S(1)} %get-tuple-element.65.refs_0_.refs_2_, f32[8,768]{1,0:T(8,128)S(1)} %fusion.8.refs_1_, bf16[256,768]{1,0:T(8,128)(2,1)S(1)} %get-tuple-element.55.refs_0_.refs_2_, ...), custom_call_target="tpu_custom_call" | custom-call | flops 11500000 | bytes 1 | tf_op jit(solution)/shard_map/B2_front_up/pallas_call | solution.py:44
  20.0 1.6 %collective-permute-start.6 = (bf16[256,768]{1,0:T(8,128)(2,1)S(1)}, bf16[256,768]{1,0:T(8,128)(2,1)S(1)}, u32[]{:S(2)}, u32[]{:S(2)}) collective-permute-start(bf16[256,768]{1,0:T(8,128)(2,1)S(1)} %get-tuple-element.67.refs_0_.refs_2_), channel_id=1, source_target_pairs={{0,2},{1,3},{2,0},{3,1},{4,6},{5,7},{6,4},{7,5},{8,10},{9,11},{10,... | collective-permute-start | bytes 1179656 | tf_op jit(solution)/shard_map/ppermute | solution.py:23
  22.8 1.3 %G_lift.1.refs_0_.refs_2_ = bf16[1024,384]{1,0:T(8,128)(2,1)S(1)} custom-call(bf16[128,768]{1,0:T(8,128)(2,1)S(1)} %T0_front_solve.1.refs_0_.refs_7_, bf16[1024,1024]{1,0:T(8,128)(2,1)S(1)} %get-tuple-element.51.refs_1_, bf16[1024,384]{1,0:T(8,128)(2,1)S(1)} %get-tuple-element.69.refs_2_, f32[8,128]{1,0:T(8,128)S(1)} %broadcast_in_dim.2.refs_3_.refs_1_), custom_call_target="tpu_custom_call" | custom-call | flops 11500000 | bytes 1 | tf_op jit(solution)/shard_map/G_lift/pallas_call | solution.py:44
  24.9 1.3 %D0_top.1.refs_0_.refs_5_ = bf16[128,768]{1,0:T(8,128)(2,1)S(1)} custom-call(bf16[128,768]{1,0:T(8,128)(2,1)S(1)} %T1_front_solve.1.refs_0_.refs_7_, f32[8,768]{1,0:T(8,128)S(1)} %fusion.8.refs_1_, bf16[128,768]{1,0:T(8,128)(2,1)S(1)} %get-tuple-element.65.refs_0_.refs_2_, bf16[128,768]{1,0:T(8,128)(2,1)S(1)} %collective-permute-done.4.refs_3_, ...), custom_call_target="tpu_custom_call" | custom-call | flops 11500000 | bytes 1 | tf_op jit(solution)/shard_map/D0_top/pallas_call | solution.py:44
  26.3 1.3 %collective-permute-start.7 = (bf16[128,768]{1,0:T(8,128)(2,1)S(1)}, bf16[128,768]{1,0:T(8,128)(2,1)S(1)}, u32[]{:S(2)}, u32[]{:S(2)}) collective-permute-start(bf16[128,768]{1,0:T(8,128)(2,1)S(1)} %get-tuple-element.70.refs_0_.refs_2_), channel_id=1, source_target_pairs={{0,4},{1,5},{2,6},{3,7},{4,0},{5,1},{6,2},{7,3},{8,12},{9,13},{10,... | collective-permute-start | bytes 589832 | tf_op jit(solution)/shard_map/ppermute | solution.py:23
  27.7 0.8 %E0_down_first.1 = (bf16[512,256]{1,0:T(8,128)(2,1)S(1)}, bf16[256,384]{1,0:T(8,128)(2,1)S(1)}) custom-call(bf16[128,768]{1,0:T(8,128)(2,1)S(1)} %D0_top.1.refs_0_.refs_5_, f32[8,128]{1,0:T(8,128)S(1)} %broadcast_in_dim.2.refs_3_.refs_1_, bf16[1024,384]{1,0:T(8,128)(2,1)S(1)} %G_lift.1.refs_0_.refs_2_, ...), custom_call_target="tpu_custom_call" | custom-call | flops 11500000 | bytes 1 | tf_op jit(solution)/shard_map/E0_down_first/pallas_call | solution.py:44
  28.6 1.6 %collective-permute-start.8 = (bf16[512,256]{1,0:T(8,128)(2,1)S(1)}, bf16[512,256]{1,0:T(8,128)(2,1)S(1)}, u32[]{:S(2)}, u32[]{:S(2)}) collective-permute-start(bf16[512,256]{1,0:T(8,128)(2,1)S(1)} %get-tuple-element.74.refs_0_), channel_id=1, source_target_pairs={{0,8},{8,0},{16,24},{24,16},{1,9},{9,1},{17,25},{25,17},{2,10},{10... | collective-permute-start | bytes 786440 | tf_op jit(solution)/shard_map/ppermute | solution.py:23
  31.5 1.6 %collective-permute-start.10 = (bf16[256,768]{1,0:T(8,128)(2,1)S(1)}, bf16[256,768]{1,0:T(8,128)(2,1)S(1)}, u32[]{:S(2)}, u32[]{:S(2)}) collective-permute-start(bf16[256,768]{1,0:T(8,128)(2,1)S(1)} %get-tuple-element.75.refs_0_.refs_2_), channel_id=1, source_target_pairs={{0,4},{1,5},{2,6},{3,7},{4,0},{5,1},{6,2},{7,3},{8,12},{9,13},{10,... | collective-permute-start | bytes 1179656 | tf_op jit(solution)/shard_map/ppermute | solution.py:23
  34.0 1.3 %D1_top.1.refs_0_.refs_5_ = bf16[128,768]{1,0:T(8,128)(2,1)S(1)} custom-call(bf16[256,768]{1,0:T(8,128)(2,1)S(1)} %T2_front_solve.1.refs_0_.refs_7_, f32[8,768]{1,0:T(8,128)S(1)} %fusion.8.refs_1_, bf16[128,768]{1,0:T(8,128)(2,1)S(1)} %get-tuple-element.70.refs_0_.refs_2_, bf16[128,768]{1,0:T(8,128)(2,1)S(1)} %collective-permute-done.7.refs_3_, ...), custom_call_target="tpu_custom_call" | custom-call | flops 11500000 | bytes 1 | tf_op jit(solution)/shard_map/D1_top/pallas_call | solution.py:44
  35.7 1.3 %collective-permute-done.8.refs_2_ = bf16[512,256]{1,0:T(8,128)(2,1)S(1)} collective-permute-done((bf16[512,256]{1,0:T(8,128)(2,1)S(1)}, bf16[512,256]{1,0:T(8,128)(2,1)S(1)}, u32[]{:S(2)}, u32[]{:S(2)}) %collective-permute-start.8) | collective-permute-done | bytes 262176 | tf_op jit(solution)/shard_map/ppermute | solution.py:23
  37.7 1.6 %collective-permute-start.12 = (bf16[512,256]{1,0:T(8,128)(2,1)S(1)}, bf16[512,256]{1,0:T(8,128)(2,1)S(1)}, u32[]{:S(2)}, u32[]{:S(2)}) collective-permute-start(bf16[512,256]{1,0:T(8,128)(2,1)S(1)} %get-tuple-element.80.refs_0_), channel_id=1, source_target_pairs={{0,8},{8,0},{16,24},{24,16},{1,9},{9,1},{17,25},{25,17},{2,10},{10... | collective-permute-start | bytes 786440 | tf_op jit(solution)/shard_map/ppermute | solution.py:23
  39.3 2.6 %collective-permute-start.11 = (bf16[256,256]{1,0:T(8,128)(2,1)S(1)}, bf16[256,256]{1,0:T(8,128)(2,1)S(1)}, u32[]{:S(2)}, u32[]{:S(2)}) collective-permute-start(bf16[256,256]{1,0:T(8,128)(2,1)S(1)} %get-tuple-element.79.refs_0_), channel_id=1, source_target_pairs={{0,16},{8,24},{16,0},{24,8},{1,17},{9,25},{17,1},{25,9},{2,18},{10... | collective-permute-start | bytes 393224 | tf_op jit(solution)/shard_map/ppermute | solution.py:23
  42.1 1.2 %D2_top.1.refs_0_.refs_5_ = bf16[256,768]{1,0:T(8,128)(2,1)S(1)} custom-call(bf16[512,256]{1,0:T(8,128)(2,1)S(1)} %get-tuple-element.80.refs_0_, f32[8,768]{1,0:T(8,128)S(1)} %fusion.8.refs_1_, bf16[256,768]{1,0:T(8,128)(2,1)S(1)} %get-tuple-element.75.refs_0_.refs_2_, bf16[256,768]{1,0:T(8,128)(2,1)S(1)} %collective-permute-done.10.refs_3_, ...), custom_call_target="tpu_custom_call" | custom-call | flops 11500000 | bytes 1 | tf_op jit(solution)/shard_map/D2_top/pallas_call | solution.py:44
  44.0 1.6 %collective-permute-start.14 = (bf16[512,256]{1,0:T(8,128)(2,1)S(1)}, bf16[512,256]{1,0:T(8,128)(2,1)}, u32[]{:S(2)}, u32[]{:S(2)}) collective-permute-start(bf16[512,256]{1,0:T(8,128)(2,1)S(1)} %get-tuple-element.83.refs_0_), channel_id=1, source_target_pairs={{0,8},{8,0},{16,24},{24,16},{1,9},{9,1},{17,25},{25,17},{2,10},{10... | collective-permute-start | bytes 786440 | tf_op jit(solution)/shard_map/ppermute | solution.py:23
  45.6 3.2 %collective-permute-done.11.refs_2_ = bf16[256,256]{1,0:T(8,128)(2,1)S(1)} collective-permute-done((bf16[256,256]{1,0:T(8,128)(2,1)S(1)}, bf16[256,256]{1,0:T(8,128)(2,1)S(1)}, u32[]{:S(2)}, u32[]{:S(2)}) %collective-permute-start.11) | collective-permute-done | bytes 131104 | tf_op jit(solution)/shard_map/ppermute | solution.py:23
  49.8 1.4 %E21_down_first.1 = (bf16[512,256]{1,0:T(8,128)(2,1)}, bf16[256,384]{1,0:T(8,128)(2,1)S(1)}) custom-call(bf16[256,256]{1,0:T(8,128)(2,1)S(1)} %get-tuple-element.87.refs_0_, f32[8,128]{1,0:T(8,128)S(1)} %broadcast_in_dim.2.refs_3_.refs_1_, bf16[1024,384]{1,0:T(8,128)(2,1)S(1)} %G_lift.1.refs_0_.refs_2_, ...), custom_call_target="tpu_custom_call" | custom-call | flops 11500000 | bytes 1 | tf_op jit(solution)/shard_map/E21_down_first/pallas_call | solution.py:44
  51.9 3.3 %collective-permute-start.15 = (bf16[512,256]{1,0:T(8,128)(2,1)}, bf16[512,256]{1,0:T(8,128)(2,1)S(1)}, u32[]{:S(2)}, u32[]{:S(2)}) collective-permute-start(bf16[512,256]{1,0:T(8,128)(2,1)} %get-tuple-element.88.refs_0_), channel_id=1, source_target_pairs={{0,8},{8,0},{16,24},{24,16},{1,9},{9,1},{17,25},{25,17},{2,10},{10... | collective-permute-start | bytes 786440 | tf_op jit(solution)/shard_map/ppermute | solution.py:23
  55.2 0.8 %collective-permute-start.16 = (bf16[256,256]{1,0:T(8,128)(2,1)S(1)}, bf16[256,256]{1,0:T(8,128)(2,1)S(1)}, u32[]{:S(2)}, u32[]{:S(2)}) collective-permute-start(bf16[256,256]{1,0:T(8,128)(2,1)S(1)} %get-tuple-element.87.refs_0_), channel_id=1, source_target_pairs={{0,16},{8,24},{16,0},{24,8},{1,17},{9,25},{17,1},{25,9},{2,18},{10... | collective-permute-start | bytes 393224 | tf_op jit(solution)/shard_map/ppermute | solution.py:23
  56.0 1.0 %F20_add.1 = (bf16[256,256]{1,0:T(8,128)(2,1)S(1)}, f32[256,256]{1,0:T(8,128)S(1)}) custom-call(bf16[512,256]{1,0:T(8,128)(2,1)} %get-tuple-element.88.refs_0_, f32[512,256]{1,0:T(8,128)S(1)} %S20_down_second.1.refs_0_.refs_1_, bf16[512,256]{1,0:T(8,128)(2,1)} %collective-permute-done.14.refs_2_), custom_call_target="tpu_custom_call" | custom-call | flops 11500000 | bytes 1 | tf_op jit(solution)/shard_map/F20_add/pallas_call | solution.py:44
  57.0 2.5 %collective-permute-start.17 = (bf16[256,256]{1,0:T(8,128)(2,1)S(1)}, bf16[256,256]{1,0:T(8,128)(2,1)S(1)}, u32[]{:S(2)}, u32[]{:S(2)}) collective-permute-start(bf16[256,256]{1,0:T(8,128)(2,1)S(1)} %get-tuple-element.89.refs_0_), channel_id=1, source_target_pairs={{0,16},{8,24},{16,0},{24,8},{1,17},{9,25},{17,1},{25,9},{2,18},{10... | collective-permute-start | bytes 393224 | tf_op jit(solution)/shard_map/ppermute | solution.py:23
  59.5 0.9 %copy-done.1 = bf16[256,384]{1,0:T(8,128)(2,1)S(1)} copy-done((bf16[256,384]{1,0:T(8,128)(2,1)S(1)}, bf16[256,384]{1,0:T(8,128)(2,1)}, u32[]{:S(2)}) %copy-start.1) | copy-done | bytes 196632
  60.8 4.3 %collective-permute-done.15.refs_2_ = bf16[512,256]{1,0:T(8,128)(2,1)S(1)} collective-permute-done((bf16[512,256]{1,0:T(8,128)(2,1)}, bf16[512,256]{1,0:T(8,128)(2,1)S(1)}, u32[]{:S(2)}, u32[]{:S(2)}) %collective-permute-start.15) | collective-permute-done | bytes 262176 | tf_op jit(solution)/shard_map/ppermute | solution.py:23
  65.2 1.0 %collective-permute-start.18 = (bf16[256,256]{1,0:T(8,128)(2,1)S(1)}, bf16[256,256]{1,0:T(8,128)(2,1)S(1)}, u32[]{:S(2)}, u32[]{:S(2)}) collective-permute-start(bf16[256,256]{1,0:T(8,128)(2,1)S(1)} %get-tuple-element.91.refs_0_), channel_id=1, source_target_pairs={{0,16},{8,24},{16,0},{24,8},{1,17},{9,25},{17,1},{25,9},{2,18},{10... | collective-permute-start | bytes 393224 | tf_op jit(solution)/shard_map/ppermute | solution.py:23
  66.2 5.0 %collective-permute-done.17.refs_2_ = bf16[256,256]{1,0:T(8,128)(2,1)S(1)} collective-permute-done((bf16[256,256]{1,0:T(8,128)(2,1)S(1)}, bf16[256,256]{1,0:T(8,128)(2,1)S(1)}, u32[]{:S(2)}, u32[]{:S(2)}) %collective-permute-start.17) | collective-permute-done | bytes 131104 | tf_op jit(solution)/shard_map/ppermute | solution.py:23
  71.3 2.4 %collective-permute-done.18.refs_2_ = bf16[256,256]{1,0:T(8,128)(2,1)S(1)} collective-permute-done((bf16[256,256]{1,0:T(8,128)(2,1)S(1)}, bf16[256,256]{1,0:T(8,128)(2,1)S(1)}, u32[]{:S(2)}, u32[]{:S(2)}) %collective-permute-start.18) | collective-permute-done | bytes 131104 | tf_op jit(solution)/shard_map/ppermute | solution.py:23
  73.9 1.1 %broadcast_select_fusion = f32[1,256,1024]{2,1,0:T(8,128)} fusion(f32[1,256,1024]{2,1,0:T(8,128)S(1)} %bitcast_dynamic-update-slice_fusion.1, f32[1,256,1024]{2,1,0:T(8,128)S(1)} %get-tuple-element.95, pred[]{:T(512)S(6)} %eq.3), kind=kLoop, calls=%fused_computation | loop fusion | flops 262144 | bytes 3145729 | tf_op jit(solution)/shard_map/jit(_where)/select_n | solution.py:447
  (57 shorter events, 10.7 us)
Async XLA Ops:
  4.8 3.1 %collective-permute-start = (bf16[256,768]{1,0:T(8,128)(2,1)S(1)}, bf16[256,768]{1,0:T(8,128)(2,1)S(1)}, u32[]{:S(2)}, u32[]{:S(2)}) collective-permute-start(bf16[256,768]{1,0:T(8,128)(2,1)S(1)} %get-tuple-element.56), channel_id=1, source_target_pairs={{0,1},{1,0},{2,3},{3,2},{4,5},{5,4},{6,7},{7,6},{8,9},{9,8},{10,11... | collective-permute-start | bytes 1179656 | tf_op jit(solution)/shard_map/ppermute | solution.py:23
  5.3 2.5 %copy-start.2 = (s32[3]{0:T(128)S(1)}, s32[3]{0:T(128)}, u32[]{:S(2)}) copy-start(s32[3]{0:T(128)} %param.12) | copy-start | bytes 40
  7.7 11.3 %collective-permute-start.2 = (bf16[256,768]{1,0:T(8,128)(2,1)S(1)}, bf16[256,768]{1,0:T(8,128)(2,1)S(1)}, u32[]{:S(2)}, u32[]{:S(2)}) collective-permute-start(bf16[256,768]{1,0:T(8,128)(2,1)S(1)} %get-tuple-element.66), channel_id=1, source_target_pairs={{0,1},{1,0},{2,3},{3,2},{4,5},{5,4},{6,7},{7,6},{8,9},{9,8},{10,11... | collective-permute-start | bytes 1179656 | tf_op jit(solution)/shard_map/ppermute | solution.py:23
  8.7 8.1 %collective-permute-start.1 = (bf16[128,768]{1,0:T(8,128)(2,1)S(1)}, bf16[128,768]{1,0:T(8,128)(2,1)S(1)}, u32[]{:S(2)}, u32[]{:S(2)}) collective-permute-start(bf16[128,768]{1,0:T(8,128)(2,1)S(1)} %get-tuple-element.59.refs_0_.refs_2_), channel_id=1, source_target_pairs={{0,2},{1,3},{2,0},{3,1},{4,6},{5,7},{6,4},{7,5},{8,10},{9,11},{10,... | collective-permute-start | bytes 589832 | tf_op jit(solution)/shard_map/ppermute | solution.py:23
  15.9 8.1 %collective-permute-start.3 = (bf16[128,768]{1,0:T(8,128)(2,1)S(1)}, bf16[128,768]{1,0:T(8,128)(2,1)S(1)}, u32[]{:S(2)}, u32[]{:S(2)}) collective-permute-start(bf16[128,768]{1,0:T(8,128)(2,1)S(1)} %get-tuple-element.63.refs_0_.refs_2_), channel_id=1, source_target_pairs={{0,2},{1,3},{2,0},{3,1},{4,6},{5,7},{6,4},{7,5},{8,10},{9,11},{10,... | collective-permute-start | bytes 589832 | tf_op jit(solution)/shard_map/ppermute | solution.py:23
  17.2 7.7 %collective-permute-start.4 = (bf16[128,768]{1,0:T(8,128)(2,1)S(1)}, bf16[128,768]{1,0:T(8,128)(2,1)S(1)}, u32[]{:S(2)}, u32[]{:S(2)}) collective-permute-start(bf16[128,768]{1,0:T(8,128)(2,1)S(1)} %get-tuple-element.65.refs_0_.refs_2_), channel_id=1, source_target_pairs={{0,4},{1,5},{2,6},{3,7},{4,0},{5,1},{6,2},{7,3},{8,12},{9,13},{10,... | collective-permute-start | bytes 589832 | tf_op jit(solution)/shard_map/ppermute | solution.py:23
  20.0 11.0 %collective-permute-start.6 = (bf16[256,768]{1,0:T(8,128)(2,1)S(1)}, bf16[256,768]{1,0:T(8,128)(2,1)S(1)}, u32[]{:S(2)}, u32[]{:S(2)}) collective-permute-start(bf16[256,768]{1,0:T(8,128)(2,1)S(1)} %get-tuple-element.67.refs_0_.refs_2_), channel_id=1, source_target_pairs={{0,2},{1,3},{2,0},{3,1},{4,6},{5,7},{6,4},{7,5},{8,10},{9,11},{10,... | collective-permute-start | bytes 1179656 | tf_op jit(solution)/shard_map/ppermute | solution.py:23
  26.2 1.5 %collective-permute-start.5 = (bf16[128,768]{1,0:T(8,128)(2,1)S(1)}, bf16[128,768]{1,0:T(8,128)(2,1)S(1)}, u32[]{:S(2)}, u32[]{:S(2)}) collective-permute-start(bf16[128,768]{1,0:T(8,128)(2,1)S(1)} %D0_top.1.refs_0_.refs_5_), channel_id=1, source_target_pairs={{0,1},{1,0},{2,3},{3,2},{4,5},{5,4},{6,7},{7,6},{8,9},{9,8},{10,11... | collective-permute-start | bytes 589832 | tf_op jit(solution)/shard_map/ppermute | solution.py:23
  26.3 7.7 %collective-permute-start.7 = (bf16[128,768]{1,0:T(8,128)(2,1)S(1)}, bf16[128,768]{1,0:T(8,128)(2,1)S(1)}, u32[]{:S(2)}, u32[]{:S(2)}) collective-permute-start(bf16[128,768]{1,0:T(8,128)(2,1)S(1)} %get-tuple-element.70.refs_0_.refs_2_), channel_id=1, source_target_pairs={{0,4},{1,5},{2,6},{3,7},{4,0},{5,1},{6,2},{7,3},{8,12},{9,13},{10,... | collective-permute-start | bytes 589832 | tf_op jit(solution)/shard_map/ppermute | solution.py:23
  28.6 8.4 %collective-permute-start.8 = (bf16[512,256]{1,0:T(8,128)(2,1)S(1)}, bf16[512,256]{1,0:T(8,128)(2,1)S(1)}, u32[]{:S(2)}, u32[]{:S(2)}) collective-permute-start(bf16[512,256]{1,0:T(8,128)(2,1)S(1)} %get-tuple-element.74.refs_0_), channel_id=1, source_target_pairs={{0,8},{8,0},{16,24},{24,16},{1,9},{9,1},{17,25},{25,17},{2,10},{10... | collective-permute-start | bytes 786440 | tf_op jit(solution)/shard_map/ppermute | solution.py:23
  31.5 10.6 %collective-permute-start.10 = (bf16[256,768]{1,0:T(8,128)(2,1)S(1)}, bf16[256,768]{1,0:T(8,128)(2,1)S(1)}, u32[]{:S(2)}, u32[]{:S(2)}) collective-permute-start(bf16[256,768]{1,0:T(8,128)(2,1)S(1)} %get-tuple-element.75.refs_0_.refs_2_), channel_id=1, source_target_pairs={{0,4},{1,5},{2,6},{3,7},{4,0},{5,1},{6,2},{7,3},{8,12},{9,13},{10,... | collective-permute-start | bytes 1179656 | tf_op jit(solution)/shard_map/ppermute | solution.py:23
  35.3 1.7 %collective-permute-start.9 = (bf16[128,768]{1,0:T(8,128)(2,1)S(1)}, bf16[128,768]{1,0:T(8,128)(2,1)S(1)}, u32[]{:S(2)}, u32[]{:S(2)}) collective-permute-start(bf16[128,768]{1,0:T(8,128)(2,1)S(1)} %D1_top.1.refs_0_.refs_5_), channel_id=1, source_target_pairs={{0,1},{1,0},{2,3},{3,2},{4,5},{5,4},{6,7},{7,6},{8,9},{9,8},{10,11... | collective-permute-start | bytes 589832 | tf_op jit(solution)/shard_map/ppermute | solution.py:23
  37.7 12.1 %collective-permute-start.12 = (bf16[512,256]{1,0:T(8,128)(2,1)S(1)}, bf16[512,256]{1,0:T(8,128)(2,1)S(1)}, u32[]{:S(2)}, u32[]{:S(2)}) collective-permute-start(bf16[512,256]{1,0:T(8,128)(2,1)S(1)} %get-tuple-element.80.refs_0_), channel_id=1, source_target_pairs={{0,8},{8,0},{16,24},{24,16},{1,9},{9,1},{17,25},{25,17},{2,10},{10... | collective-permute-start | bytes 786440 | tf_op jit(solution)/shard_map/ppermute | solution.py:23
  39.3 9.5 %collective-permute-start.11 = (bf16[256,256]{1,0:T(8,128)(2,1)S(1)}, bf16[256,256]{1,0:T(8,128)(2,1)S(1)}, u32[]{:S(2)}, u32[]{:S(2)}) collective-permute-start(bf16[256,256]{1,0:T(8,128)(2,1)S(1)} %get-tuple-element.79.refs_0_), channel_id=1, source_target_pairs={{0,16},{8,24},{16,0},{24,8},{1,17},{9,25},{17,1},{25,9},{2,18},{10... | collective-permute-start | bytes 393224 | tf_op jit(solution)/shard_map/ppermute | solution.py:23
  43.3 6.6 %collective-permute-start.13 = (bf16[256,768]{1,0:T(8,128)(2,1)S(1)}, bf16[256,768]{1,0:T(8,128)(2,1)S(1)}, u32[]{:S(2)}, u32[]{:S(2)}) collective-permute-start(bf16[256,768]{1,0:T(8,128)(2,1)S(1)} %D2_top.1.refs_0_.refs_5_), channel_id=1, source_target_pairs={{0,1},{1,0},{2,3},{3,2},{4,5},{5,4},{6,7},{7,6},{8,9},{9,8},{10,11... | collective-permute-start | bytes 1179656 | tf_op jit(solution)/shard_map/ppermute | solution.py:23
  44.0 12.0 %collective-permute-start.14 = (bf16[512,256]{1,0:T(8,128)(2,1)S(1)}, bf16[512,256]{1,0:T(8,128)(2,1)}, u32[]{:S(2)}, u32[]{:S(2)}) collective-permute-start(bf16[512,256]{1,0:T(8,128)(2,1)S(1)} %get-tuple-element.83.refs_0_), channel_id=1, source_target_pairs={{0,8},{8,0},{16,24},{24,16},{1,9},{9,1},{17,25},{25,17},{2,10},{10... | collective-permute-start | bytes 786440 | tf_op jit(solution)/shard_map/ppermute | solution.py:23
  51.2 0.7 copy-start
  51.9 13.3 %collective-permute-start.15 = (bf16[512,256]{1,0:T(8,128)(2,1)}, bf16[512,256]{1,0:T(8,128)(2,1)S(1)}, u32[]{:S(2)}, u32[]{:S(2)}) collective-permute-start(bf16[512,256]{1,0:T(8,128)(2,1)} %get-tuple-element.88.refs_0_), channel_id=1, source_target_pairs={{0,8},{8,0},{16,24},{24,16},{1,9},{9,1},{17,25},{25,17},{2,10},{10... | collective-permute-start | bytes 786440 | tf_op jit(solution)/shard_map/ppermute | solution.py:23
  55.2 11.0 %collective-permute-start.16 = (bf16[256,256]{1,0:T(8,128)(2,1)S(1)}, bf16[256,256]{1,0:T(8,128)(2,1)S(1)}, u32[]{:S(2)}, u32[]{:S(2)}) collective-permute-start(bf16[256,256]{1,0:T(8,128)(2,1)S(1)} %get-tuple-element.87.refs_0_), channel_id=1, source_target_pairs={{0,16},{8,24},{16,0},{24,8},{1,17},{9,25},{17,1},{25,9},{2,18},{10... | collective-permute-start | bytes 393224 | tf_op jit(solution)/shard_map/ppermute | solution.py:23
  57.0 14.2 %collective-permute-start.17 = (bf16[256,256]{1,0:T(8,128)(2,1)S(1)}, bf16[256,256]{1,0:T(8,128)(2,1)S(1)}, u32[]{:S(2)}, u32[]{:S(2)}) collective-permute-start(bf16[256,256]{1,0:T(8,128)(2,1)S(1)} %get-tuple-element.89.refs_0_), channel_id=1, source_target_pairs={{0,16},{8,24},{16,0},{24,8},{1,17},{9,25},{17,1},{25,9},{2,18},{10... | collective-permute-start | bytes 393224 | tf_op jit(solution)/shard_map/ppermute | solution.py:23
  59.5 0.9 %copy-start.1 = (bf16[256,384]{1,0:T(8,128)(2,1)S(1)}, bf16[256,384]{1,0:T(8,128)(2,1)}, u32[]{:S(2)}) copy-start(bf16[256,384]{1,0:T(8,128)(2,1)} %copy-done) | copy-start | bytes 589828
  65.2 8.5 %collective-permute-start.18 = (bf16[256,256]{1,0:T(8,128)(2,1)S(1)}, bf16[256,256]{1,0:T(8,128)(2,1)S(1)}, u32[]{:S(2)}, u32[]{:S(2)}) collective-permute-start(bf16[256,256]{1,0:T(8,128)(2,1)S(1)} %get-tuple-element.91.refs_0_), channel_id=1, source_target_pairs={{0,16},{8,24},{16,0},{24,8},{1,17},{9,25},{17,1},{25,9},{2,18},{10... | collective-permute-start | bytes 393224 | tf_op jit(solution)/shard_map/ppermute | solution.py:23

commit v3 on v2

--- a/solution.py
+++ b/solution.py
@@ -9,10 +9,10 @@
 
 WIDE = jnp.float32
 NARROW = jnp.bfloat16
-VMEM_LIMIT = 24 * 1024 * 1024
+VMEM_LIMIT = 16 * 1024 * 1024
 SHARES = (1, 1, 2)
 GROUPS = ((0, 1), (2,))
-PARTS = ((((0, 0, 1), (1, 0, 1)),), (((0, 0, 1), (1, 0, 1)),), (((0, 0, 2),), ((1, 0, 2),)))
+PARTS = ((((0, 0, 1), (1, 0, 1)),), (((0, 0, 1), (1, 0, 1)),), (((0, 0, 2),), ((1, 0, 1),), ((1, 1, 1),)))
 COST = 0.01
 TILES = 2
 
@@ -35,8 +35,11 @@
         self.tag = None
         self.cost = COST
 
-    def __call__(self, kernel, outs, scalars, arrays, name, far=(), out_space=pltpu.VMEM, scratch=()):
+    def __call__(self, kernel, outs, scalars, arrays, name, far=(), spaces=None, scratch=(), place=None):
         after = [] if self.last is None else [self.last]
+        spaces = spaces or [pltpu.VMEM] * len(outs)
+        taken = [] if place is None else [place]
+        aliases = {len(after) + len(scalars) + len(arrays): 0} if taken else {}
 
         def run(*refs):
             kernel(*refs[len(after) :])
@@ -47,16 +50,18 @@
             in_specs=[pl.BlockSpec(memory_space=pl.ANY)] * len(after)
             + [pl.BlockSpec(memory_space=pltpu.SMEM)] * len(scalars)
             + [pl.BlockSpec(memory_space=pltpu.VMEM)] * len(arrays)
+            + [pl.BlockSpec(memory_space=pltpu.HBM)] * len(taken)
             + [pl.BlockSpec(memory_space=pl.ANY)] * len(far),
-            out_specs=[pl.BlockSpec(memory_space=out_space)] * len(outs),
+            out_specs=[pl.BlockSpec(memory_space=space) for space in spaces],
+            input_output_aliases=aliases,
             scratch_shapes=scratch,
             cost_estimate=pl.CostEstimate(
                 flops=int(self.cost * 1.15e9), bytes_accessed=1, transcendentals=0
             ),
             compiler_params=pltpu.CompilerParams(vmem_limit_bytes=VMEM_LIMIT),
             name=self.tag + "_" + name,
-        )(*after, *scalars, *arrays, *[pltpu.with_memory_space_constraint(a, pltpu.HBM) for a in far])
-        self.last = results[0]
+        )(*after, *scalars, *arrays, *taken, *[pltpu.with_memory_space_constraint(a, pltpu.HBM) for a in far])
+        self.last = results[-1]
         return results
 
 
@@ -227,8 +232,21 @@
     rest[...] = total[rows:]
 
 
-def last_add_kernel(kept, came, total):
+def finish_kernel(spans, kept, came, *refs):
+    out, token, total, sems = refs[-4:]
+    count = out.shape[1] // 2
+    core = lax.axis_index("leaf") & 1
     total[...] = kept[...] + came[...].astype(WIDE)
+    token[...] = jnp.zeros_like(token)
+    copies, at = [], 0
+    for number, (side, start, width) in enumerate(spans):
+        column = (core if side == 0 else 1 - core) * count + start
+        target = out.at[:, pl.ds(pl.multiple_of(column, 128), width)]
+        copies.append(pltpu.make_async_copy(total.at[:, pl.ds(at, width)], target, sems.at[number]))
+        copies[-1].start()
+        at += width
+    for copy in copies:
+        copy.wait()
 
 
 def body(
@@ -244,7 +262,6 @@
     levels = lax.axis_size("leaf").bit_length() - 1
     shifts = lax.axis_size("shift")
     steps = shifts.bit_length() - 1
-    core = lax.axis_index("leaf") & 1
     inverse_in, coupling_in, rhs_in = leaf_inverse[0, 0], leaf_coupling[0, 0], leaf_rhs[0]
     fronts_in, links_in = front_inverse[0, :, 0], front_coupling[0, :, 0]
     order, columns = rhs_in.shape
@@ -410,9 +427,13 @@
 
     def last(n, part=0):
         s = state[n]
-        (s["total", part],) = chain(
-            last_add_kernel, [((block, pieces(n, part)[1]), WIDE)], [],
-            [s["kept", part], s["sum_came", part]], "last_add",
+        spans, width = pieces(n, part)
+        targets = tuple((side, offsets[n] + start, size) for side, start, size in spans)
+        held["out"], _ = chain(
+            functools.partial(finish_kernel, targets), [((block, columns), WIDE), ((8, 128), WIDE)], [],
+            [s["kept", part], s["sum_came", part]], "finish", place=held.get("out"),
+            spaces=[pltpu.HBM, pltpu.VMEM],
+            scratch=[pltpu.VMEM((block, width), WIDE), pltpu.SemaphoreType.DMA((len(spans),))],
         )
 
     run = {
@@ -433,21 +454,10 @@
         chain.cost = float(cost or COST)
         run[step[0]](*[int(digit) for digit in chain.tag[1:] or "0"])
 
-    sides = {}
-    for n, chunk in enumerate(PARTS):
-        for part in range(len(chunk)):
-            at = 0
-            for side, start, width in pieces(n, part)[0]:
-                sides[side, offsets[n] + start] = state[n]["total", part][:, at : at + width]
-                at += width
-    owned = [sides[key] for key in sorted(sides) if not key[0]]
-    others = [sides[key] for key in sorted(sides) if key[0]]
-    low = jnp.concatenate(owned + others, axis=1)
-    high = jnp.concatenate(others + owned, axis=1)
-    return jnp.where(core == 0, low, high)[None]
-
-
-ORDER = ("A0", "A1", "B0", "Q", "B1", "C0", "B2", "T0", "G", "C1", "T1", "D0", "E0", "C2", "T2", "D1", "S0", "F0", "E1", "D2", "E20", "Z0", "S20", "S1", "F1:3", "E21", "F20", "S21", "F21", "Z1", "Z20", "Z21")
+    return held["out"][None]
+
+
+ORDER = ("A0", "A1", "B0:0.5", "Q", "B1", "C0:0.5", "B2", "G", "C1", "T1", "T0", "D0", "E0", "C2", "S0", "D1", "F0:0.5", "E1", "T2", "D2", "E20", "S1", "F1", "Z0:3", "E21", "S20", "S21", "E22", "F20", "S22", "Z1", "F21", "F22", "Z20", "Z21", "Z22:0.5")
 
 
 def solution(mesh):

time: 75.3 us -> 73.9 us (0.981)
  waiting for transfers between devices: 18.7 us -> 14 us
  starting transfers between devices: 25.4 us -> 28.5 us
  Pallas kernels: 27 us -> 30 us
  local copies, waits for them, and re-layouts: 1.82 us -> 0.01 us
  other arithmetic: 1.19 us -> 0.07 us
    ppermute x19 -> x21, waiting for transfers between devices: 18.7 us -> 14 us  [exchange(): return lax.ppermute(value, axis, pairs)]
    ppermute x19 -> x21, starting transfers between devices: 25.4 us -> 28.5 us  [exchange(): return lax.ppermute(value, axis, pairs)]
    pallas_call x32 -> x36, Pallas kernels: 27 us -> 30 us  [__call__(): pl.pallas_call(run, out_shape=[jax.ShapeDtypeStruct(shape, kind) for shap...]
    unnamed x13 -> x2, local copies, waits for them, and re-layouts: 1.73 us -> 0.01 us
    select_n x1 -> x0, other arithmetic: 1.12 us -> none  [body(): return jnp.where(core == 0, low, high)[None]]
  transfers between devices with their start and end apart: 19 -> 21, of which waited for: 11 -> 9; matrix products, arithmetic and copies ran while one was open for 0% -> 0% of each run, Pallas kernels for 29% -> 32%
where the time goes in v3:
time: 73.9 us; the launch traced here: 73.7 us
  Pallas kernels  30 us (41%)
  starting transfers between devices  28.5 us (39%)
  waiting for transfers between devices  14 us (19%)
  between operations  1.13 us (2%)
    pallas_call x36, Pallas kernels, __call__(): pl.pallas_call(run, out_shape=[jax.ShapeDtypeStruct(shape, kind) for shap...  30 us
    ppermute x21, starting transfers between devices, exchange(): return lax.ppermute(value, axis, pairs)  28.5 us
    ppermute x21, waiting for transfers between devices, exchange(): return lax.ppermute(value, axis, pairs)  14 us
  transfers between devices with their start and end apart: 21, of which 9 were waited for; matrix products, arithmetic and copies ran while one was open for 0% of the time, Pallas kernels for 32%

profile of v3, /device:TPU:0, one launch (start us, length us, event | category | flops | bytes accessed | tf_op | source)
XLA Modules:
  0.0 73.7 jit_solution(5325894766769653849)
XLA Ops:
  0.0 4.8 %A0_leaf_up.1 = (bf16[256,768]{1,0:T(8,128)(2,1)S(1)}, bf16[256,768]{1,0:T(8,128)(2,1)S(1)}, bf16[1024,512]{1,0:T(8,128)(2,1)S(1)}, bf16[768,384]{1,0:T(8,128)(2...) custom-call(bf16[1024,1024]{1,0:T(8,128)(2,1)} %bitcast.12, ...), custom_call_target="tpu_custom_call" | custom-call | flops 11500000 | bytes 1 | tf_op jit(solution)/shard_map/A0_leaf_up/pallas_call | solution.py:47
  5.3 2.4 %A1_leaf_up.1 = (bf16[256,768]{1,0:T(8,128)(2,1)S(1)}, bf16[256,768]{1,0:T(8,128)(2,1)S(1)}, bf16[1024,512]{1,0:T(8,128)(2,1)S(1)}, bf16[2,768,768]{2,1,0:T(8,128)(2,1)S(1)}, bf16[1,768,768]{2,1,0:T(8,128)(2,1)S(1)}) custom-call(bf16[768,768]{1,0:T(8,128)(2,1)S(1)} %get-tuple-element.63.refs_0_.refs_5_.refs_3_, ...), custom_call_target="tpu_custom_call" | custom-call | flops 11500000 | bytes 1 | tf_op jit(solution)/shard_map/A1_leaf_up/pallas_call | solution.py:47
  7.9 0.8 %B0_front_up.1 = (bf16[128,768]{1,0:T(8,128)(2,1)S(1)}, bf16[128,768]{1,0:T(8,128)(2,1)S(1)}) custom-call(bf16[1,768,768]{2,1,0:T(8,128)(2,1)S(1)} %get-tuple-element.68.refs_0_.refs_5_, f32[8,768]{1,0:T(8,128)S(1)} %fusion.refs_1_, bf16[256,768]{1,0:T(8,128)(2,1)S(1)} %get-tuple-element.69.refs_2_, bf16[256,768]{1,0:T(8,128)(2,1)S(1)} %collective-permute-done.refs_3_, ...), custom_call_target="tpu_custom_call" | custom-call | flops 575000000 | bytes 1 | tf_op jit(solution)/shard_map/B0_front_up/pallas_call | solution.py:47
  8.7 3.0 %collective-permute-start.1 = (bf16[128,768]{1,0:T(8,128)(2,1)S(1)}, bf16[128,768]{1,0:T(8,128)(2,1)S(1)}, u32[]{:S(2)}, u32[]{:S(2)}) collective-permute-start(bf16[128,768]{1,0:T(8,128)(2,1)S(1)} %get-tuple-element.76.refs_2_), channel_id=1, source_target_pairs={{0,2},{1,3},{2,0},{3,1},{4,6},{5,7},{6,4},{7,5},{8,10},{9,11},{10,... | collective-permute-start | bytes 589832 | tf_op jit(solution)/shard_map/ppermute | solution.py:23
  11.7 3.3 %Q_products.1 = (bf16[2,768,768]{2,1,0:T(8,128)(2,1)S(1)}, bf16[1,768,768]{2,1,0:T(8,128)(2,1)S(1)}) custom-call(bf16[128,768]{1,0:T(8,128)(2,1)S(1)} %get-tuple-element.72.refs_0_.refs_6_, f32[8,768]{1,0:T(8,128)S(1)} %fusion.refs_1_, bf16[768,768]{1,0:T(8,128)(2,1)S(1)} %get-tuple-element.71.refs_4_.refs_2_, ...), custom_call_target="tpu_custom_call" | custom-call | flops 11500000 | bytes 1 | tf_op jit(solution)/shard_map/Q_products/pallas_call | solution.py:47
  15.1 0.8 %B1_front_up.1 = (bf16[128,768]{1,0:T(8,128)(2,1)S(1)}, bf16[128,768]{1,0:T(8,128)(2,1)S(1)}) custom-call(bf16[1,768,768]{2,1,0:T(8,128)(2,1)S(1)} %get-tuple-element.74.refs_0_.refs_4_, f32[8,768]{1,0:T(8,128)S(1)} %fusion.refs_1_, bf16[256,768]{1,0:T(8,128)(2,1)S(1)} %get-tuple-element.69.refs_2_, bf16[256,768]{1,0:T(8,128)(2,1)S(1)} %collective-permute-done.refs_3_, ...), custom_call_target="tpu_custom_call" | custom-call | flops 11500000 | bytes 1 | tf_op jit(solution)/shard_map/B1_front_up/pallas_call | solution.py:47
  16.0 0.9 %collective-permute-done.1.refs_3_ = bf16[128,768]{1,0:T(8,128)(2,1)S(1)} collective-permute-done((bf16[128,768]{1,0:T(8,128)(2,1)S(1)}, bf16[128,768]{1,0:T(8,128)(2,1)S(1)}, u32[]{:S(2)}, u32[]{:S(2)}) %collective-permute-start.1) | collective-permute-done | bytes 196640 | tf_op jit(solution)/shard_map/ppermute | solution.py:23
  17.2 1.8 %collective-permute-start.4 = (bf16[128,768]{1,0:T(8,128)(2,1)S(1)}, bf16[128,768]{1,0:T(8,128)(2,1)S(1)}, u32[]{:S(2)}, u32[]{:S(2)}) collective-permute-start(bf16[128,768]{1,0:T(8,128)(2,1)S(1)} %get-tuple-element.84.refs_2_), channel_id=1, source_target_pairs={{0,4},{1,5},{2,6},{3,7},{4,0},{5,1},{6,2},{7,3},{8,12},{9,13},{10,... | collective-permute-start | bytes 589832 | tf_op jit(solution)/shard_map/ppermute | solution.py:23
  19.0 1.0 %B2_front_up.1 = (bf16[256,768]{1,0:T(8,128)(2,1)S(1)}, bf16[256,768]{1,0:T(8,128)(2,1)S(1)}) custom-call(bf16[128,768]{1,0:T(8,128)(2,1)S(1)} %get-tuple-element.77.refs_0_.refs_2_, f32[8,768]{1,0:T(8,128)S(1)} %fusion.refs_1_, bf16[256,768]{1,0:T(8,128)(2,1)S(1)} %get-tuple-element.78.refs_2_, bf16[256,768]{1,0:T(8,128)(2,1)S(1)} %collective-permute-done.2.refs_3_, ...), custom_call_target="tpu_custom_call" | custom-call | flops 11500000 | bytes 1 | tf_op jit(solution)/shard_map/B2_front_up/pallas_call | solution.py:47
  20.0 1.5 %collective-permute-start.6 = (bf16[256,768]{1,0:T(8,128)(2,1)S(1)}, bf16[256,768]{1,0:T(8,128)(2,1)S(1)}, u32[]{:S(2)}, u32[]{:S(2)}) collective-permute-start(bf16[256,768]{1,0:T(8,128)(2,1)S(1)} %get-tuple-element.88.refs_2_), channel_id=1, source_target_pairs={{0,2},{1,3},{2,0},{3,1},{4,6},{5,7},{6,4},{7,5},{8,10},{9,11},{10,... | collective-permute-start | bytes 1179656 | tf_op jit(solution)/shard_map/ppermute | solution.py:23
  22.2 1.3 %G_lift.1.refs_0_.refs_2_ = bf16[1024,384]{1,0:T(8,128)(2,1)S(1)} custom-call(bf16[256,768]{1,0:T(8,128)(2,1)S(1)} %get-tuple-element.80.refs_0_.refs_6_, bf16[1024,1024]{1,0:T(8,128)(2,1)S(1)} %get-tuple-element.64.refs_1_, bf16[1024,384]{1,0:T(8,128)(2,1)S(1)} %get-tuple-element.81.refs_2_, f32[8,128]{1,0:T(8,128)S(1)} %broadcast_in_dim.4.refs_3_.refs_1_), custom_call_target="tpu_custom_call" | custom-call | flops 11500000 | bytes 1 | tf_op jit(solution)/shard_map/G_lift/pallas_call | solution.py:47
  24.9 1.3 %D0_top.1.refs_0_.refs_5_ = bf16[128,768]{1,0:T(8,128)(2,1)S(1)} custom-call(bf16[128,768]{1,0:T(8,128)(2,1)S(1)} %T0_front_solve.1.refs_0_.refs_7_, f32[8,768]{1,0:T(8,128)S(1)} %fusion.refs_1_, bf16[128,768]{1,0:T(8,128)(2,1)S(1)} %get-tuple-element.84.refs_2_, bf16[128,768]{1,0:T(8,128)(2,1)S(1)} %collective-permute-done.4.refs_3_, ...), custom_call_target="tpu_custom_call" | custom-call | flops 11500000 | bytes 1 | tf_op jit(solution)/shard_map/D0_top/pallas_call | solution.py:47
  26.3 1.9 %collective-permute-start.7 = (bf16[128,768]{1,0:T(8,128)(2,1)S(1)}, bf16[128,768]{1,0:T(8,128)(2,1)S(1)}, u32[]{:S(2)}, u32[]{:S(2)}) collective-permute-start(bf16[128,768]{1,0:T(8,128)(2,1)S(1)} %get-tuple-element.90.refs_2_), channel_id=1, source_target_pairs={{0,4},{1,5},{2,6},{3,7},{4,0},{5,1},{6,2},{7,3},{8,12},{9,13},{10,... | collective-permute-start | bytes 589832 | tf_op jit(solution)/shard_map/ppermute | solution.py:23
  28.2 0.8 %E0_down_first.1 = (bf16[512,256]{1,0:T(8,128)(2,1)S(1)}, bf16[256,384]{1,0:T(8,128)(2,1)S(1)}) custom-call(bf16[128,768]{1,0:T(8,128)(2,1)S(1)} %D0_top.1.refs_0_.refs_5_, f32[8,128]{1,0:T(8,128)S(1)} %broadcast_in_dim.4.refs_3_.refs_1_, bf16[1024,384]{1,0:T(8,128)(2,1)S(1)} %G_lift.1.refs_0_.refs_2_, ...), custom_call_target="tpu_custom_call" | custom-call | flops 11500000 | bytes 1 | tf_op jit(solution)/shard_map/E0_down_first/pallas_call | solution.py:47
  29.0 1.6 %collective-permute-start.8 = (bf16[512,256]{1,0:T(8,128)(2,1)S(1)}, bf16[512,256]{1,0:T(8,128)(2,1)S(1)}, u32[]{:S(2)}, u32[]{:S(2)}) collective-permute-start(bf16[512,256]{1,0:T(8,128)(2,1)S(1)} %get-tuple-element.91), channel_id=1, source_target_pairs={{0,8},{8,0},{16,24},{24,16},{1,9},{9,1},{17,25},{25,17},{2,10},{10... | collective-permute-start | bytes 786440 | tf_op jit(solution)/shard_map/ppermute | solution.py:23
  31.4 1.6 %collective-permute-start.10 = (bf16[256,768]{1,0:T(8,128)(2,1)S(1)}, bf16[256,768]{1,0:T(8,128)(2,1)S(1)}, u32[]{:S(2)}, u32[]{:S(2)}) collective-permute-start(bf16[256,768]{1,0:T(8,128)(2,1)S(1)} %get-tuple-element.94.refs_2_), channel_id=1, source_target_pairs={{0,4},{1,5},{2,6},{3,7},{4,0},{5,1},{6,2},{7,3},{8,12},{9,13},{10,... | collective-permute-start | bytes 1179656 | tf_op jit(solution)/shard_map/ppermute | solution.py:23
  33.6 1.3 %D1_top.1.refs_0_.refs_5_ = bf16[128,768]{1,0:T(8,128)(2,1)S(1)} custom-call(f32[512,256]{1,0:T(8,128)S(1)} %S0_down_second.1.refs_0_.refs_1_, f32[8,768]{1,0:T(8,128)S(1)} %fusion.refs_1_, bf16[128,768]{1,0:T(8,128)(2,1)S(1)} %get-tuple-element.90.refs_2_, bf16[128,768]{1,0:T(8,128)(2,1)S(1)} %collective-permute-done.7.refs_3_, ...), custom_call_target="tpu_custom_call" | custom-call | flops 11500000 | bytes 1 | tf_op jit(solution)/shard_map/D1_top/pallas_call | solution.py:47
  35.0 2.4 %collective-permute-done.8.refs_2_ = bf16[512,256]{1,0:T(8,128)(2,1)S(1)} collective-permute-done((bf16[512,256]{1,0:T(8,128)(2,1)S(1)}, bf16[512,256]{1,0:T(8,128)(2,1)S(1)}, u32[]{:S(2)}, u32[]{:S(2)}) %collective-permute-start.8) | collective-permute-done | bytes 262176 | tf_op jit(solution)/shard_map/ppermute | solution.py:23
  38.1 1.6 %collective-permute-start.11 = (bf16[512,256]{1,0:T(8,128)(2,1)S(1)}, bf16[512,256]{1,0:T(8,128)(2,1)S(1)}, u32[]{:S(2)}, u32[]{:S(2)}) collective-permute-start(bf16[512,256]{1,0:T(8,128)(2,1)S(1)} %get-tuple-element.97), channel_id=1, source_target_pairs={{0,8},{8,0},{16,24},{24,16},{1,9},{9,1},{17,25},{25,17},{2,10},{10... | collective-permute-start | bytes 786440 | tf_op jit(solution)/shard_map/ppermute | solution.py:23
  39.8 2.6 %collective-permute-start.12 = (bf16[256,256]{1,0:T(8,128)(2,1)S(1)}, bf16[256,256]{1,0:T(8,128)(2,1)S(1)}, u32[]{:S(2)}, u32[]{:S(2)}) collective-permute-start(bf16[256,256]{1,0:T(8,128)(2,1)S(1)} %get-tuple-element.99), channel_id=1, source_target_pairs={{0,16},{8,24},{16,0},{24,8},{1,17},{9,25},{17,1},{25,9},{2,18},{10... | collective-permute-start | bytes 393224 | tf_op jit(solution)/shard_map/ppermute | solution.py:23
  42.9 1.2 %D2_top.1.refs_0_.refs_5_ = bf16[256,768]{1,0:T(8,128)(2,1)S(1)} custom-call(bf16[256,768]{1,0:T(8,128)(2,1)S(1)} %T2_front_solve.1.refs_0_.refs_7_, f32[8,768]{1,0:T(8,128)S(1)} %fusion.refs_1_, bf16[256,768]{1,0:T(8,128)(2,1)S(1)} %get-tuple-element.94.refs_2_, bf16[256,768]{1,0:T(8,128)(2,1)S(1)} %collective-permute-done.10.refs_3_, ...), custom_call_target="tpu_custom_call" | custom-call | flops 11500000 | bytes 1 | tf_op jit(solution)/shard_map/D2_top/pallas_call | solution.py:47
  44.8 0.8 %collective-permute-start.14 = (bf16[512,256]{1,0:T(8,128)(2,1)S(1)}, bf16[512,256]{1,0:T(8,128)(2,1)S(1)}, u32[]{:S(2)}, u32[]{:S(2)}) collective-permute-start(bf16[512,256]{1,0:T(8,128)(2,1)S(1)} %get-tuple-element.103), channel_id=1, source_target_pairs={{0,8},{8,0},{16,24},{24,16},{1,9},{9,1},{17,25},{25,17},{2,10},{10... | collective-permute-start | bytes 786440 | tf_op jit(solution)/shard_map/ppermute | solution.py:23
  46.0 3.2 %collective-permute-done.11.refs_2_ = bf16[512,256]{1,0:T(8,128)(2,1)S(1)} collective-permute-done((bf16[512,256]{1,0:T(8,128)(2,1)S(1)}, bf16[512,256]{1,0:T(8,128)(2,1)S(1)}, u32[]{:S(2)}, u32[]{:S(2)}) %collective-permute-start.11) | collective-permute-done | bytes 262176 | tf_op jit(solution)/shard_map/ppermute | solution.py:23
  49.2 2.5 %collective-permute-start.15 = (bf16[256,256]{1,0:T(8,128)(2,1)S(1)}, bf16[256,256]{1,0:T(8,128)(2,1)S(1)}, u32[]{:S(2)}, u32[]{:S(2)}) collective-permute-start(bf16[256,256]{1,0:T(8,128)(2,1)S(1)} %get-tuple-element.105), channel_id=1, source_target_pairs={{0,16},{8,24},{16,0},{24,8},{1,17},{9,25},{17,1},{25,9},{2,18},{10... | collective-permute-start | bytes 393224 | tf_op jit(solution)/shard_map/ppermute | solution.py:23
  53.3 2.5 %collective-permute-start.16 = (bf16[512,128]{1,0:T(8,128)(2,1)S(1)}, bf16[512,128]{1,0:T(8,128)(2,1)S(1)}, u32[]{:S(2)}, u32[]{:S(2)}) collective-permute-start(bf16[512,128]{1,0:T(8,128)(2,1)S(1)} %get-tuple-element.108), channel_id=1, source_target_pairs={{0,8},{8,0},{16,24},{24,16},{1,9},{9,1},{17,25},{25,17},{2,10},{10... | collective-permute-start | bytes 393224 | tf_op jit(solution)/shard_map/ppermute | solution.py:23
  56.8 0.8 %collective-permute-done.14.refs_2_ = bf16[512,256]{1,0:T(8,128)(2,1)S(1)} collective-permute-done((bf16[512,256]{1,0:T(8,128)(2,1)S(1)}, bf16[512,256]{1,0:T(8,128)(2,1)S(1)}, u32[]{:S(2)}, u32[]{:S(2)}) %collective-permute-start.14) | collective-permute-done | bytes 262176 | tf_op jit(solution)/shard_map/ppermute | solution.py:23
  57.6 2.5 %collective-permute-start.18 = (bf16[256,256]{1,0:T(8,128)(2,1)S(1)}, bf16[256,256]{1,0:T(8,128)(2,1)S(1)}, u32[]{:S(2)}, u32[]{:S(2)}) collective-permute-start(bf16[256,256]{1,0:T(8,128)(2,1)S(1)} %get-tuple-element.112), channel_id=1, source_target_pairs={{0,16},{8,24},{16,0},{24,8},{1,17},{9,25},{17,1},{25,9},{2,18},{10... | collective-permute-start | bytes 393224 | tf_op jit(solution)/shard_map/ppermute | solution.py:23
  61.2 3.1 %collective-permute-start.19 = (bf16[256,128]{1,0:T(8,128)(2,1)S(1)}, bf16[256,128]{1,0:T(8,128)(2,1)S(1)}, u32[]{:S(2)}, u32[]{:S(2)}) collective-permute-start(bf16[256,128]{1,0:T(8,128)(2,1)S(1)} %get-tuple-element.115), channel_id=1, source_target_pairs={{0,16},{8,24},{16,0},{24,8},{1,17},{9,25},{17,1},{25,9},{2,18},{10... | collective-permute-start | bytes 196616 | tf_op jit(solution)/shard_map/ppermute | solution.py:23
  64.3 2.0 %collective-permute-done.17.refs_2_ = bf16[512,128]{1,0:T(8,128)(2,1)S(1)} collective-permute-done((bf16[512,128]{1,0:T(8,128)(2,1)S(1)}, bf16[512,128]{1,0:T(8,128)(2,1)S(1)}, u32[]{:S(2)}, u32[]{:S(2)}) %collective-permute-start.17) | collective-permute-done | bytes 131104 | tf_op jit(solution)/shard_map/ppermute | solution.py:23
  67.4 3.3 %collective-permute-done.19.refs_2_ = bf16[256,128]{1,0:T(8,128)(2,1)S(1)} collective-permute-done((bf16[256,128]{1,0:T(8,128)(2,1)S(1)}, bf16[256,128]{1,0:T(8,128)(2,1)S(1)}, u32[]{:S(2)}, u32[]{:S(2)}) %collective-permute-start.19) | collective-permute-done | bytes 65568 | tf_op jit(solution)/shard_map/ppermute | solution.py:23
  71.5 0.9 %collective-permute-done.20.refs_2_ = bf16[256,128]{1,0:T(8,128)(2,1)S(1)} collective-permute-done((bf16[256,128]{1,0:T(8,128)(2,1)S(1)}, bf16[256,128]{1,0:T(8,128)(2,1)S(1)}, u32[]{:S(2)}, u32[]{:S(2)}) %collective-permute-start.20) | collective-permute-done | bytes 65568 | tf_op jit(solution)/shard_map/ppermute | solution.py:23
  72.3 1.2 %Z22_finish.1 = (f32[256,1024]{1,0:T(8,128)}, f32[8,128]{1,0:T(8,128)}) custom-call(f32[8,128]{1,0:T(8,128)S(1)} %get-tuple-element.117.refs_0_, f32[256,128]{1,0:T(8,128)S(1)} %get-tuple-element.111.refs_0_.refs_1_, bf16[256,128]{1,0:T(8,128)(2,1)S(1)} %collective-permute-done.20.refs_2_, ...), custom_call_target="tpu_custom_call", output_to_operand_aliasing={{0}: (3, {})} | custom-call | flops 575000000 | bytes 1 | tf_op jit(solution)/shard_map/Z22_finish/pallas_call | solution.py:47
  (51 shorter events, 11.8 us)
Async XLA Ops:
  4.8 3.1 %collective-permute-start = (bf16[256,768]{1,0:T(8,128)(2,1)S(1)}, bf16[256,768]{1,0:T(8,128)(2,1)S(1)}, u32[]{:S(2)}, u32[]{:S(2)}) collective-permute-start(bf16[256,768]{1,0:T(8,128)(2,1)S(1)} %get-tuple-element.70), channel_id=1, source_target_pairs={{0,1},{1,0},{2,3},{3,2},{4,5},{5,4},{6,7},{7,6},{8,9},{9,8},{10,11... | collective-permute-start | bytes 1179656 | tf_op jit(solution)/shard_map/ppermute | solution.py:23
  5.3 2.5 %copy-start = (s32[3]{0:T(128)S(1)}, s32[3]{0:T(128)}, u32[]{:S(2)}) copy-start(s32[3]{0:T(128)} %param.12) | copy-start | bytes 40
  7.7 11.3 %collective-permute-start.2 = (bf16[256,768]{1,0:T(8,128)(2,1)S(1)}, bf16[256,768]{1,0:T(8,128)(2,1)S(1)}, u32[]{:S(2)}, u32[]{:S(2)}) collective-permute-start(bf16[256,768]{1,0:T(8,128)(2,1)S(1)} %get-tuple-element.79), channel_id=1, source_target_pairs={{0,1},{1,0},{2,3},{3,2},{4,5},{5,4},{6,7},{7,6},{8,9},{9,8},{10,11... | collective-permute-start | bytes 1179656 | tf_op jit(solution)/shard_map/ppermute | solution.py:23
  8.7 8.1 %collective-permute-start.1 = (bf16[128,768]{1,0:T(8,128)(2,1)S(1)}, bf16[128,768]{1,0:T(8,128)(2,1)S(1)}, u32[]{:S(2)}, u32[]{:S(2)}) collective-permute-start(bf16[128,768]{1,0:T(8,128)(2,1)S(1)} %get-tuple-element.76.refs_2_), channel_id=1, source_target_pairs={{0,2},{1,3},{2,0},{3,1},{4,6},{5,7},{6,4},{7,5},{8,10},{9,11},{10,... | collective-permute-start | bytes 589832 | tf_op jit(solution)/shard_map/ppermute | solution.py:23
  15.9 7.6 %collective-permute-start.3 = (bf16[128,768]{1,0:T(8,128)(2,1)S(1)}, bf16[128,768]{1,0:T(8,128)(2,1)S(1)}, u32[]{:S(2)}, u32[]{:S(2)}) collective-permute-start(bf16[128,768]{1,0:T(8,128)(2,1)S(1)} %get-tuple-element.82.refs_2_), channel_id=1, source_target_pairs={{0,2},{1,3},{2,0},{3,1},{4,6},{5,7},{6,4},{7,5},{8,10},{9,11},{10,... | collective-permute-start | bytes 589832 | tf_op jit(solution)/shard_map/ppermute | solution.py:23
  17.2 7.7 %collective-permute-start.4 = (bf16[128,768]{1,0:T(8,128)(2,1)S(1)}, bf16[128,768]{1,0:T(8,128)(2,1)S(1)}, u32[]{:S(2)}, u32[]{:S(2)}) collective-permute-start(bf16[128,768]{1,0:T(8,128)(2,1)S(1)} %get-tuple-element.84.refs_2_), channel_id=1, source_target_pairs={{0,4},{1,5},{2,6},{3,7},{4,0},{5,1},{6,2},{7,3},{8,12},{9,13},{10,... | collective-permute-start | bytes 589832 | tf_op jit(solution)/shard_map/ppermute | solution.py:23
  20.0 10.9 %collective-permute-start.6 = (bf16[256,768]{1,0:T(8,128)(2,1)S(1)}, bf16[256,768]{1,0:T(8,128)(2,1)S(1)}, u32[]{:S(2)}, u32[]{:S(2)}) collective-permute-start(bf16[256,768]{1,0:T(8,128)(2,1)S(1)} %get-tuple-element.88.refs_2_), channel_id=1, source_target_pairs={{0,2},{1,3},{2,0},{3,1},{4,6},{5,7},{6,4},{7,5},{8,10},{9,11},{10,... | collective-permute-start | bytes 1179656 | tf_op jit(solution)/shard_map/ppermute | solution.py:23
  26.2 1.9 %collective-permute-start.5 = (bf16[128,768]{1,0:T(8,128)(2,1)S(1)}, bf16[128,768]{1,0:T(8,128)(2,1)S(1)}, u32[]{:S(2)}, u32[]{:S(2)}) collective-permute-start(bf16[128,768]{1,0:T(8,128)(2,1)S(1)} %D0_top.1.refs_0_.refs_5_), channel_id=1, source_target_pairs={{0,1},{1,0},{2,3},{3,2},{4,5},{5,4},{6,7},{7,6},{8,9},{9,8},{10,11... | collective-permute-start | bytes 589832 | tf_op jit(solution)/shard_map/ppermute | solution.py:23
  26.3 7.3 %collective-permute-start.7 = (bf16[128,768]{1,0:T(8,128)(2,1)S(1)}, bf16[128,768]{1,0:T(8,128)(2,1)S(1)}, u32[]{:S(2)}, u32[]{:S(2)}) collective-permute-start(bf16[128,768]{1,0:T(8,128)(2,1)S(1)} %get-tuple-element.90.refs_2_), channel_id=1, source_target_pairs={{0,4},{1,5},{2,6},{3,7},{4,0},{5,1},{6,2},{7,3},{8,12},{9,13},{10,... | collective-permute-start | bytes 589832 | tf_op jit(solution)/shard_map/ppermute | solution.py:23
  29.0 8.4 %collective-permute-start.8 = (bf16[512,256]{1,0:T(8,128)(2,1)S(1)}, bf16[512,256]{1,0:T(8,128)(2,1)S(1)}, u32[]{:S(2)}, u32[]{:S(2)}) collective-permute-start(bf16[512,256]{1,0:T(8,128)(2,1)S(1)} %get-tuple-element.91), channel_id=1, source_target_pairs={{0,8},{8,0},{16,24},{24,16},{1,9},{9,1},{17,25},{25,17},{2,10},{10... | collective-permute-start | bytes 786440 | tf_op jit(solution)/shard_map/ppermute | solution.py:23
  31.4 11.5 %collective-permute-start.10 = (bf16[256,768]{1,0:T(8,128)(2,1)S(1)}, bf16[256,768]{1,0:T(8,128)(2,1)S(1)}, u32[]{:S(2)}, u32[]{:S(2)}) collective-permute-start(bf16[256,768]{1,0:T(8,128)(2,1)S(1)} %get-tuple-element.94.refs_2_), channel_id=1, source_target_pairs={{0,4},{1,5},{2,6},{3,7},{4,0},{5,1},{6,2},{7,3},{8,12},{9,13},{10,... | collective-permute-start | bytes 1179656 | tf_op jit(solution)/shard_map/ppermute | solution.py:23
  35.0 2.5 %collective-permute-start.9 = (bf16[128,768]{1,0:T(8,128)(2,1)S(1)}, bf16[128,768]{1,0:T(8,128)(2,1)S(1)}, u32[]{:S(2)}, u32[]{:S(2)}) collective-permute-start(bf16[128,768]{1,0:T(8,128)(2,1)S(1)} %D1_top.1.refs_0_.refs_5_), channel_id=1, source_target_pairs={{0,1},{1,0},{2,3},{3,2},{4,5},{5,4},{6,7},{7,6},{8,9},{9,8},{10,11... | collective-permute-start | bytes 589832 | tf_op jit(solution)/shard_map/ppermute | solution.py:23
  38.1 11.0 %collective-permute-start.11 = (bf16[512,256]{1,0:T(8,128)(2,1)S(1)}, bf16[512,256]{1,0:T(8,128)(2,1)S(1)}, u32[]{:S(2)}, u32[]{:S(2)}) collective-permute-start(bf16[512,256]{1,0:T(8,128)(2,1)S(1)} %get-tuple-element.97), channel_id=1, source_target_pairs={{0,8},{8,0},{16,24},{24,16},{1,9},{9,1},{17,25},{25,17},{2,10},{10... | collective-permute-start | bytes 786440 | tf_op jit(solution)/shard_map/ppermute | solution.py:23
  39.8 11.9 %collective-permute-start.12 = (bf16[256,256]{1,0:T(8,128)(2,1)S(1)}, bf16[256,256]{1,0:T(8,128)(2,1)S(1)}, u32[]{:S(2)}, u32[]{:S(2)}) collective-permute-start(bf16[256,256]{1,0:T(8,128)(2,1)S(1)} %get-tuple-element.99), channel_id=1, source_target_pairs={{0,16},{8,24},{16,0},{24,8},{1,17},{9,25},{17,1},{25,9},{2,18},{10... | collective-permute-start | bytes 393224 | tf_op jit(solution)/shard_map/ppermute | solution.py:23
  44.1 8.3 %collective-permute-start.13 = (bf16[256,768]{1,0:T(8,128)(2,1)S(1)}, bf16[256,768]{1,0:T(8,128)(2,1)S(1)}, u32[]{:S(2)}, u32[]{:S(2)}) collective-permute-start(bf16[256,768]{1,0:T(8,128)(2,1)S(1)} %D2_top.1.refs_0_.refs_5_), channel_id=1, source_target_pairs={{0,1},{1,0},{2,3},{3,2},{4,5},{5,4},{6,7},{7,6},{8,9},{9,8},{10,11... | collective-permute-start | bytes 1179656 | tf_op jit(solution)/shard_map/ppermute | solution.py:23
  44.8 12.7 %collective-permute-start.14 = (bf16[512,256]{1,0:T(8,128)(2,1)S(1)}, bf16[512,256]{1,0:T(8,128)(2,1)S(1)}, u32[]{:S(2)}, u32[]{:S(2)}) collective-permute-start(bf16[512,256]{1,0:T(8,128)(2,1)S(1)} %get-tuple-element.103), channel_id=1, source_target_pairs={{0,8},{8,0},{16,24},{24,16},{1,9},{9,1},{17,25},{25,17},{2,10},{10... | collective-permute-start | bytes 786440 | tf_op jit(solution)/shard_map/ppermute | solution.py:23
  49.2 11.2 %collective-permute-start.15 = (bf16[256,256]{1,0:T(8,128)(2,1)S(1)}, bf16[256,256]{1,0:T(8,128)(2,1)S(1)}, u32[]{:S(2)}, u32[]{:S(2)}) collective-permute-start(bf16[256,256]{1,0:T(8,128)(2,1)S(1)} %get-tuple-element.105), channel_id=1, source_target_pairs={{0,16},{8,24},{16,0},{24,8},{1,17},{9,25},{17,1},{25,9},{2,18},{10... | collective-permute-start | bytes 393224 | tf_op jit(solution)/shard_map/ppermute | solution.py:23
  53.3 7.8 %collective-permute-start.16 = (bf16[512,128]{1,0:T(8,128)(2,1)S(1)}, bf16[512,128]{1,0:T(8,128)(2,1)S(1)}, u32[]{:S(2)}, u32[]{:S(2)}) collective-permute-start(bf16[512,128]{1,0:T(8,128)(2,1)S(1)} %get-tuple-element.108), channel_id=1, source_target_pairs={{0,8},{8,0},{16,24},{24,16},{1,9},{9,1},{17,25},{25,17},{2,10},{10... | collective-permute-start | bytes 393224 | tf_op jit(solution)/shard_map/ppermute | solution.py:23
  56.7 9.6 %collective-permute-start.17 = (bf16[512,128]{1,0:T(8,128)(2,1)S(1)}, bf16[512,128]{1,0:T(8,128)(2,1)S(1)}, u32[]{:S(2)}, u32[]{:S(2)}) collective-permute-start(bf16[512,128]{1,0:T(8,128)(2,1)S(1)} %get-tuple-element.110), channel_id=1, source_target_pairs={{0,8},{8,0},{16,24},{24,16},{1,9},{9,1},{17,25},{25,17},{2,10},{10... | collective-permute-start | bytes 393224 | tf_op jit(solution)/shard_map/ppermute | solution.py:23
  57.6 9.1 %collective-permute-start.18 = (bf16[256,256]{1,0:T(8,128)(2,1)S(1)}, bf16[256,256]{1,0:T(8,128)(2,1)S(1)}, u32[]{:S(2)}, u32[]{:S(2)}) collective-permute-start(bf16[256,256]{1,0:T(8,128)(2,1)S(1)} %get-tuple-element.112), channel_id=1, source_target_pairs={{0,16},{8,24},{16,0},{24,8},{1,17},{9,25},{17,1},{25,9},{2,18},{10... | collective-permute-start | bytes 393224 | tf_op jit(solution)/shard_map/ppermute | solution.py:23
  61.2 9.6 %collective-permute-start.19 = (bf16[256,128]{1,0:T(8,128)(2,1)S(1)}, bf16[256,128]{1,0:T(8,128)(2,1)S(1)}, u32[]{:S(2)}, u32[]{:S(2)}) collective-permute-start(bf16[256,128]{1,0:T(8,128)(2,1)S(1)} %get-tuple-element.115), channel_id=1, source_target_pairs={{0,16},{8,24},{16,0},{24,8},{1,17},{9,25},{17,1},{25,9},{2,18},{10... | collective-permute-start | bytes 196616 | tf_op jit(solution)/shard_map/ppermute | solution.py:23
  66.3 6.0 %collective-permute-start.20 = (bf16[256,128]{1,0:T(8,128)(2,1)S(1)}, bf16[256,128]{1,0:T(8,128)(2,1)S(1)}, u32[]{:S(2)}, u32[]{:S(2)}) collective-permute-start(bf16[256,128]{1,0:T(8,128)(2,1)S(1)} %get-tuple-element.118), channel_id=1, source_target_pairs={{0,16},{8,24},{16,0},{24,8},{1,17},{9,25},{17,1},{25,9},{2,18},{10... | collective-permute-start | bytes 196616 | tf_op jit(solution)/shard_map/ppermute | solution.py:23

commit v4 on v3

--- a/solution.py
+++ b/solution.py
@@ -14,7 +14,7 @@
 GROUPS = ((0, 1), (2,))
 PARTS = ((((0, 0, 1), (1, 0, 1)),), (((0, 0, 1), (1, 0, 1)),), (((0, 0, 2),), ((1, 0, 1),), ((1, 1, 1),)))
 COST = 0.01
-TILES = 2
+TILES = 4
 
 
 def exchange(value, axis, bit):
@@ -113,7 +113,7 @@
     for part in range(parts):
         for copy in blocks[part * len(blocks) // parts : (part + 1) * len(blocks) // parts]:
             copy.wait()
-        if part == parts - 1:
+        if part == 0:
             later = [load(fronts_in.at[0], front), load(links_in.at[0], link), load(coupling_in, coupling)]
             if width < count:
                 later += load_columns(width, count - width)

time: 73.9 us -> 73.6 us (level)
  no operation moved by 1% of the time
where the time goes in v4:
time: 73.6 us; the launch traced here: 73.5 us
  Pallas kernels  29.7 us (40%)
  starting transfers between devices  28.5 us (39%)
  waiting for transfers between devices  14 us (19%)
  between operations  1.13 us (2%)
    pallas_call x36, Pallas kernels, __call__(): pl.pallas_call(run, out_shape=[jax.ShapeDtypeStruct(shape, kind) for shap...  29.7 us
    ppermute x21, starting transfers between devices, exchange(): return lax.ppermute(value, axis, pairs)  28.5 us
    ppermute x21, waiting for transfers between devices, exchange(): return lax.ppermute(value, axis, pairs)  14 us
  transfers between devices with their start and end apart: 21, of which 9 were waited for; matrix products, arithmetic and copies ran while one was open for 0% of the time, Pallas kernels for 32%

profile of v4, /device:TPU:0, one launch (start us, length us, event | category | flops | bytes accessed | tf_op | source)
XLA Modules:
  0.0 73.5 jit_solution(9270760473839358584)
XLA Ops:
  0.0 4.5 %A0_leaf_up.1 = (bf16[256,768]{1,0:T(8,128)(2,1)S(1)}, bf16[256,768]{1,0:T(8,128)(2,1)S(1)}, bf16[1024,512]{1,0:T(8,128)(2,1)S(1)}, bf16[768,384]{1,0:T(8,128)(2...) custom-call(bf16[1024,1024]{1,0:T(8,128)(2,1)} %bitcast.12, ...), custom_call_target="tpu_custom_call" | custom-call | flops 11500000 | bytes 1 | tf_op jit(solution)/shard_map/A0_leaf_up/pallas_call | solution.py:47
  5.1 2.4 %A1_leaf_up.1 = (bf16[256,768]{1,0:T(8,128)(2,1)S(1)}, bf16[256,768]{1,0:T(8,128)(2,1)S(1)}, bf16[1024,512]{1,0:T(8,128)(2,1)S(1)}, bf16[2,768,768]{2,1,0:T(8,128)(2,1)S(1)}, bf16[1,768,768]{2,1,0:T(8,128)(2,1)S(1)}) custom-call(bf16[768,768]{1,0:T(8,128)(2,1)S(1)} %get-tuple-element.63.refs_0_.refs_5_.refs_3_, ...), custom_call_target="tpu_custom_call" | custom-call | flops 11500000 | bytes 1 | tf_op jit(solution)/shard_map/A1_leaf_up/pallas_call | solution.py:47
  7.7 0.8 %B0_front_up.1 = (bf16[128,768]{1,0:T(8,128)(2,1)S(1)}, bf16[128,768]{1,0:T(8,128)(2,1)S(1)}) custom-call(bf16[1,768,768]{2,1,0:T(8,128)(2,1)S(1)} %get-tuple-element.68.refs_0_.refs_5_, f32[8,768]{1,0:T(8,128)S(1)} %fusion.refs_1_, bf16[256,768]{1,0:T(8,128)(2,1)S(1)} %get-tuple-element.69.refs_2_, bf16[256,768]{1,0:T(8,128)(2,1)S(1)} %collective-permute-done.refs_3_, ...), custom_call_target="tpu_custom_call" | custom-call | flops 575000000 | bytes 1 | tf_op jit(solution)/shard_map/B0_front_up/pallas_call | solution.py:47
  8.5 3.0 %collective-permute-start.1 = (bf16[128,768]{1,0:T(8,128)(2,1)S(1)}, bf16[128,768]{1,0:T(8,128)(2,1)S(1)}, u32[]{:S(2)}, u32[]{:S(2)}) collective-permute-start(bf16[128,768]{1,0:T(8,128)(2,1)S(1)} %get-tuple-element.76.refs_2_), channel_id=1, source_target_pairs={{0,2},{1,3},{2,0},{3,1},{4,6},{5,7},{6,4},{7,5},{8,10},{9,11},{10,... | collective-permute-start | bytes 589832 | tf_op jit(solution)/shard_map/ppermute | solution.py:23
  11.5 3.3 %Q_products.1 = (bf16[2,768,768]{2,1,0:T(8,128)(2,1)S(1)}, bf16[1,768,768]{2,1,0:T(8,128)(2,1)S(1)}) custom-call(bf16[128,768]{1,0:T(8,128)(2,1)S(1)} %get-tuple-element.72.refs_0_.refs_6_, f32[8,768]{1,0:T(8,128)S(1)} %fusion.refs_1_, bf16[768,768]{1,0:T(8,128)(2,1)S(1)} %get-tuple-element.71.refs_4_.refs_2_, ...), custom_call_target="tpu_custom_call" | custom-call | flops 11500000 | bytes 1 | tf_op jit(solution)/shard_map/Q_products/pallas_call | solution.py:47
  14.8 0.8 %B1_front_up.1 = (bf16[128,768]{1,0:T(8,128)(2,1)S(1)}, bf16[128,768]{1,0:T(8,128)(2,1)S(1)}) custom-call(bf16[1,768,768]{2,1,0:T(8,128)(2,1)S(1)} %get-tuple-element.74.refs_0_.refs_4_, f32[8,768]{1,0:T(8,128)S(1)} %fusion.refs_1_, bf16[256,768]{1,0:T(8,128)(2,1)S(1)} %get-tuple-element.69.refs_2_, bf16[256,768]{1,0:T(8,128)(2,1)S(1)} %collective-permute-done.refs_3_, ...), custom_call_target="tpu_custom_call" | custom-call | flops 11500000 | bytes 1 | tf_op jit(solution)/shard_map/B1_front_up/pallas_call | solution.py:47
  15.7 0.9 %collective-permute-done.1.refs_3_ = bf16[128,768]{1,0:T(8,128)(2,1)S(1)} collective-permute-done((bf16[128,768]{1,0:T(8,128)(2,1)S(1)}, bf16[128,768]{1,0:T(8,128)(2,1)S(1)}, u32[]{:S(2)}, u32[]{:S(2)}) %collective-permute-start.1) | collective-permute-done | bytes 196640 | tf_op jit(solution)/shard_map/ppermute | solution.py:23
  16.9 1.8 %collective-permute-start.4 = (bf16[128,768]{1,0:T(8,128)(2,1)S(1)}, bf16[128,768]{1,0:T(8,128)(2,1)S(1)}, u32[]{:S(2)}, u32[]{:S(2)}) collective-permute-start(bf16[128,768]{1,0:T(8,128)(2,1)S(1)} %get-tuple-element.84.refs_2_), channel_id=1, source_target_pairs={{0,4},{1,5},{2,6},{3,7},{4,0},{5,1},{6,2},{7,3},{8,12},{9,13},{10,... | collective-permute-start | bytes 589832 | tf_op jit(solution)/shard_map/ppermute | solution.py:23
  18.7 1.0 %B2_front_up.1 = (bf16[256,768]{1,0:T(8,128)(2,1)S(1)}, bf16[256,768]{1,0:T(8,128)(2,1)S(1)}) custom-call(bf16[128,768]{1,0:T(8,128)(2,1)S(1)} %get-tuple-element.77.refs_0_.refs_2_, f32[8,768]{1,0:T(8,128)S(1)} %fusion.refs_1_, bf16[256,768]{1,0:T(8,128)(2,1)S(1)} %get-tuple-element.78.refs_2_, bf16[256,768]{1,0:T(8,128)(2,1)S(1)} %collective-permute-done.2.refs_3_, ...), custom_call_target="tpu_custom_call" | custom-call | flops 11500000 | bytes 1 | tf_op jit(solution)/shard_map/B2_front_up/pallas_call | solution.py:47
  19.7 1.6 %collective-permute-start.6 = (bf16[256,768]{1,0:T(8,128)(2,1)S(1)}, bf16[256,768]{1,0:T(8,128)(2,1)S(1)}, u32[]{:S(2)}, u32[]{:S(2)}) collective-permute-start(bf16[256,768]{1,0:T(8,128)(2,1)S(1)} %get-tuple-element.88.refs_2_), channel_id=1, source_target_pairs={{0,2},{1,3},{2,0},{3,1},{4,6},{5,7},{6,4},{7,5},{8,10},{9,11},{10,... | collective-permute-start | bytes 1179656 | tf_op jit(solution)/shard_map/ppermute | solution.py:23
  21.9 1.3 %G_lift.1.refs_0_.refs_2_ = bf16[1024,384]{1,0:T(8,128)(2,1)S(1)} custom-call(bf16[256,768]{1,0:T(8,128)(2,1)S(1)} %get-tuple-element.80.refs_0_.refs_6_, bf16[1024,1024]{1,0:T(8,128)(2,1)S(1)} %get-tuple-element.64.refs_1_, bf16[1024,384]{1,0:T(8,128)(2,1)S(1)} %get-tuple-element.81.refs_2_, f32[8,128]{1,0:T(8,128)S(1)} %broadcast_in_dim.4.refs_3_.refs_1_), custom_call_target="tpu_custom_call" | custom-call | flops 11500000 | bytes 1 | tf_op jit(solution)/shard_map/G_lift/pallas_call | solution.py:47
  24.6 1.3 %D0_top.1.refs_0_.refs_5_ = bf16[128,768]{1,0:T(8,128)(2,1)S(1)} custom-call(bf16[128,768]{1,0:T(8,128)(2,1)S(1)} %T0_front_solve.1.refs_0_.refs_7_, f32[8,768]{1,0:T(8,128)S(1)} %fusion.refs_1_, bf16[128,768]{1,0:T(8,128)(2,1)S(1)} %get-tuple-element.84.refs_2_, bf16[128,768]{1,0:T(8,128)(2,1)S(1)} %collective-permute-done.4.refs_3_, ...), custom_call_target="tpu_custom_call" | custom-call | flops 11500000 | bytes 1 | tf_op jit(solution)/shard_map/D0_top/pallas_call | solution.py:47
  26.0 1.9 %collective-permute-start.7 = (bf16[128,768]{1,0:T(8,128)(2,1)S(1)}, bf16[128,768]{1,0:T(8,128)(2,1)S(1)}, u32[]{:S(2)}, u32[]{:S(2)}) collective-permute-start(bf16[128,768]{1,0:T(8,128)(2,1)S(1)} %get-tuple-element.90.refs_2_), channel_id=1, source_target_pairs={{0,4},{1,5},{2,6},{3,7},{4,0},{5,1},{6,2},{7,3},{8,12},{9,13},{10,... | collective-permute-start | bytes 589832 | tf_op jit(solution)/shard_map/ppermute | solution.py:23
  27.9 0.8 %E0_down_first.1 = (bf16[512,256]{1,0:T(8,128)(2,1)S(1)}, bf16[256,384]{1,0:T(8,128)(2,1)S(1)}) custom-call(bf16[128,768]{1,0:T(8,128)(2,1)S(1)} %D0_top.1.refs_0_.refs_5_, f32[8,128]{1,0:T(8,128)S(1)} %broadcast_in_dim.4.refs_3_.refs_1_, bf16[1024,384]{1,0:T(8,128)(2,1)S(1)} %G_lift.1.refs_0_.refs_2_, ...), custom_call_target="tpu_custom_call" | custom-call | flops 11500000 | bytes 1 | tf_op jit(solution)/shard_map/E0_down_first/pallas_call | solution.py:47
  28.7 1.6 %collective-permute-start.8 = (bf16[512,256]{1,0:T(8,128)(2,1)S(1)}, bf16[512,256]{1,0:T(8,128)(2,1)S(1)}, u32[]{:S(2)}, u32[]{:S(2)}) collective-permute-start(bf16[512,256]{1,0:T(8,128)(2,1)S(1)} %get-tuple-element.91), channel_id=1, source_target_pairs={{0,8},{8,0},{16,24},{24,16},{1,9},{9,1},{17,25},{25,17},{2,10},{10... | collective-permute-start | bytes 786440 | tf_op jit(solution)/shard_map/ppermute | solution.py:23
  31.2 1.6 %collective-permute-start.10 = (bf16[256,768]{1,0:T(8,128)(2,1)S(1)}, bf16[256,768]{1,0:T(8,128)(2,1)S(1)}, u32[]{:S(2)}, u32[]{:S(2)}) collective-permute-start(bf16[256,768]{1,0:T(8,128)(2,1)S(1)} %get-tuple-element.94.refs_2_), channel_id=1, source_target_pairs={{0,4},{1,5},{2,6},{3,7},{4,0},{5,1},{6,2},{7,3},{8,12},{9,13},{10,... | collective-permute-start | bytes 1179656 | tf_op jit(solution)/shard_map/ppermute | solution.py:23
  33.4 1.3 %D1_top.1.refs_0_.refs_5_ = bf16[128,768]{1,0:T(8,128)(2,1)S(1)} custom-call(f32[512,256]{1,0:T(8,128)S(1)} %S0_down_second.1.refs_0_.refs_1_, f32[8,768]{1,0:T(8,128)S(1)} %fusion.refs_1_, bf16[128,768]{1,0:T(8,128)(2,1)S(1)} %get-tuple-element.90.refs_2_, bf16[128,768]{1,0:T(8,128)(2,1)S(1)} %collective-permute-done.7.refs_3_, ...), custom_call_target="tpu_custom_call" | custom-call | flops 11500000 | bytes 1 | tf_op jit(solution)/shard_map/D1_top/pallas_call | solution.py:47
  34.8 2.4 %collective-permute-done.8.refs_2_ = bf16[512,256]{1,0:T(8,128)(2,1)S(1)} collective-permute-done((bf16[512,256]{1,0:T(8,128)(2,1)S(1)}, bf16[512,256]{1,0:T(8,128)(2,1)S(1)}, u32[]{:S(2)}, u32[]{:S(2)}) %collective-permute-start.8) | collective-permute-done | bytes 262176 | tf_op jit(solution)/shard_map/ppermute | solution.py:23
  37.9 1.6 %collective-permute-start.11 = (bf16[512,256]{1,0:T(8,128)(2,1)S(1)}, bf16[512,256]{1,0:T(8,128)(2,1)S(1)}, u32[]{:S(2)}, u32[]{:S(2)}) collective-permute-start(bf16[512,256]{1,0:T(8,128)(2,1)S(1)} %get-tuple-element.97), channel_id=1, source_target_pairs={{0,8},{8,0},{16,24},{24,16},{1,9},{9,1},{17,25},{25,17},{2,10},{10... | collective-permute-start | bytes 786440 | tf_op jit(solution)/shard_map/ppermute | solution.py:23
  39.5 2.6 %collective-permute-start.12 = (bf16[256,256]{1,0:T(8,128)(2,1)S(1)}, bf16[256,256]{1,0:T(8,128)(2,1)S(1)}, u32[]{:S(2)}, u32[]{:S(2)}) collective-permute-start(bf16[256,256]{1,0:T(8,128)(2,1)S(1)} %get-tuple-element.99), channel_id=1, source_target_pairs={{0,16},{8,24},{16,0},{24,8},{1,17},{9,25},{17,1},{25,9},{2,18},{10... | collective-permute-start | bytes 393224 | tf_op jit(solution)/shard_map/ppermute | solution.py:23
  42.6 1.2 %D2_top.1.refs_0_.refs_5_ = bf16[256,768]{1,0:T(8,128)(2,1)S(1)} custom-call(bf16[256,768]{1,0:T(8,128)(2,1)S(1)} %T2_front_solve.1.refs_0_.refs_7_, f32[8,768]{1,0:T(8,128)S(1)} %fusion.refs_1_, bf16[256,768]{1,0:T(8,128)(2,1)S(1)} %get-tuple-element.94.refs_2_, bf16[256,768]{1,0:T(8,128)(2,1)S(1)} %collective-permute-done.10.refs_3_, ...), custom_call_target="tpu_custom_call" | custom-call | flops 11500000 | bytes 1 | tf_op jit(solution)/shard_map/D2_top/pallas_call | solution.py:47
  44.5 0.8 %collective-permute-start.14 = (bf16[512,256]{1,0:T(8,128)(2,1)S(1)}, bf16[512,256]{1,0:T(8,128)(2,1)S(1)}, u32[]{:S(2)}, u32[]{:S(2)}) collective-permute-start(bf16[512,256]{1,0:T(8,128)(2,1)S(1)} %get-tuple-element.103), channel_id=1, source_target_pairs={{0,8},{8,0},{16,24},{24,16},{1,9},{9,1},{17,25},{25,17},{2,10},{10... | collective-permute-start | bytes 786440 | tf_op jit(solution)/shard_map/ppermute | solution.py:23
  45.7 3.2 %collective-permute-done.11.refs_2_ = bf16[512,256]{1,0:T(8,128)(2,1)S(1)} collective-permute-done((bf16[512,256]{1,0:T(8,128)(2,1)S(1)}, bf16[512,256]{1,0:T(8,128)(2,1)S(1)}, u32[]{:S(2)}, u32[]{:S(2)}) %collective-permute-start.11) | collective-permute-done | bytes 262176 | tf_op jit(solution)/shard_map/ppermute | solution.py:23
  48.9 2.5 %collective-permute-start.15 = (bf16[256,256]{1,0:T(8,128)(2,1)S(1)}, bf16[256,256]{1,0:T(8,128)(2,1)S(1)}, u32[]{:S(2)}, u32[]{:S(2)}) collective-permute-start(bf16[256,256]{1,0:T(8,128)(2,1)S(1)} %get-tuple-element.105), channel_id=1, source_target_pairs={{0,16},{8,24},{16,0},{24,8},{1,17},{9,25},{17,1},{25,9},{2,18},{10... | collective-permute-start | bytes 393224 | tf_op jit(solution)/shard_map/ppermute | solution.py:23
  53.1 2.5 %collective-permute-start.16 = (bf16[512,128]{1,0:T(8,128)(2,1)S(1)}, bf16[512,128]{1,0:T(8,128)(2,1)S(1)}, u32[]{:S(2)}, u32[]{:S(2)}) collective-permute-start(bf16[512,128]{1,0:T(8,128)(2,1)S(1)} %get-tuple-element.108), channel_id=1, source_target_pairs={{0,8},{8,0},{16,24},{24,16},{1,9},{9,1},{17,25},{25,17},{2,10},{10... | collective-permute-start | bytes 393224 | tf_op jit(solution)/shard_map/ppermute | solution.py:23
  56.5 0.8 %collective-permute-done.14.refs_2_ = bf16[512,256]{1,0:T(8,128)(2,1)S(1)} collective-permute-done((bf16[512,256]{1,0:T(8,128)(2,1)S(1)}, bf16[512,256]{1,0:T(8,128)(2,1)S(1)}, u32[]{:S(2)}, u32[]{:S(2)}) %collective-permute-start.14) | collective-permute-done | bytes 262176 | tf_op jit(solution)/shard_map/ppermute | solution.py:23
  57.4 2.5 %collective-permute-start.18 = (bf16[256,256]{1,0:T(8,128)(2,1)S(1)}, bf16[256,256]{1,0:T(8,128)(2,1)S(1)}, u32[]{:S(2)}, u32[]{:S(2)}) collective-permute-start(bf16[256,256]{1,0:T(8,128)(2,1)S(1)} %get-tuple-element.112), channel_id=1, source_target_pairs={{0,16},{8,24},{16,0},{24,8},{1,17},{9,25},{17,1},{25,9},{2,18},{10... | collective-permute-start | bytes 393224 | tf_op jit(solution)/shard_map/ppermute | solution.py:23
  60.9 3.1 %collective-permute-start.19 = (bf16[256,128]{1,0:T(8,128)(2,1)S(1)}, bf16[256,128]{1,0:T(8,128)(2,1)S(1)}, u32[]{:S(2)}, u32[]{:S(2)}) collective-permute-start(bf16[256,128]{1,0:T(8,128)(2,1)S(1)} %get-tuple-element.115), channel_id=1, source_target_pairs={{0,16},{8,24},{16,0},{24,8},{1,17},{9,25},{17,1},{25,9},{2,18},{10... | collective-permute-start | bytes 196616 | tf_op jit(solution)/shard_map/ppermute | solution.py:23
  64.0 2.0 %collective-permute-done.17.refs_2_ = bf16[512,128]{1,0:T(8,128)(2,1)S(1)} collective-permute-done((bf16[512,128]{1,0:T(8,128)(2,1)S(1)}, bf16[512,128]{1,0:T(8,128)(2,1)S(1)}, u32[]{:S(2)}, u32[]{:S(2)}) %collective-permute-start.17) | collective-permute-done | bytes 131104 | tf_op jit(solution)/shard_map/ppermute | solution.py:23
  67.2 3.3 %collective-permute-done.19.refs_2_ = bf16[256,128]{1,0:T(8,128)(2,1)S(1)} collective-permute-done((bf16[256,128]{1,0:T(8,128)(2,1)S(1)}, bf16[256,128]{1,0:T(8,128)(2,1)S(1)}, u32[]{:S(2)}, u32[]{:S(2)}) %collective-permute-start.19) | collective-permute-done | bytes 65568 | tf_op jit(solution)/shard_map/ppermute | solution.py:23
  71.2 0.9 %collective-permute-done.20.refs_2_ = bf16[256,128]{1,0:T(8,128)(2,1)S(1)} collective-permute-done((bf16[256,128]{1,0:T(8,128)(2,1)S(1)}, bf16[256,128]{1,0:T(8,128)(2,1)S(1)}, u32[]{:S(2)}, u32[]{:S(2)}) %collective-permute-start.20) | collective-permute-done | bytes 65568 | tf_op jit(solution)/shard_map/ppermute | solution.py:23
  72.0 1.2 %Z22_finish.1 = (f32[256,1024]{1,0:T(8,128)}, f32[8,128]{1,0:T(8,128)}) custom-call(f32[8,128]{1,0:T(8,128)S(1)} %get-tuple-element.117.refs_0_, f32[256,128]{1,0:T(8,128)S(1)} %get-tuple-element.111.refs_0_.refs_1_, bf16[256,128]{1,0:T(8,128)(2,1)S(1)} %collective-permute-done.20.refs_2_, ...), custom_call_target="tpu_custom_call", output_to_operand_aliasing={{0}: (3, {})} | custom-call | flops 575000000 | bytes 1 | tf_op jit(solution)/shard_map/Z22_finish/pallas_call | solution.py:47
  (51 shorter events, 11.8 us)
Async XLA Ops:
  4.6 3.1 %collective-permute-start = (bf16[256,768]{1,0:T(8,128)(2,1)S(1)}, bf16[256,768]{1,0:T(8,128)(2,1)S(1)}, u32[]{:S(2)}, u32[]{:S(2)}) collective-permute-start(bf16[256,768]{1,0:T(8,128)(2,1)S(1)} %get-tuple-element.70), channel_id=1, source_target_pairs={{0,1},{1,0},{2,3},{3,2},{4,5},{5,4},{6,7},{7,6},{8,9},{9,8},{10,11... | collective-permute-start | bytes 1179656 | tf_op jit(solution)/shard_map/ppermute | solution.py:23
  5.1 2.5 %copy-start = (s32[3]{0:T(128)S(1)}, s32[3]{0:T(128)}, u32[]{:S(2)}) copy-start(s32[3]{0:T(128)} %param.12) | copy-start | bytes 40
  7.5 11.3 %collective-permute-start.2 = (bf16[256,768]{1,0:T(8,128)(2,1)S(1)}, bf16[256,768]{1,0:T(8,128)(2,1)S(1)}, u32[]{:S(2)}, u32[]{:S(2)}) collective-permute-start(bf16[256,768]{1,0:T(8,128)(2,1)S(1)} %get-tuple-element.79), channel_id=1, source_target_pairs={{0,1},{1,0},{2,3},{3,2},{4,5},{5,4},{6,7},{7,6},{8,9},{9,8},{10,11... | collective-permute-start | bytes 1179656 | tf_op jit(solution)/shard_map/ppermute | solution.py:23
  8.5 8.1 %collective-permute-start.1 = (bf16[128,768]{1,0:T(8,128)(2,1)S(1)}, bf16[128,768]{1,0:T(8,128)(2,1)S(1)}, u32[]{:S(2)}, u32[]{:S(2)}) collective-permute-start(bf16[128,768]{1,0:T(8,128)(2,1)S(1)} %get-tuple-element.76.refs_2_), channel_id=1, source_target_pairs={{0,2},{1,3},{2,0},{3,1},{4,6},{5,7},{6,4},{7,5},{8,10},{9,11},{10,... | collective-permute-start | bytes 589832 | tf_op jit(solution)/shard_map/ppermute | solution.py:23
  15.6 7.6 %collective-permute-start.3 = (bf16[128,768]{1,0:T(8,128)(2,1)S(1)}, bf16[128,768]{1,0:T(8,128)(2,1)S(1)}, u32[]{:S(2)}, u32[]{:S(2)}) collective-permute-start(bf16[128,768]{1,0:T(8,128)(2,1)S(1)} %get-tuple-element.82.refs_2_), channel_id=1, source_target_pairs={{0,2},{1,3},{2,0},{3,1},{4,6},{5,7},{6,4},{7,5},{8,10},{9,11},{10,... | collective-permute-start | bytes 589832 | tf_op jit(solution)/shard_map/ppermute | solution.py:23
  16.9 7.7 %collective-permute-start.4 = (bf16[128,768]{1,0:T(8,128)(2,1)S(1)}, bf16[128,768]{1,0:T(8,128)(2,1)S(1)}, u32[]{:S(2)}, u32[]{:S(2)}) collective-permute-start(bf16[128,768]{1,0:T(8,128)(2,1)S(1)} %get-tuple-element.84.refs_2_), channel_id=1, source_target_pairs={{0,4},{1,5},{2,6},{3,7},{4,0},{5,1},{6,2},{7,3},{8,12},{9,13},{10,... | collective-permute-start | bytes 589832 | tf_op jit(solution)/shard_map/ppermute | solution.py:23
  19.7 10.9 %collective-permute-start.6 = (bf16[256,768]{1,0:T(8,128)(2,1)S(1)}, bf16[256,768]{1,0:T(8,128)(2,1)S(1)}, u32[]{:S(2)}, u32[]{:S(2)}) collective-permute-start(bf16[256,768]{1,0:T(8,128)(2,1)S(1)} %get-tuple-element.88.refs_2_), channel_id=1, source_target_pairs={{0,2},{1,3},{2,0},{3,1},{4,6},{5,7},{6,4},{7,5},{8,10},{9,11},{10,... | collective-permute-start | bytes 1179656 | tf_op jit(solution)/shard_map/ppermute | solution.py:23
  26.0 1.9 %collective-permute-start.5 = (bf16[128,768]{1,0:T(8,128)(2,1)S(1)}, bf16[128,768]{1,0:T(8,128)(2,1)S(1)}, u32[]{:S(2)}, u32[]{:S(2)}) collective-permute-start(bf16[128,768]{1,0:T(8,128)(2,1)S(1)} %D0_top.1.refs_0_.refs_5_), channel_id=1, source_target_pairs={{0,1},{1,0},{2,3},{3,2},{4,5},{5,4},{6,7},{7,6},{8,9},{9,8},{10,11... | collective-permute-start | bytes 589832 | tf_op jit(solution)/shard_map/ppermute | solution.py:23
  26.0 7.4 %collective-permute-start.7 = (bf16[128,768]{1,0:T(8,128)(2,1)S(1)}, bf16[128,768]{1,0:T(8,128)(2,1)S(1)}, u32[]{:S(2)}, u32[]{:S(2)}) collective-permute-start(bf16[128,768]{1,0:T(8,128)(2,1)S(1)} %get-tuple-element.90.refs_2_), channel_id=1, source_target_pairs={{0,4},{1,5},{2,6},{3,7},{4,0},{5,1},{6,2},{7,3},{8,12},{9,13},{10,... | collective-permute-start | bytes 589832 | tf_op jit(solution)/shard_map/ppermute | solution.py:23
  28.7 8.4 %collective-permute-start.8 = (bf16[512,256]{1,0:T(8,128)(2,1)S(1)}, bf16[512,256]{1,0:T(8,128)(2,1)S(1)}, u32[]{:S(2)}, u32[]{:S(2)}) collective-permute-start(bf16[512,256]{1,0:T(8,128)(2,1)S(1)} %get-tuple-element.91), channel_id=1, source_target_pairs={{0,8},{8,0},{16,24},{24,16},{1,9},{9,1},{17,25},{25,17},{2,10},{10... | collective-permute-start | bytes 786440 | tf_op jit(solution)/shard_map/ppermute | solution.py:23
  31.2 11.4 %collective-permute-start.10 = (bf16[256,768]{1,0:T(8,128)(2,1)S(1)}, bf16[256,768]{1,0:T(8,128)(2,1)S(1)}, u32[]{:S(2)}, u32[]{:S(2)}) collective-permute-start(bf16[256,768]{1,0:T(8,128)(2,1)S(1)} %get-tuple-element.94.refs_2_), channel_id=1, source_target_pairs={{0,4},{1,5},{2,6},{3,7},{4,0},{5,1},{6,2},{7,3},{8,12},{9,13},{10,... | collective-permute-start | bytes 1179656 | tf_op jit(solution)/shard_map/ppermute | solution.py:23
  34.7 2.5 %collective-permute-start.9 = (bf16[128,768]{1,0:T(8,128)(2,1)S(1)}, bf16[128,768]{1,0:T(8,128)(2,1)S(1)}, u32[]{:S(2)}, u32[]{:S(2)}) collective-permute-start(bf16[128,768]{1,0:T(8,128)(2,1)S(1)} %D1_top.1.refs_0_.refs_5_), channel_id=1, source_target_pairs={{0,1},{1,0},{2,3},{3,2},{4,5},{5,4},{6,7},{7,6},{8,9},{9,8},{10,11... | collective-permute-start | bytes 589832 | tf_op jit(solution)/shard_map/ppermute | solution.py:23
  37.9 11.0 %collective-permute-start.11 = (bf16[512,256]{1,0:T(8,128)(2,1)S(1)}, bf16[512,256]{1,0:T(8,128)(2,1)S(1)}, u32[]{:S(2)}, u32[]{:S(2)}) collective-permute-start(bf16[512,256]{1,0:T(8,128)(2,1)S(1)} %get-tuple-element.97), channel_id=1, source_target_pairs={{0,8},{8,0},{16,24},{24,16},{1,9},{9,1},{17,25},{25,17},{2,10},{10... | collective-permute-start | bytes 786440 | tf_op jit(solution)/shard_map/ppermute | solution.py:23
  39.5 11.9 %collective-permute-start.12 = (bf16[256,256]{1,0:T(8,128)(2,1)S(1)}, bf16[256,256]{1,0:T(8,128)(2,1)S(1)}, u32[]{:S(2)}, u32[]{:S(2)}) collective-permute-start(bf16[256,256]{1,0:T(8,128)(2,1)S(1)} %get-tuple-element.99), channel_id=1, source_target_pairs={{0,16},{8,24},{16,0},{24,8},{1,17},{9,25},{17,1},{25,9},{2,18},{10... | collective-permute-start | bytes 393224 | tf_op jit(solution)/shard_map/ppermute | solution.py:23
  43.8 8.4 %collective-permute-start.13 = (bf16[256,768]{1,0:T(8,128)(2,1)S(1)}, bf16[256,768]{1,0:T(8,128)(2,1)S(1)}, u32[]{:S(2)}, u32[]{:S(2)}) collective-permute-start(bf16[256,768]{1,0:T(8,128)(2,1)S(1)} %D2_top.1.refs_0_.refs_5_), channel_id=1, source_target_pairs={{0,1},{1,0},{2,3},{3,2},{4,5},{5,4},{6,7},{7,6},{8,9},{9,8},{10,11... | collective-permute-start | bytes 1179656 | tf_op jit(solution)/shard_map/ppermute | solution.py:23
  44.5 12.8 %collective-permute-start.14 = (bf16[512,256]{1,0:T(8,128)(2,1)S(1)}, bf16[512,256]{1,0:T(8,128)(2,1)S(1)}, u32[]{:S(2)}, u32[]{:S(2)}) collective-permute-start(bf16[512,256]{1,0:T(8,128)(2,1)S(1)} %get-tuple-element.103), channel_id=1, source_target_pairs={{0,8},{8,0},{16,24},{24,16},{1,9},{9,1},{17,25},{25,17},{2,10},{10... | collective-permute-start | bytes 786440 | tf_op jit(solution)/shard_map/ppermute | solution.py:23
  48.9 11.2 %collective-permute-start.15 = (bf16[256,256]{1,0:T(8,128)(2,1)S(1)}, bf16[256,256]{1,0:T(8,128)(2,1)S(1)}, u32[]{:S(2)}, u32[]{:S(2)}) collective-permute-start(bf16[256,256]{1,0:T(8,128)(2,1)S(1)} %get-tuple-element.105), channel_id=1, source_target_pairs={{0,16},{8,24},{16,0},{24,8},{1,17},{9,25},{17,1},{25,9},{2,18},{10... | collective-permute-start | bytes 393224 | tf_op jit(solution)/shard_map/ppermute | solution.py:23
  53.1 7.8 %collective-permute-start.16 = (bf16[512,128]{1,0:T(8,128)(2,1)S(1)}, bf16[512,128]{1,0:T(8,128)(2,1)S(1)}, u32[]{:S(2)}, u32[]{:S(2)}) collective-permute-start(bf16[512,128]{1,0:T(8,128)(2,1)S(1)} %get-tuple-element.108), channel_id=1, source_target_pairs={{0,8},{8,0},{16,24},{24,16},{1,9},{9,1},{17,25},{25,17},{2,10},{10... | collective-permute-start | bytes 393224 | tf_op jit(solution)/shard_map/ppermute | solution.py:23
  56.4 9.6 %collective-permute-start.17 = (bf16[512,128]{1,0:T(8,128)(2,1)S(1)}, bf16[512,128]{1,0:T(8,128)(2,1)S(1)}, u32[]{:S(2)}, u32[]{:S(2)}) collective-permute-start(bf16[512,128]{1,0:T(8,128)(2,1)S(1)} %get-tuple-element.110), channel_id=1, source_target_pairs={{0,8},{8,0},{16,24},{24,16},{1,9},{9,1},{17,25},{25,17},{2,10},{10... | collective-permute-start | bytes 393224 | tf_op jit(solution)/shard_map/ppermute | solution.py:23
  57.4 9.1 %collective-permute-start.18 = (bf16[256,256]{1,0:T(8,128)(2,1)S(1)}, bf16[256,256]{1,0:T(8,128)(2,1)S(1)}, u32[]{:S(2)}, u32[]{:S(2)}) collective-permute-start(bf16[256,256]{1,0:T(8,128)(2,1)S(1)} %get-tuple-element.112), channel_id=1, source_target_pairs={{0,16},{8,24},{16,0},{24,8},{1,17},{9,25},{17,1},{25,9},{2,18},{10... | collective-permute-start | bytes 393224 | tf_op jit(solution)/shard_map/ppermute | solution.py:23
  60.9 9.5 %collective-permute-start.19 = (bf16[256,128]{1,0:T(8,128)(2,1)S(1)}, bf16[256,128]{1,0:T(8,128)(2,1)S(1)}, u32[]{:S(2)}, u32[]{:S(2)}) collective-permute-start(bf16[256,128]{1,0:T(8,128)(2,1)S(1)} %get-tuple-element.115), channel_id=1, source_target_pairs={{0,16},{8,24},{16,0},{24,8},{1,17},{9,25},{17,1},{25,9},{2,18},{10... | collective-permute-start | bytes 196616 | tf_op jit(solution)/shard_map/ppermute | solution.py:23
  66.1 6.0 %collective-permute-start.20 = (bf16[256,128]{1,0:T(8,128)(2,1)S(1)}, bf16[256,128]{1,0:T(8,128)(2,1)S(1)}, u32[]{:S(2)}, u32[]{:S(2)}) collective-permute-start(bf16[256,128]{1,0:T(8,128)(2,1)S(1)} %get-tuple-element.118), channel_id=1, source_target_pairs={{0,16},{8,24},{16,0},{24,8},{1,17},{9,25},{17,1},{25,9},{2,18},{10... | collective-permute-start | bytes 196616 | tf_op jit(solution)/shard_map/ppermute | solution.py:23

commit v5 on v4

--- a/solution.py
+++ b/solution.py
@@ -101,10 +101,13 @@
             for number, mask in enumerate(masks)
         ]
 
+    row_copy = load(rows_in, rows)
     first = load_columns(0, width)
     blocks = load_blocks(inverse_in, inverse)
-    small = [load(rows_in, rows)]
-    small += load_blocks(coupling_in, mixed)
+    small = load_blocks(coupling_in, mixed)
+    row_copy.wait()
+    selected = selector(rows, own.shape[1])
+    chosen[...] = selected
 
     for copy in first:
         copy.wait()
@@ -121,10 +124,8 @@
         half[tile, :] = dot(inverse[tile, :], both).astype(NARROW)
     for copy in small:
         copy.wait()
-    selected = selector(rows, own.shape[1])
-    chosen[...] = selected
     boundary = dot(half[...], mixed[...], 0, 0).astype(NARROW)
-    placed = dot(boundary, selected, 1, 1).astype(NARROW)
+    placed = dot(boundary, chosen[...], 1, 1).astype(NARROW)
     own[...] = placed[:width]
     other[...] = placed[width:]
     for copy in later:

time: 73.6 us -> 73.6 us (level)
  transfers between devices with their start and end apart: 21 -> 21, of which waited for: 9 -> 9; matrix products, arithmetic and copies ran while one was open for 0% -> 0% of each run, Pallas kernels for 32% -> 33%
where the time goes in v5:
time: 73.6 us; the launch traced here: 73.5 us
  Pallas kernels  29.7 us (40%)
  starting transfers between devices  28.5 us (39%)
  waiting for transfers between devices  14 us (19%)
  between operations  1.13 us (2%)
    pallas_call x36, Pallas kernels, __call__(): pl.pallas_call(run, out_shape=[jax.ShapeDtypeStruct(shape, kind) for shap...  29.7 us
    ppermute x21, starting transfers between devices, exchange(): return lax.ppermute(value, axis, pairs)  28.5 us
    ppermute x21, waiting for transfers between devices, exchange(): return lax.ppermute(value, axis, pairs)  14 us
  transfers between devices with their start and end apart: 21, of which 9 were waited for; matrix products, arithmetic and copies ran while one was open for 0% of the time, Pallas kernels for 33%

profile of v5, /device:TPU:0, one launch (start us, length us, event | category | flops | bytes accessed | tf_op | source)
XLA Modules:
  0.0 73.5 jit_solution(15276548510822844148)
XLA Ops:
  0.0 4.6 %A0_leaf_up.1 = (bf16[256,768]{1,0:T(8,128)(2,1)S(1)}, bf16[256,768]{1,0:T(8,128)(2,1)S(1)}, bf16[1024,512]{1,0:T(8,128)(2,1)S(1)}, bf16[768,384]{1,0:T(8,128)(2...) custom-call(bf16[1024,1024]{1,0:T(8,128)(2,1)} %bitcast.12, ...), custom_call_target="tpu_custom_call" | custom-call | flops 11500000 | bytes 1 | tf_op jit(solution)/shard_map/A0_leaf_up/pallas_call | solution.py:47
  5.1 2.4 %A1_leaf_up.1 = (bf16[256,768]{1,0:T(8,128)(2,1)S(1)}, bf16[256,768]{1,0:T(8,128)(2,1)S(1)}, bf16[1024,512]{1,0:T(8,128)(2,1)S(1)}, bf16[2,768,768]{2,1,0:T(8,128)(2,1)S(1)}, bf16[1,768,768]{2,1,0:T(8,128)(2,1)S(1)}) custom-call(bf16[768,768]{1,0:T(8,128)(2,1)S(1)} %get-tuple-element.63.refs_0_.refs_5_.refs_3_, ...), custom_call_target="tpu_custom_call" | custom-call | flops 11500000 | bytes 1 | tf_op jit(solution)/shard_map/A1_leaf_up/pallas_call | solution.py:47
  7.7 0.8 %B0_front_up.1 = (bf16[128,768]{1,0:T(8,128)(2,1)S(1)}, bf16[128,768]{1,0:T(8,128)(2,1)S(1)}) custom-call(bf16[1,768,768]{2,1,0:T(8,128)(2,1)S(1)} %get-tuple-element.68.refs_0_.refs_5_, f32[8,768]{1,0:T(8,128)S(1)} %fusion.refs_1_, bf16[256,768]{1,0:T(8,128)(2,1)S(1)} %get-tuple-element.69.refs_2_, bf16[256,768]{1,0:T(8,128)(2,1)S(1)} %collective-permute-done.refs_3_, ...), custom_call_target="tpu_custom_call" | custom-call | flops 575000000 | bytes 1 | tf_op jit(solution)/shard_map/B0_front_up/pallas_call | solution.py:47
  8.5 3.0 %collective-permute-start.1 = (bf16[128,768]{1,0:T(8,128)(2,1)S(1)}, bf16[128,768]{1,0:T(8,128)(2,1)S(1)}, u32[]{:S(2)}, u32[]{:S(2)}) collective-permute-start(bf16[128,768]{1,0:T(8,128)(2,1)S(1)} %get-tuple-element.76.refs_2_), channel_id=1, source_target_pairs={{0,2},{1,3},{2,0},{3,1},{4,6},{5,7},{6,4},{7,5},{8,10},{9,11},{10,... | collective-permute-start | bytes 589832 | tf_op jit(solution)/shard_map/ppermute | solution.py:23
  11.5 3.3 %Q_products.1 = (bf16[2,768,768]{2,1,0:T(8,128)(2,1)S(1)}, bf16[1,768,768]{2,1,0:T(8,128)(2,1)S(1)}) custom-call(bf16[128,768]{1,0:T(8,128)(2,1)S(1)} %get-tuple-element.72.refs_0_.refs_6_, f32[8,768]{1,0:T(8,128)S(1)} %fusion.refs_1_, bf16[768,768]{1,0:T(8,128)(2,1)S(1)} %get-tuple-element.71.refs_4_.refs_2_, ...), custom_call_target="tpu_custom_call" | custom-call | flops 11500000 | bytes 1 | tf_op jit(solution)/shard_map/Q_products/pallas_call | solution.py:47
  14.8 0.8 %B1_front_up.1 = (bf16[128,768]{1,0:T(8,128)(2,1)S(1)}, bf16[128,768]{1,0:T(8,128)(2,1)S(1)}) custom-call(bf16[1,768,768]{2,1,0:T(8,128)(2,1)S(1)} %get-tuple-element.74.refs_0_.refs_4_, f32[8,768]{1,0:T(8,128)S(1)} %fusion.refs_1_, bf16[256,768]{1,0:T(8,128)(2,1)S(1)} %get-tuple-element.69.refs_2_, bf16[256,768]{1,0:T(8,128)(2,1)S(1)} %collective-permute-done.refs_3_, ...), custom_call_target="tpu_custom_call" | custom-call | flops 11500000 | bytes 1 | tf_op jit(solution)/shard_map/B1_front_up/pallas_call | solution.py:47
  15.7 0.9 %collective-permute-done.1.refs_3_ = bf16[128,768]{1,0:T(8,128)(2,1)S(1)} collective-permute-done((bf16[128,768]{1,0:T(8,128)(2,1)S(1)}, bf16[128,768]{1,0:T(8,128)(2,1)S(1)}, u32[]{:S(2)}, u32[]{:S(2)}) %collective-permute-start.1) | collective-permute-done | bytes 196640 | tf_op jit(solution)/shard_map/ppermute | solution.py:23
  16.9 1.8 %collective-permute-start.4 = (bf16[128,768]{1,0:T(8,128)(2,1)S(1)}, bf16[128,768]{1,0:T(8,128)(2,1)S(1)}, u32[]{:S(2)}, u32[]{:S(2)}) collective-permute-start(bf16[128,768]{1,0:T(8,128)(2,1)S(1)} %get-tuple-element.84.refs_2_), channel_id=1, source_target_pairs={{0,4},{1,5},{2,6},{3,7},{4,0},{5,1},{6,2},{7,3},{8,12},{9,13},{10,... | collective-permute-start | bytes 589832 | tf_op jit(solution)/shard_map/ppermute | solution.py:23
  18.8 1.0 %B2_front_up.1 = (bf16[256,768]{1,0:T(8,128)(2,1)S(1)}, bf16[256,768]{1,0:T(8,128)(2,1)S(1)}) custom-call(bf16[128,768]{1,0:T(8,128)(2,1)S(1)} %get-tuple-element.77.refs_0_.refs_2_, f32[8,768]{1,0:T(8,128)S(1)} %fusion.refs_1_, bf16[256,768]{1,0:T(8,128)(2,1)S(1)} %get-tuple-element.78.refs_2_, bf16[256,768]{1,0:T(8,128)(2,1)S(1)} %collective-permute-done.2.refs_3_, ...), custom_call_target="tpu_custom_call" | custom-call | flops 11500000 | bytes 1 | tf_op jit(solution)/shard_map/B2_front_up/pallas_call | solution.py:47
  19.7 1.6 %collective-permute-start.6 = (bf16[256,768]{1,0:T(8,128)(2,1)S(1)}, bf16[256,768]{1,0:T(8,128)(2,1)S(1)}, u32[]{:S(2)}, u32[]{:S(2)}) collective-permute-start(bf16[256,768]{1,0:T(8,128)(2,1)S(1)} %get-tuple-element.88.refs_2_), channel_id=1, source_target_pairs={{0,2},{1,3},{2,0},{3,1},{4,6},{5,7},{6,4},{7,5},{8,10},{9,11},{10,... | collective-permute-start | bytes 1179656 | tf_op jit(solution)/shard_map/ppermute | solution.py:23
  21.9 1.3 %G_lift.1.refs_0_.refs_2_ = bf16[1024,384]{1,0:T(8,128)(2,1)S(1)} custom-call(bf16[256,768]{1,0:T(8,128)(2,1)S(1)} %get-tuple-element.80.refs_0_.refs_6_, bf16[1024,1024]{1,0:T(8,128)(2,1)S(1)} %get-tuple-element.64.refs_1_, bf16[1024,384]{1,0:T(8,128)(2,1)S(1)} %get-tuple-element.81.refs_2_, f32[8,128]{1,0:T(8,128)S(1)} %broadcast_in_dim.4.refs_3_.refs_1_), custom_call_target="tpu_custom_call" | custom-call | flops 11500000 | bytes 1 | tf_op jit(solution)/shard_map/G_lift/pallas_call | solution.py:47
  24.7 1.3 %D0_top.1.refs_0_.refs_5_ = bf16[128,768]{1,0:T(8,128)(2,1)S(1)} custom-call(bf16[128,768]{1,0:T(8,128)(2,1)S(1)} %T0_front_solve.1.refs_0_.refs_7_, f32[8,768]{1,0:T(8,128)S(1)} %fusion.refs_1_, bf16[128,768]{1,0:T(8,128)(2,1)S(1)} %get-tuple-element.84.refs_2_, bf16[128,768]{1,0:T(8,128)(2,1)S(1)} %collective-permute-done.4.refs_3_, ...), custom_call_target="tpu_custom_call" | custom-call | flops 11500000 | bytes 1 | tf_op jit(solution)/shard_map/D0_top/pallas_call | solution.py:47
  26.1 1.9 %collective-permute-start.7 = (bf16[128,768]{1,0:T(8,128)(2,1)S(1)}, bf16[128,768]{1,0:T(8,128)(2,1)S(1)}, u32[]{:S(2)}, u32[]{:S(2)}) collective-permute-start(bf16[128,768]{1,0:T(8,128)(2,1)S(1)} %get-tuple-element.90.refs_2_), channel_id=1, source_target_pairs={{0,4},{1,5},{2,6},{3,7},{4,0},{5,1},{6,2},{7,3},{8,12},{9,13},{10,... | collective-permute-start | bytes 589832 | tf_op jit(solution)/shard_map/ppermute | solution.py:23
  27.9 0.8 %E0_down_first.1 = (bf16[512,256]{1,0:T(8,128)(2,1)S(1)}, bf16[256,384]{1,0:T(8,128)(2,1)S(1)}) custom-call(bf16[128,768]{1,0:T(8,128)(2,1)S(1)} %D0_top.1.refs_0_.refs_5_, f32[8,128]{1,0:T(8,128)S(1)} %broadcast_in_dim.4.refs_3_.refs_1_, bf16[1024,384]{1,0:T(8,128)(2,1)S(1)} %G_lift.1.refs_0_.refs_2_, ...), custom_call_target="tpu_custom_call" | custom-call | flops 11500000 | bytes 1 | tf_op jit(solution)/shard_map/E0_down_first/pallas_call | solution.py:47
  28.7 1.6 %collective-permute-start.8 = (bf16[512,256]{1,0:T(8,128)(2,1)S(1)}, bf16[512,256]{1,0:T(8,128)(2,1)S(1)}, u32[]{:S(2)}, u32[]{:S(2)}) collective-permute-start(bf16[512,256]{1,0:T(8,128)(2,1)S(1)} %get-tuple-element.91), channel_id=1, source_target_pairs={{0,8},{8,0},{16,24},{24,16},{1,9},{9,1},{17,25},{25,17},{2,10},{10... | collective-permute-start | bytes 786440 | tf_op jit(solution)/shard_map/ppermute | solution.py:23
  31.2 1.6 %collective-permute-start.10 = (bf16[256,768]{1,0:T(8,128)(2,1)S(1)}, bf16[256,768]{1,0:T(8,128)(2,1)S(1)}, u32[]{:S(2)}, u32[]{:S(2)}) collective-permute-start(bf16[256,768]{1,0:T(8,128)(2,1)S(1)} %get-tuple-element.94.refs_2_), channel_id=1, source_target_pairs={{0,4},{1,5},{2,6},{3,7},{4,0},{5,1},{6,2},{7,3},{8,12},{9,13},{10,... | collective-permute-start | bytes 1179656 | tf_op jit(solution)/shard_map/ppermute | solution.py:23
  33.4 1.3 %D1_top.1.refs_0_.refs_5_ = bf16[128,768]{1,0:T(8,128)(2,1)S(1)} custom-call(f32[512,256]{1,0:T(8,128)S(1)} %S0_down_second.1.refs_0_.refs_1_, f32[8,768]{1,0:T(8,128)S(1)} %fusion.refs_1_, bf16[128,768]{1,0:T(8,128)(2,1)S(1)} %get-tuple-element.90.refs_2_, bf16[128,768]{1,0:T(8,128)(2,1)S(1)} %collective-permute-done.7.refs_3_, ...), custom_call_target="tpu_custom_call" | custom-call | flops 11500000 | bytes 1 | tf_op jit(solution)/shard_map/D1_top/pallas_call | solution.py:47
  34.8 2.4 %collective-permute-done.8.refs_2_ = bf16[512,256]{1,0:T(8,128)(2,1)S(1)} collective-permute-done((bf16[512,256]{1,0:T(8,128)(2,1)S(1)}, bf16[512,256]{1,0:T(8,128)(2,1)S(1)}, u32[]{:S(2)}, u32[]{:S(2)}) %collective-permute-start.8) | collective-permute-done | bytes 262176 | tf_op jit(solution)/shard_map/ppermute | solution.py:23
  37.9 1.6 %collective-permute-start.11 = (bf16[512,256]{1,0:T(8,128)(2,1)S(1)}, bf16[512,256]{1,0:T(8,128)(2,1)S(1)}, u32[]{:S(2)}, u32[]{:S(2)}) collective-permute-start(bf16[512,256]{1,0:T(8,128)(2,1)S(1)} %get-tuple-element.97), channel_id=1, source_target_pairs={{0,8},{8,0},{16,24},{24,16},{1,9},{9,1},{17,25},{25,17},{2,10},{10... | collective-permute-start | bytes 786440 | tf_op jit(solution)/shard_map/ppermute | solution.py:23
  39.5 2.6 %collective-permute-start.12 = (bf16[256,256]{1,0:T(8,128)(2,1)S(1)}, bf16[256,256]{1,0:T(8,128)(2,1)S(1)}, u32[]{:S(2)}, u32[]{:S(2)}) collective-permute-start(bf16[256,256]{1,0:T(8,128)(2,1)S(1)} %get-tuple-element.99), channel_id=1, source_target_pairs={{0,16},{8,24},{16,0},{24,8},{1,17},{9,25},{17,1},{25,9},{2,18},{10... | collective-permute-start | bytes 393224 | tf_op jit(solution)/shard_map/ppermute | solution.py:23
  42.6 1.2 %D2_top.1.refs_0_.refs_5_ = bf16[256,768]{1,0:T(8,128)(2,1)S(1)} custom-call(bf16[256,768]{1,0:T(8,128)(2,1)S(1)} %T2_front_solve.1.refs_0_.refs_7_, f32[8,768]{1,0:T(8,128)S(1)} %fusion.refs_1_, bf16[256,768]{1,0:T(8,128)(2,1)S(1)} %get-tuple-element.94.refs_2_, bf16[256,768]{1,0:T(8,128)(2,1)S(1)} %collective-permute-done.10.refs_3_, ...), custom_call_target="tpu_custom_call" | custom-call | flops 11500000 | bytes 1 | tf_op jit(solution)/shard_map/D2_top/pallas_call | solution.py:47
  44.6 0.8 %collective-permute-start.14 = (bf16[512,256]{1,0:T(8,128)(2,1)S(1)}, bf16[512,256]{1,0:T(8,128)(2,1)S(1)}, u32[]{:S(2)}, u32[]{:S(2)}) collective-permute-start(bf16[512,256]{1,0:T(8,128)(2,1)S(1)} %get-tuple-element.103), channel_id=1, source_target_pairs={{0,8},{8,0},{16,24},{24,16},{1,9},{9,1},{17,25},{25,17},{2,10},{10... | collective-permute-start | bytes 786440 | tf_op jit(solution)/shard_map/ppermute | solution.py:23
  45.7 3.2 %collective-permute-done.11.refs_2_ = bf16[512,256]{1,0:T(8,128)(2,1)S(1)} collective-permute-done((bf16[512,256]{1,0:T(8,128)(2,1)S(1)}, bf16[512,256]{1,0:T(8,128)(2,1)S(1)}, u32[]{:S(2)}, u32[]{:S(2)}) %collective-permute-start.11) | collective-permute-done | bytes 262176 | tf_op jit(solution)/shard_map/ppermute | solution.py:23
  48.9 2.5 %collective-permute-start.15 = (bf16[256,256]{1,0:T(8,128)(2,1)S(1)}, bf16[256,256]{1,0:T(8,128)(2,1)S(1)}, u32[]{:S(2)}, u32[]{:S(2)}) collective-permute-start(bf16[256,256]{1,0:T(8,128)(2,1)S(1)} %get-tuple-element.105), channel_id=1, source_target_pairs={{0,16},{8,24},{16,0},{24,8},{1,17},{9,25},{17,1},{25,9},{2,18},{10... | collective-permute-start | bytes 393224 | tf_op jit(solution)/shard_map/ppermute | solution.py:23
  53.1 2.5 %collective-permute-start.16 = (bf16[512,128]{1,0:T(8,128)(2,1)S(1)}, bf16[512,128]{1,0:T(8,128)(2,1)S(1)}, u32[]{:S(2)}, u32[]{:S(2)}) collective-permute-start(bf16[512,128]{1,0:T(8,128)(2,1)S(1)} %get-tuple-element.108), channel_id=1, source_target_pairs={{0,8},{8,0},{16,24},{24,16},{1,9},{9,1},{17,25},{25,17},{2,10},{10... | collective-permute-start | bytes 393224 | tf_op jit(solution)/shard_map/ppermute | solution.py:23
  56.5 0.8 %collective-permute-done.14.refs_2_ = bf16[512,256]{1,0:T(8,128)(2,1)S(1)} collective-permute-done((bf16[512,256]{1,0:T(8,128)(2,1)S(1)}, bf16[512,256]{1,0:T(8,128)(2,1)S(1)}, u32[]{:S(2)}, u32[]{:S(2)}) %collective-permute-start.14) | collective-permute-done | bytes 262176 | tf_op jit(solution)/shard_map/ppermute | solution.py:23
  57.4 2.5 %collective-permute-start.18 = (bf16[256,256]{1,0:T(8,128)(2,1)S(1)}, bf16[256,256]{1,0:T(8,128)(2,1)S(1)}, u32[]{:S(2)}, u32[]{:S(2)}) collective-permute-start(bf16[256,256]{1,0:T(8,128)(2,1)S(1)} %get-tuple-element.112), channel_id=1, source_target_pairs={{0,16},{8,24},{16,0},{24,8},{1,17},{9,25},{17,1},{25,9},{2,18},{10... | collective-permute-start | bytes 393224 | tf_op jit(solution)/shard_map/ppermute | solution.py:23
  61.0 3.1 %collective-permute-start.19 = (bf16[256,128]{1,0:T(8,128)(2,1)S(1)}, bf16[256,128]{1,0:T(8,128)(2,1)S(1)}, u32[]{:S(2)}, u32[]{:S(2)}) collective-permute-start(bf16[256,128]{1,0:T(8,128)(2,1)S(1)} %get-tuple-element.115), channel_id=1, source_target_pairs={{0,16},{8,24},{16,0},{24,8},{1,17},{9,25},{17,1},{25,9},{2,18},{10... | collective-permute-start | bytes 196616 | tf_op jit(solution)/shard_map/ppermute | solution.py:23
  64.1 2.0 %collective-permute-done.17.refs_2_ = bf16[512,128]{1,0:T(8,128)(2,1)S(1)} collective-permute-done((bf16[512,128]{1,0:T(8,128)(2,1)S(1)}, bf16[512,128]{1,0:T(8,128)(2,1)S(1)}, u32[]{:S(2)}, u32[]{:S(2)}) %collective-permute-start.17) | collective-permute-done | bytes 131104 | tf_op jit(solution)/shard_map/ppermute | solution.py:23
  67.2 3.3 %collective-permute-done.19.refs_2_ = bf16[256,128]{1,0:T(8,128)(2,1)S(1)} collective-permute-done((bf16[256,128]{1,0:T(8,128)(2,1)S(1)}, bf16[256,128]{1,0:T(8,128)(2,1)S(1)}, u32[]{:S(2)}, u32[]{:S(2)}) %collective-permute-start.19) | collective-permute-done | bytes 65568 | tf_op jit(solution)/shard_map/ppermute | solution.py:23
  71.2 0.9 %collective-permute-done.20.refs_2_ = bf16[256,128]{1,0:T(8,128)(2,1)S(1)} collective-permute-done((bf16[256,128]{1,0:T(8,128)(2,1)S(1)}, bf16[256,128]{1,0:T(8,128)(2,1)S(1)}, u32[]{:S(2)}, u32[]{:S(2)}) %collective-permute-start.20) | collective-permute-done | bytes 65568 | tf_op jit(solution)/shard_map/ppermute | solution.py:23
  72.1 1.2 %Z22_finish.1 = (f32[256,1024]{1,0:T(8,128)}, f32[8,128]{1,0:T(8,128)}) custom-call(f32[8,128]{1,0:T(8,128)S(1)} %get-tuple-element.117.refs_0_, f32[256,128]{1,0:T(8,128)S(1)} %get-tuple-element.111.refs_0_.refs_1_, bf16[256,128]{1,0:T(8,128)(2,1)S(1)} %collective-permute-done.20.refs_2_, ...), custom_call_target="tpu_custom_call", output_to_operand_aliasing={{0}: (3, {})} | custom-call | flops 575000000 | bytes 1 | tf_op jit(solution)/shard_map/Z22_finish/pallas_call | solution.py:47
  (51 shorter events, 11.8 us)
Async XLA Ops:
  4.6 3.1 %collective-permute-start = (bf16[256,768]{1,0:T(8,128)(2,1)S(1)}, bf16[256,768]{1,0:T(8,128)(2,1)S(1)}, u32[]{:S(2)}, u32[]{:S(2)}) collective-permute-start(bf16[256,768]{1,0:T(8,128)(2,1)S(1)} %get-tuple-element.70), channel_id=1, source_target_pairs={{0,1},{1,0},{2,3},{3,2},{4,5},{5,4},{6,7},{7,6},{8,9},{9,8},{10,11... | collective-permute-start | bytes 1179656 | tf_op jit(solution)/shard_map/ppermute | solution.py:23
  5.1 2.5 %copy-start = (s32[3]{0:T(128)S(1)}, s32[3]{0:T(128)}, u32[]{:S(2)}) copy-start(s32[3]{0:T(128)} %param.12) | copy-start | bytes 40
  7.5 11.3 %collective-permute-start.2 = (bf16[256,768]{1,0:T(8,128)(2,1)S(1)}, bf16[256,768]{1,0:T(8,128)(2,1)S(1)}, u32[]{:S(2)}, u32[]{:S(2)}) collective-permute-start(bf16[256,768]{1,0:T(8,128)(2,1)S(1)} %get-tuple-element.79), channel_id=1, source_target_pairs={{0,1},{1,0},{2,3},{3,2},{4,5},{5,4},{6,7},{7,6},{8,9},{9,8},{10,11... | collective-permute-start | bytes 1179656 | tf_op jit(solution)/shard_map/ppermute | solution.py:23
  8.5 8.1 %collective-permute-start.1 = (bf16[128,768]{1,0:T(8,128)(2,1)S(1)}, bf16[128,768]{1,0:T(8,128)(2,1)S(1)}, u32[]{:S(2)}, u32[]{:S(2)}) collective-permute-start(bf16[128,768]{1,0:T(8,128)(2,1)S(1)} %get-tuple-element.76.refs_2_), channel_id=1, source_target_pairs={{0,2},{1,3},{2,0},{3,1},{4,6},{5,7},{6,4},{7,5},{8,10},{9,11},{10,... | collective-permute-start | bytes 589832 | tf_op jit(solution)/shard_map/ppermute | solution.py:23
  15.6 7.6 %collective-permute-start.3 = (bf16[128,768]{1,0:T(8,128)(2,1)S(1)}, bf16[128,768]{1,0:T(8,128)(2,1)S(1)}, u32[]{:S(2)}, u32[]{:S(2)}) collective-permute-start(bf16[128,768]{1,0:T(8,128)(2,1)S(1)} %get-tuple-element.82.refs_2_), channel_id=1, source_target_pairs={{0,2},{1,3},{2,0},{3,1},{4,6},{5,7},{6,4},{7,5},{8,10},{9,11},{10,... | collective-permute-start | bytes 589832 | tf_op jit(solution)/shard_map/ppermute | solution.py:23
  16.9 7.7 %collective-permute-start.4 = (bf16[128,768]{1,0:T(8,128)(2,1)S(1)}, bf16[128,768]{1,0:T(8,128)(2,1)S(1)}, u32[]{:S(2)}, u32[]{:S(2)}) collective-permute-start(bf16[128,768]{1,0:T(8,128)(2,1)S(1)} %get-tuple-element.84.refs_2_), channel_id=1, source_target_pairs={{0,4},{1,5},{2,6},{3,7},{4,0},{5,1},{6,2},{7,3},{8,12},{9,13},{10,... | collective-permute-start | bytes 589832 | tf_op jit(solution)/shard_map/ppermute | solution.py:23
  19.7 11.0 %collective-permute-start.6 = (bf16[256,768]{1,0:T(8,128)(2,1)S(1)}, bf16[256,768]{1,0:T(8,128)(2,1)S(1)}, u32[]{:S(2)}, u32[]{:S(2)}) collective-permute-start(bf16[256,768]{1,0:T(8,128)(2,1)S(1)} %get-tuple-element.88.refs_2_), channel_id=1, source_target_pairs={{0,2},{1,3},{2,0},{3,1},{4,6},{5,7},{6,4},{7,5},{8,10},{9,11},{10,... | collective-permute-start | bytes 1179656 | tf_op jit(solution)/shard_map/ppermute | solution.py:23
  26.0 1.9 %collective-permute-start.5 = (bf16[128,768]{1,0:T(8,128)(2,1)S(1)}, bf16[128,768]{1,0:T(8,128)(2,1)S(1)}, u32[]{:S(2)}, u32[]{:S(2)}) collective-permute-start(bf16[128,768]{1,0:T(8,128)(2,1)S(1)} %D0_top.1.refs_0_.refs_5_), channel_id=1, source_target_pairs={{0,1},{1,0},{2,3},{3,2},{4,5},{5,4},{6,7},{7,6},{8,9},{9,8},{10,11... | collective-permute-start | bytes 589832 | tf_op jit(solution)/shard_map/ppermute | solution.py:23
  26.1 7.3 %collective-permute-start.7 = (bf16[128,768]{1,0:T(8,128)(2,1)S(1)}, bf16[128,768]{1,0:T(8,128)(2,1)S(1)}, u32[]{:S(2)}, u32[]{:S(2)}) collective-permute-start(bf16[128,768]{1,0:T(8,128)(2,1)S(1)} %get-tuple-element.90.refs_2_), channel_id=1, source_target_pairs={{0,4},{1,5},{2,6},{3,7},{4,0},{5,1},{6,2},{7,3},{8,12},{9,13},{10,... | collective-permute-start | bytes 589832 | tf_op jit(solution)/shard_map/ppermute | solution.py:23
  28.7 8.4 %collective-permute-start.8 = (bf16[512,256]{1,0:T(8,128)(2,1)S(1)}, bf16[512,256]{1,0:T(8,128)(2,1)S(1)}, u32[]{:S(2)}, u32[]{:S(2)}) collective-permute-start(bf16[512,256]{1,0:T(8,128)(2,1)S(1)} %get-tuple-element.91), channel_id=1, source_target_pairs={{0,8},{8,0},{16,24},{24,16},{1,9},{9,1},{17,25},{25,17},{2,10},{10... | collective-permute-start | bytes 786440 | tf_op jit(solution)/shard_map/ppermute | solution.py:23
  31.2 11.4 %collective-permute-start.10 = (bf16[256,768]{1,0:T(8,128)(2,1)S(1)}, bf16[256,768]{1,0:T(8,128)(2,1)S(1)}, u32[]{:S(2)}, u32[]{:S(2)}) collective-permute-start(bf16[256,768]{1,0:T(8,128)(2,1)S(1)} %get-tuple-element.94.refs_2_), channel_id=1, source_target_pairs={{0,4},{1,5},{2,6},{3,7},{4,0},{5,1},{6,2},{7,3},{8,12},{9,13},{10,... | collective-permute-start | bytes 1179656 | tf_op jit(solution)/shard_map/ppermute | solution.py:23
  34.7 2.5 %collective-permute-start.9 = (bf16[128,768]{1,0:T(8,128)(2,1)S(1)}, bf16[128,768]{1,0:T(8,128)(2,1)S(1)}, u32[]{:S(2)}, u32[]{:S(2)}) collective-permute-start(bf16[128,768]{1,0:T(8,128)(2,1)S(1)} %D1_top.1.refs_0_.refs_5_), channel_id=1, source_target_pairs={{0,1},{1,0},{2,3},{3,2},{4,5},{5,4},{6,7},{7,6},{8,9},{9,8},{10,11... | collective-permute-start | bytes 589832 | tf_op jit(solution)/shard_map/ppermute | solution.py:23
  37.9 11.0 %collective-permute-start.11 = (bf16[512,256]{1,0:T(8,128)(2,1)S(1)}, bf16[512,256]{1,0:T(8,128)(2,1)S(1)}, u32[]{:S(2)}, u32[]{:S(2)}) collective-permute-start(bf16[512,256]{1,0:T(8,128)(2,1)S(1)} %get-tuple-element.97), channel_id=1, source_target_pairs={{0,8},{8,0},{16,24},{24,16},{1,9},{9,1},{17,25},{25,17},{2,10},{10... | collective-permute-start | bytes 786440 | tf_op jit(solution)/shard_map/ppermute | solution.py:23
  39.5 11.9 %collective-permute-start.12 = (bf16[256,256]{1,0:T(8,128)(2,1)S(1)}, bf16[256,256]{1,0:T(8,128)(2,1)S(1)}, u32[]{:S(2)}, u32[]{:S(2)}) collective-permute-start(bf16[256,256]{1,0:T(8,128)(2,1)S(1)} %get-tuple-element.99), channel_id=1, source_target_pairs={{0,16},{8,24},{16,0},{24,8},{1,17},{9,25},{17,1},{25,9},{2,18},{10... | collective-permute-start | bytes 393224 | tf_op jit(solution)/shard_map/ppermute | solution.py:23
  43.8 8.4 %collective-permute-start.13 = (bf16[256,768]{1,0:T(8,128)(2,1)S(1)}, bf16[256,768]{1,0:T(8,128)(2,1)S(1)}, u32[]{:S(2)}, u32[]{:S(2)}) collective-permute-start(bf16[256,768]{1,0:T(8,128)(2,1)S(1)} %D2_top.1.refs_0_.refs_5_), channel_id=1, source_target_pairs={{0,1},{1,0},{2,3},{3,2},{4,5},{5,4},{6,7},{7,6},{8,9},{9,8},{10,11... | collective-permute-start | bytes 1179656 | tf_op jit(solution)/shard_map/ppermute | solution.py:23
  44.6 12.8 %collective-permute-start.14 = (bf16[512,256]{1,0:T(8,128)(2,1)S(1)}, bf16[512,256]{1,0:T(8,128)(2,1)S(1)}, u32[]{:S(2)}, u32[]{:S(2)}) collective-permute-start(bf16[512,256]{1,0:T(8,128)(2,1)S(1)} %get-tuple-element.103), channel_id=1, source_target_pairs={{0,8},{8,0},{16,24},{24,16},{1,9},{9,1},{17,25},{25,17},{2,10},{10... | collective-permute-start | bytes 786440 | tf_op jit(solution)/shard_map/ppermute | solution.py:23
  48.9 11.2 %collective-permute-start.15 = (bf16[256,256]{1,0:T(8,128)(2,1)S(1)}, bf16[256,256]{1,0:T(8,128)(2,1)S(1)}, u32[]{:S(2)}, u32[]{:S(2)}) collective-permute-start(bf16[256,256]{1,0:T(8,128)(2,1)S(1)} %get-tuple-element.105), channel_id=1, source_target_pairs={{0,16},{8,24},{16,0},{24,8},{1,17},{9,25},{17,1},{25,9},{2,18},{10... | collective-permute-start | bytes 393224 | tf_op jit(solution)/shard_map/ppermute | solution.py:23
  53.1 7.8 %collective-permute-start.16 = (bf16[512,128]{1,0:T(8,128)(2,1)S(1)}, bf16[512,128]{1,0:T(8,128)(2,1)S(1)}, u32[]{:S(2)}, u32[]{:S(2)}) collective-permute-start(bf16[512,128]{1,0:T(8,128)(2,1)S(1)} %get-tuple-element.108), channel_id=1, source_target_pairs={{0,8},{8,0},{16,24},{24,16},{1,9},{9,1},{17,25},{25,17},{2,10},{10... | collective-permute-start | bytes 393224 | tf_op jit(solution)/shard_map/ppermute | solution.py:23
  56.5 9.6 %collective-permute-start.17 = (bf16[512,128]{1,0:T(8,128)(2,1)S(1)}, bf16[512,128]{1,0:T(8,128)(2,1)S(1)}, u32[]{:S(2)}, u32[]{:S(2)}) collective-permute-start(bf16[512,128]{1,0:T(8,128)(2,1)S(1)} %get-tuple-element.110), channel_id=1, source_target_pairs={{0,8},{8,0},{16,24},{24,16},{1,9},{9,1},{17,25},{25,17},{2,10},{10... | collective-permute-start | bytes 393224 | tf_op jit(solution)/shard_map/ppermute | solution.py:23
  57.4 9.1 %collective-permute-start.18 = (bf16[256,256]{1,0:T(8,128)(2,1)S(1)}, bf16[256,256]{1,0:T(8,128)(2,1)S(1)}, u32[]{:S(2)}, u32[]{:S(2)}) collective-permute-start(bf16[256,256]{1,0:T(8,128)(2,1)S(1)} %get-tuple-element.112), channel_id=1, source_target_pairs={{0,16},{8,24},{16,0},{24,8},{1,17},{9,25},{17,1},{25,9},{2,18},{10... | collective-permute-start | bytes 393224 | tf_op jit(solution)/shard_map/ppermute | solution.py:23
  61.0 9.5 %collective-permute-start.19 = (bf16[256,128]{1,0:T(8,128)(2,1)S(1)}, bf16[256,128]{1,0:T(8,128)(2,1)S(1)}, u32[]{:S(2)}, u32[]{:S(2)}) collective-permute-start(bf16[256,128]{1,0:T(8,128)(2,1)S(1)} %get-tuple-element.115), channel_id=1, source_target_pairs={{0,16},{8,24},{16,0},{24,8},{1,17},{9,25},{17,1},{25,9},{2,18},{10... | collective-permute-start | bytes 196616 | tf_op jit(solution)/shard_map/ppermute | solution.py:23
  66.1 6.0 %collective-permute-start.20 = (bf16[256,128]{1,0:T(8,128)(2,1)S(1)}, bf16[256,128]{1,0:T(8,128)(2,1)S(1)}, u32[]{:S(2)}, u32[]{:S(2)}) collective-permute-start(bf16[256,128]{1,0:T(8,128)(2,1)S(1)} %get-tuple-element.118), channel_id=1, source_target_pairs={{0,16},{8,24},{16,0},{24,8},{1,17},{9,25},{17,1},{25,9},{2,18},{10... | collective-permute-start | bytes 196616 | tf_op jit(solution)/shard_map/ppermute | solution.py:23

commit v6 on v4

--- a/solution.py
+++ b/solution.py
@@ -457,7 +457,7 @@
     return held["out"][None]
 
 
-ORDER = ("A0", "A1", "B0:0.5", "Q", "B1", "C0:0.5", "B2", "G", "C1", "T1", "T0", "D0", "E0", "C2", "S0", "D1", "F0:0.5", "E1", "T2", "D2", "E20", "S1", "F1", "Z0:3", "E21", "S20", "S21", "E22", "F20", "S22", "Z1", "F21", "F22", "Z20", "Z21", "Z22:0.5")
+ORDER = ("A0", "A1", "B0:0.5", "Q", "B1", "C0:0.5", "B2", "G", "C1", "T1", "T0", "D0", "E0", "C2", "S0", "D1", "F0:0.5", "E1", "T2", "D2", "E20", "S1", "F1", "E21", "Z0:3", "S20", "S21", "E22", "F20", "S22", "Z1", "F21", "F22", "Z20", "Z21", "Z22:0.5")
 
 
 def solution(mesh):

time: 73.6 us -> 80 us (1.087)
  waiting for transfers between devices: 14 us -> 21.7 us
  starting transfers between devices: 28.5 us -> 27.2 us
    ppermute x21, waiting for transfers between devices: 14 us -> 21.7 us  [exchange(): return lax.ppermute(value, axis, pairs)]
    ppermute x21, starting transfers between devices: 28.5 us -> 27.2 us  [exchange(): return lax.ppermute(value, axis, pairs)]
  transfers between devices with their start and end apart: 21 -> 21, of which waited for: 9 -> 10; matrix products, arithmetic and copies ran while one was open for 0% -> 0% of each run, Pallas kernels for 32% -> 28%
where the time goes in v6:
time: 80 us; the launch traced here: 79.8 us
  Pallas kernels  29.7 us (37%)
  starting transfers between devices  27.2 us (34%)
  waiting for transfers between devices  21.7 us (27%)
  between operations  1.13 us (1%)
    pallas_call x36, Pallas kernels, __call__(): pl.pallas_call(run, out_shape=[jax.ShapeDtypeStruct(shape, kind) for shap...  29.7 us
    ppermute x21, starting transfers between devices, exchange(): return lax.ppermute(value, axis, pairs)  27.2 us
    ppermute x21, waiting for transfers between devices, exchange(): return lax.ppermute(value, axis, pairs)  21.7 us
  transfers between devices with their start and end apart: 21, of which 10 were waited for; matrix products, arithmetic and copies ran while one was open for 0% of the time, Pallas kernels for 28%

profile of v6, /device:TPU:0, one launch (start us, length us, event | category | flops | bytes accessed | tf_op | source)
XLA Modules:
  0.0 79.8 jit_solution(2234067385829442851)
XLA Ops:
  0.0 4.5 %A0_leaf_up.1 = (bf16[256,768]{1,0:T(8,128)(2,1)S(1)}, bf16[256,768]{1,0:T(8,128)(2,1)S(1)}, bf16[1024,512]{1,0:T(8,128)(2,1)S(1)}, bf16[768,384]{1,0:T(8,128)(2...) custom-call(bf16[1024,1024]{1,0:T(8,128)(2,1)} %bitcast.12, ...), custom_call_target="tpu_custom_call" | custom-call | flops 11500000 | bytes 1 | tf_op jit(solution)/shard_map/A0_leaf_up/pallas_call | solution.py:47
  5.1 2.4 %A1_leaf_up.1 = (bf16[256,768]{1,0:T(8,128)(2,1)S(1)}, bf16[256,768]{1,0:T(8,128)(2,1)S(1)}, bf16[1024,512]{1,0:T(8,128)(2,1)S(1)}, bf16[2,768,768]{2,1,0:T(8,128)(2,1)S(1)}, bf16[1,768,768]{2,1,0:T(8,128)(2,1)S(1)}) custom-call(bf16[768,768]{1,0:T(8,128)(2,1)S(1)} %get-tuple-element.63.refs_0_.refs_5_.refs_3_, ...), custom_call_target="tpu_custom_call" | custom-call | flops 11500000 | bytes 1 | tf_op jit(solution)/shard_map/A1_leaf_up/pallas_call | solution.py:47
  8.5 3.0 %collective-permute-start.1 = (bf16[128,768]{1,0:T(8,128)(2,1)S(1)}, bf16[128,768]{1,0:T(8,128)(2,1)S(1)}, u32[]{:S(2)}, u32[]{:S(2)}) collective-permute-start(bf16[128,768]{1,0:T(8,128)(2,1)S(1)} %get-tuple-element.76.refs_2_), channel_id=1, source_target_pairs={{0,2},{1,3},{2,0},{3,1},{4,6},{5,7},{6,4},{7,5},{8,10},{9,11},{10,... | collective-permute-start | bytes 589832 | tf_op jit(solution)/shard_map/ppermute | solution.py:23
  11.5 3.3 %Q_products.1 = (bf16[2,768,768]{2,1,0:T(8,128)(2,1)S(1)}, bf16[1,768,768]{2,1,0:T(8,128)(2,1)S(1)}) custom-call(bf16[128,768]{1,0:T(8,128)(2,1)S(1)} %get-tuple-element.72.refs_0_.refs_6_, f32[8,768]{1,0:T(8,128)S(1)} %fusion.refs_1_, bf16[768,768]{1,0:T(8,128)(2,1)S(1)} %get-tuple-element.71.refs_4_.refs_2_, ...), custom_call_target="tpu_custom_call" | custom-call | flops 11500000 | bytes 1 | tf_op jit(solution)/shard_map/Q_products/pallas_call | solution.py:47
  15.7 0.9 %collective-permute-done.1.refs_3_ = bf16[128,768]{1,0:T(8,128)(2,1)S(1)} collective-permute-done((bf16[128,768]{1,0:T(8,128)(2,1)S(1)}, bf16[128,768]{1,0:T(8,128)(2,1)S(1)}, u32[]{:S(2)}, u32[]{:S(2)}) %collective-permute-start.1) | collective-permute-done | bytes 196640 | tf_op jit(solution)/shard_map/ppermute | solution.py:23
  16.9 1.8 %collective-permute-start.4 = (bf16[128,768]{1,0:T(8,128)(2,1)S(1)}, bf16[128,768]{1,0:T(8,128)(2,1)S(1)}, u32[]{:S(2)}, u32[]{:S(2)}) collective-permute-start(bf16[128,768]{1,0:T(8,128)(2,1)S(1)} %get-tuple-element.84.refs_2_), channel_id=1, source_target_pairs={{0,4},{1,5},{2,6},{3,7},{4,0},{5,1},{6,2},{7,3},{8,12},{9,13},{10,... | collective-permute-start | bytes 589832 | tf_op jit(solution)/shard_map/ppermute | solution.py:23
  18.7 1.0 %B2_front_up.1 = (bf16[256,768]{1,0:T(8,128)(2,1)S(1)}, bf16[256,768]{1,0:T(8,128)(2,1)S(1)}) custom-call(bf16[128,768]{1,0:T(8,128)(2,1)S(1)} %get-tuple-element.77.refs_0_.refs_2_, f32[8,768]{1,0:T(8,128)S(1)} %fusion.refs_1_, bf16[256,768]{1,0:T(8,128)(2,1)S(1)} %get-tuple-element.78.refs_2_, bf16[256,768]{1,0:T(8,128)(2,1)S(1)} %collective-permute-done.2.refs_3_, ...), custom_call_target="tpu_custom_call" | custom-call | flops 11500000 | bytes 1 | tf_op jit(solution)/shard_map/B2_front_up/pallas_call | solution.py:47
  19.7 1.6 %collective-permute-start.6 = (bf16[256,768]{1,0:T(8,128)(2,1)S(1)}, bf16[256,768]{1,0:T(8,128)(2,1)S(1)}, u32[]{:S(2)}, u32[]{:S(2)}) collective-permute-start(bf16[256,768]{1,0:T(8,128)(2,1)S(1)} %get-tuple-element.88.refs_2_), channel_id=1, source_target_pairs={{0,2},{1,3},{2,0},{3,1},{4,6},{5,7},{6,4},{7,5},{8,10},{9,11},{10,... | collective-permute-start | bytes 1179656 | tf_op jit(solution)/shard_map/ppermute | solution.py:23
  21.9 1.3 %G_lift.1.refs_0_.refs_2_ = bf16[1024,384]{1,0:T(8,128)(2,1)S(1)} custom-call(bf16[256,768]{1,0:T(8,128)(2,1)S(1)} %get-tuple-element.80.refs_0_.refs_6_, bf16[1024,1024]{1,0:T(8,128)(2,1)S(1)} %get-tuple-element.64.refs_1_, bf16[1024,384]{1,0:T(8,128)(2,1)S(1)} %get-tuple-element.81.refs_2_, f32[8,128]{1,0:T(8,128)S(1)} %broadcast_in_dim.4.refs_3_.refs_1_), custom_call_target="tpu_custom_call" | custom-call | flops 11500000 | bytes 1 | tf_op jit(solution)/shard_map/G_lift/pallas_call | solution.py:47
  24.6 1.3 %D0_top.1.refs_0_.refs_5_ = bf16[128,768]{1,0:T(8,128)(2,1)S(1)} custom-call(bf16[128,768]{1,0:T(8,128)(2,1)S(1)} %T0_front_solve.1.refs_0_.refs_7_, f32[8,768]{1,0:T(8,128)S(1)} %fusion.refs_1_, bf16[128,768]{1,0:T(8,128)(2,1)S(1)} %get-tuple-element.84.refs_2_, bf16[128,768]{1,0:T(8,128)(2,1)S(1)} %collective-permute-done.4.refs_3_, ...), custom_call_target="tpu_custom_call" | custom-call | flops 11500000 | bytes 1 | tf_op jit(solution)/shard_map/D0_top/pallas_call | solution.py:47
  26.0 1.9 %collective-permute-start.7 = (bf16[128,768]{1,0:T(8,128)(2,1)S(1)}, bf16[128,768]{1,0:T(8,128)(2,1)S(1)}, u32[]{:S(2)}, u32[]{:S(2)}) collective-permute-start(bf16[128,768]{1,0:T(8,128)(2,1)S(1)} %get-tuple-element.90.refs_2_), channel_id=1, source_target_pairs={{0,4},{1,5},{2,6},{3,7},{4,0},{5,1},{6,2},{7,3},{8,12},{9,13},{10,... | collective-permute-start | bytes 589832 | tf_op jit(solution)/shard_map/ppermute | solution.py:23
  27.9 0.8 %E0_down_first.1 = (bf16[512,256]{1,0:T(8,128)(2,1)S(1)}, bf16[256,384]{1,0:T(8,128)(2,1)S(1)}) custom-call(bf16[128,768]{1,0:T(8,128)(2,1)S(1)} %D0_top.1.refs_0_.refs_5_, f32[8,128]{1,0:T(8,128)S(1)} %broadcast_in_dim.4.refs_3_.refs_1_, bf16[1024,384]{1,0:T(8,128)(2,1)S(1)} %G_lift.1.refs_0_.refs_2_, ...), custom_call_target="tpu_custom_call" | custom-call | flops 11500000 | bytes 1 | tf_op jit(solution)/shard_map/E0_down_first/pallas_call | solution.py:47
  28.7 1.9 %collective-permute-done.6.refs_3_ = bf16[256,768]{1,0:T(8,128)(2,1)S(1)} collective-permute-done((bf16[256,768]{1,0:T(8,128)(2,1)S(1)}, bf16[256,768]{1,0:T(8,128)(2,1)S(1)}, u32[]{:S(2)}, u32[]{:S(2)}) %collective-permute-start.6) | collective-permute-done | bytes 393248 | tf_op jit(solution)/shard_map/ppermute | solution.py:23
  31.2 1.6 %collective-permute-start.10 = (bf16[256,768]{1,0:T(8,128)(2,1)S(1)}, bf16[256,768]{1,0:T(8,128)(2,1)S(1)}, u32[]{:S(2)}, u32[]{:S(2)}) collective-permute-start(bf16[256,768]{1,0:T(8,128)(2,1)S(1)} %get-tuple-element.94.refs_2_), channel_id=1, source_target_pairs={{0,4},{1,5},{2,6},{3,7},{4,0},{5,1},{6,2},{7,3},{8,12},{9,13},{10,... | collective-permute-start | bytes 1179656 | tf_op jit(solution)/shard_map/ppermute | solution.py:23
  32.8 1.6 %collective-permute-start.8 = (bf16[512,256]{1,0:T(8,128)(2,1)S(1)}, bf16[512,256]{1,0:T(8,128)(2,1)S(1)}, u32[]{:S(2)}, u32[]{:S(2)}) collective-permute-start(bf16[512,256]{1,0:T(8,128)(2,1)S(1)} %get-tuple-element.91), channel_id=1, source_target_pairs={{0,8},{8,0},{16,24},{24,16},{1,9},{9,1},{17,25},{25,17},{2,10},{10... | collective-permute-start | bytes 786440 | tf_op jit(solution)/shard_map/ppermute | solution.py:23
  34.7 1.3 %D1_top.1.refs_0_.refs_5_ = bf16[128,768]{1,0:T(8,128)(2,1)S(1)} custom-call(f32[512,256]{1,0:T(8,128)S(1)} %S0_down_second.1.refs_0_.refs_1_, f32[8,768]{1,0:T(8,128)S(1)} %fusion.refs_1_, bf16[128,768]{1,0:T(8,128)(2,1)S(1)} %get-tuple-element.90.refs_2_, bf16[128,768]{1,0:T(8,128)(2,1)S(1)} %collective-permute-done.7.refs_3_, ...), custom_call_target="tpu_custom_call" | custom-call | flops 11500000 | bytes 1 | tf_op jit(solution)/shard_map/D1_top/pallas_call | solution.py:47
  36.1 3.5 %collective-permute-done.8.refs_2_ = bf16[512,256]{1,0:T(8,128)(2,1)S(1)} collective-permute-done((bf16[512,256]{1,0:T(8,128)(2,1)S(1)}, bf16[512,256]{1,0:T(8,128)(2,1)S(1)}, u32[]{:S(2)}, u32[]{:S(2)}) %collective-permute-start.8) | collective-permute-done | bytes 262176 | tf_op jit(solution)/shard_map/ppermute | solution.py:23
  40.8 1.0 %collective-permute-done.10.refs_3_ = bf16[256,768]{1,0:T(8,128)(2,1)S(1)} collective-permute-done((bf16[256,768]{1,0:T(8,128)(2,1)S(1)}, bf16[256,768]{1,0:T(8,128)(2,1)S(1)}, u32[]{:S(2)}, u32[]{:S(2)}) %collective-permute-start.10) | collective-permute-done | bytes 393248 | tf_op jit(solution)/shard_map/ppermute | solution.py:23
  41.8 1.2 %D2_top.1.refs_0_.refs_5_ = bf16[256,768]{1,0:T(8,128)(2,1)S(1)} custom-call(bf16[256,768]{1,0:T(8,128)(2,1)S(1)} %T2_front_solve.1.refs_0_.refs_7_, f32[8,768]{1,0:T(8,128)S(1)} %fusion.refs_1_, bf16[256,768]{1,0:T(8,128)(2,1)S(1)} %get-tuple-element.94.refs_2_, bf16[256,768]{1,0:T(8,128)(2,1)S(1)} %collective-permute-done.10.refs_3_, ...), custom_call_target="tpu_custom_call" | custom-call | flops 11500000 | bytes 1 | tf_op jit(solution)/shard_map/D2_top/pallas_call | solution.py:47
  43.1 1.6 %collective-permute-start.11 = (bf16[512,256]{1,0:T(8,128)(2,1)S(1)}, bf16[512,256]{1,0:T(8,128)(2,1)S(1)}, u32[]{:S(2)}, u32[]{:S(2)}) collective-permute-start(bf16[512,256]{1,0:T(8,128)(2,1)S(1)} %get-tuple-element.97), channel_id=1, source_target_pairs={{0,8},{8,0},{16,24},{24,16},{1,9},{9,1},{17,25},{25,17},{2,10},{10... | collective-permute-start | bytes 786440 | tf_op jit(solution)/shard_map/ppermute | solution.py:23
  44.7 2.6 %collective-permute-start.13 = (bf16[256,256]{1,0:T(8,128)(2,1)S(1)}, bf16[256,256]{1,0:T(8,128)(2,1)S(1)}, u32[]{:S(2)}, u32[]{:S(2)}) collective-permute-start(bf16[256,256]{1,0:T(8,128)(2,1)S(1)} %get-tuple-element.100), channel_id=1, source_target_pairs={{0,16},{8,24},{16,0},{24,8},{1,17},{9,25},{17,1},{25,9},{2,18},{10... | collective-permute-start | bytes 393224 | tf_op jit(solution)/shard_map/ppermute | solution.py:23
  48.8 6.3 %collective-permute-done.11.refs_2_ = bf16[512,256]{1,0:T(8,128)(2,1)S(1)} collective-permute-done((bf16[512,256]{1,0:T(8,128)(2,1)S(1)}, bf16[512,256]{1,0:T(8,128)(2,1)S(1)}, u32[]{:S(2)}, u32[]{:S(2)}) %collective-permute-start.11) | collective-permute-done | bytes 262176 | tf_op jit(solution)/shard_map/ppermute | solution.py:23
  55.1 1.7 %collective-permute-start.15 = (bf16[256,256]{1,0:T(8,128)(2,1)S(1)}, bf16[256,256]{1,0:T(8,128)(2,1)S(1)}, u32[]{:S(2)}, u32[]{:S(2)}) collective-permute-start(bf16[256,256]{1,0:T(8,128)(2,1)S(1)} %get-tuple-element.105), channel_id=1, source_target_pairs={{0,16},{8,24},{16,0},{24,8},{1,17},{9,25},{17,1},{25,9},{2,18},{10... | collective-permute-start | bytes 393224 | tf_op jit(solution)/shard_map/ppermute | solution.py:23
  58.5 2.5 %collective-permute-start.16 = (bf16[512,128]{1,0:T(8,128)(2,1)S(1)}, bf16[512,128]{1,0:T(8,128)(2,1)S(1)}, u32[]{:S(2)}, u32[]{:S(2)}) collective-permute-start(bf16[512,128]{1,0:T(8,128)(2,1)S(1)} %get-tuple-element.108), channel_id=1, source_target_pairs={{0,8},{8,0},{16,24},{24,16},{1,9},{9,1},{17,25},{25,17},{2,10},{10... | collective-permute-start | bytes 393224 | tf_op jit(solution)/shard_map/ppermute | solution.py:23
  62.0 1.5 %collective-permute-done.14.refs_2_ = bf16[512,256]{1,0:T(8,128)(2,1)S(1)} collective-permute-done((bf16[512,256]{1,0:T(8,128)(2,1)S(1)}, bf16[512,256]{1,0:T(8,128)(2,1)S(1)}, u32[]{:S(2)}, u32[]{:S(2)}) %collective-permute-start.14) | collective-permute-done | bytes 262176 | tf_op jit(solution)/shard_map/ppermute | solution.py:23
  63.6 1.0 %collective-permute-start.18 = (bf16[256,256]{1,0:T(8,128)(2,1)S(1)}, bf16[256,256]{1,0:T(8,128)(2,1)S(1)}, u32[]{:S(2)}, u32[]{:S(2)}) collective-permute-start(bf16[256,256]{1,0:T(8,128)(2,1)S(1)} %get-tuple-element.112), channel_id=1, source_target_pairs={{0,16},{8,24},{16,0},{24,8},{1,17},{9,25},{17,1},{25,9},{2,18},{10... | collective-permute-start | bytes 393224 | tf_op jit(solution)/shard_map/ppermute | solution.py:23
  66.3 3.8 %collective-permute-start.19 = (bf16[256,128]{1,0:T(8,128)(2,1)S(1)}, bf16[256,128]{1,0:T(8,128)(2,1)S(1)}, u32[]{:S(2)}, u32[]{:S(2)}) collective-permute-start(bf16[256,128]{1,0:T(8,128)(2,1)S(1)} %get-tuple-element.115), channel_id=1, source_target_pairs={{0,16},{8,24},{16,0},{24,8},{1,17},{9,25},{17,1},{25,9},{2,18},{10... | collective-permute-start | bytes 196616 | tf_op jit(solution)/shard_map/ppermute | solution.py:23
  70.2 2.0 %collective-permute-done.17.refs_2_ = bf16[512,128]{1,0:T(8,128)(2,1)S(1)} collective-permute-done((bf16[512,128]{1,0:T(8,128)(2,1)S(1)}, bf16[512,128]{1,0:T(8,128)(2,1)S(1)}, u32[]{:S(2)}, u32[]{:S(2)}) %collective-permute-start.17) | collective-permute-done | bytes 131104 | tf_op jit(solution)/shard_map/ppermute | solution.py:23
  72.3 0.9 %collective-permute-start.20 = (bf16[256,128]{1,0:T(8,128)(2,1)S(1)}, bf16[256,128]{1,0:T(8,128)(2,1)S(1)}, u32[]{:S(2)}, u32[]{:S(2)}) collective-permute-start(bf16[256,128]{1,0:T(8,128)(2,1)S(1)} %get-tuple-element.118), channel_id=1, source_target_pairs={{0,16},{8,24},{16,0},{24,8},{1,17},{9,25},{17,1},{25,9},{2,18},{10... | collective-permute-start | bytes 196616 | tf_op jit(solution)/shard_map/ppermute | solution.py:23
  73.9 2.5 %collective-permute-done.19.refs_2_ = bf16[256,128]{1,0:T(8,128)(2,1)S(1)} collective-permute-done((bf16[256,128]{1,0:T(8,128)(2,1)S(1)}, bf16[256,128]{1,0:T(8,128)(2,1)S(1)}, u32[]{:S(2)}, u32[]{:S(2)}) %collective-permute-start.19) | collective-permute-done | bytes 65568 | tf_op jit(solution)/shard_map/ppermute | solution.py:23
  77.1 1.3 %collective-permute-done.20.refs_2_ = bf16[256,128]{1,0:T(8,128)(2,1)S(1)} collective-permute-done((bf16[256,128]{1,0:T(8,128)(2,1)S(1)}, bf16[256,128]{1,0:T(8,128)(2,1)S(1)}, u32[]{:S(2)}, u32[]{:S(2)}) %collective-permute-start.20) | collective-permute-done | bytes 65568 | tf_op jit(solution)/shard_map/ppermute | solution.py:23
  78.4 1.3 %Z22_finish.1 = (f32[256,1024]{1,0:T(8,128)}, f32[8,128]{1,0:T(8,128)}) custom-call(f32[8,128]{1,0:T(8,128)S(1)} %get-tuple-element.117.refs_0_, f32[256,128]{1,0:T(8,128)S(1)} %get-tuple-element.111.refs_0_.refs_1_, bf16[256,128]{1,0:T(8,128)(2,1)S(1)} %collective-permute-done.20.refs_2_, ...), custom_call_target="tpu_custom_call", output_to_operand_aliasing={{0}: (3, {})} | custom-call | flops 575000000 | bytes 1 | tf_op jit(solution)/shard_map/Z22_finish/pallas_call | solution.py:47
  (51 shorter events, 13.7 us)
Async XLA Ops:
  4.6 3.1 %collective-permute-start = (bf16[256,768]{1,0:T(8,128)(2,1)S(1)}, bf16[256,768]{1,0:T(8,128)(2,1)S(1)}, u32[]{:S(2)}, u32[]{:S(2)}) collective-permute-start(bf16[256,768]{1,0:T(8,128)(2,1)S(1)} %get-tuple-element.70), channel_id=1, source_target_pairs={{0,1},{1,0},{2,3},{3,2},{4,5},{5,4},{6,7},{7,6},{8,9},{9,8},{10,11... | collective-permute-start | bytes 1179656 | tf_op jit(solution)/shard_map/ppermute | solution.py:23
  5.1 2.5 %copy-start = (s32[3]{0:T(128)S(1)}, s32[3]{0:T(128)}, u32[]{:S(2)}) copy-start(s32[3]{0:T(128)} %param.12) | copy-start | bytes 40
  7.5 11.3 %collective-permute-start.2 = (bf16[256,768]{1,0:T(8,128)(2,1)S(1)}, bf16[256,768]{1,0:T(8,128)(2,1)S(1)}, u32[]{:S(2)}, u32[]{:S(2)}) collective-permute-start(bf16[256,768]{1,0:T(8,128)(2,1)S(1)} %get-tuple-element.79), channel_id=1, source_target_pairs={{0,1},{1,0},{2,3},{3,2},{4,5},{5,4},{6,7},{7,6},{8,9},{9,8},{10,11... | collective-permute-start | bytes 1179656 | tf_op jit(solution)/shard_map/ppermute | solution.py:23
  8.5 8.1 %collective-permute-start.1 = (bf16[128,768]{1,0:T(8,128)(2,1)S(1)}, bf16[128,768]{1,0:T(8,128)(2,1)S(1)}, u32[]{:S(2)}, u32[]{:S(2)}) collective-permute-start(bf16[128,768]{1,0:T(8,128)(2,1)S(1)} %get-tuple-element.76.refs_2_), channel_id=1, source_target_pairs={{0,2},{1,3},{2,0},{3,1},{4,6},{5,7},{6,4},{7,5},{8,10},{9,11},{10,... | collective-permute-start | bytes 589832 | tf_op jit(solution)/shard_map/ppermute | solution.py:23
  15.6 7.6 %collective-permute-start.3 = (bf16[128,768]{1,0:T(8,128)(2,1)S(1)}, bf16[128,768]{1,0:T(8,128)(2,1)S(1)}, u32[]{:S(2)}, u32[]{:S(2)}) collective-permute-start(bf16[128,768]{1,0:T(8,128)(2,1)S(1)} %get-tuple-element.82.refs_2_), channel_id=1, source_target_pairs={{0,2},{1,3},{2,0},{3,1},{4,6},{5,7},{6,4},{7,5},{8,10},{9,11},{10,... | collective-permute-start | bytes 589832 | tf_op jit(solution)/shard_map/ppermute | solution.py:23
  16.9 7.7 %collective-permute-start.4 = (bf16[128,768]{1,0:T(8,128)(2,1)S(1)}, bf16[128,768]{1,0:T(8,128)(2,1)S(1)}, u32[]{:S(2)}, u32[]{:S(2)}) collective-permute-start(bf16[128,768]{1,0:T(8,128)(2,1)S(1)} %get-tuple-element.84.refs_2_), channel_id=1, source_target_pairs={{0,4},{1,5},{2,6},{3,7},{4,0},{5,1},{6,2},{7,3},{8,12},{9,13},{10,... | collective-permute-start | bytes 589832 | tf_op jit(solution)/shard_map/ppermute | solution.py:23
  19.7 10.9 %collective-permute-start.6 = (bf16[256,768]{1,0:T(8,128)(2,1)S(1)}, bf16[256,768]{1,0:T(8,128)(2,1)S(1)}, u32[]{:S(2)}, u32[]{:S(2)}) collective-permute-start(bf16[256,768]{1,0:T(8,128)(2,1)S(1)} %get-tuple-element.88.refs_2_), channel_id=1, source_target_pairs={{0,2},{1,3},{2,0},{3,1},{4,6},{5,7},{6,4},{7,5},{8,10},{9,11},{10,... | collective-permute-start | bytes 1179656 | tf_op jit(solution)/shard_map/ppermute | solution.py:23
  26.0 1.9 %collective-permute-start.5 = (bf16[128,768]{1,0:T(8,128)(2,1)S(1)}, bf16[128,768]{1,0:T(8,128)(2,1)S(1)}, u32[]{:S(2)}, u32[]{:S(2)}) collective-permute-start(bf16[128,768]{1,0:T(8,128)(2,1)S(1)} %D0_top.1.refs_0_.refs_5_), channel_id=1, source_target_pairs={{0,1},{1,0},{2,3},{3,2},{4,5},{5,4},{6,7},{7,6},{8,9},{9,8},{10,11... | collective-permute-start | bytes 589832 | tf_op jit(solution)/shard_map/ppermute | solution.py:23
  26.0 8.6 %collective-permute-start.7 = (bf16[128,768]{1,0:T(8,128)(2,1)S(1)}, bf16[128,768]{1,0:T(8,128)(2,1)S(1)}, u32[]{:S(2)}, u32[]{:S(2)}) collective-permute-start(bf16[128,768]{1,0:T(8,128)(2,1)S(1)} %get-tuple-element.90.refs_2_), channel_id=1, source_target_pairs={{0,4},{1,5},{2,6},{3,7},{4,0},{5,1},{6,2},{7,3},{8,12},{9,13},{10,... | collective-permute-start | bytes 589832 | tf_op jit(solution)/shard_map/ppermute | solution.py:23
  31.2 10.7 %collective-permute-start.10 = (bf16[256,768]{1,0:T(8,128)(2,1)S(1)}, bf16[256,768]{1,0:T(8,128)(2,1)S(1)}, u32[]{:S(2)}, u32[]{:S(2)}) collective-permute-start(bf16[256,768]{1,0:T(8,128)(2,1)S(1)} %get-tuple-element.94.refs_2_), channel_id=1, source_target_pairs={{0,4},{1,5},{2,6},{3,7},{4,0},{5,1},{6,2},{7,3},{8,12},{9,13},{10,... | collective-permute-start | bytes 1179656 | tf_op jit(solution)/shard_map/ppermute | solution.py:23
  32.8 6.8 %collective-permute-start.8 = (bf16[512,256]{1,0:T(8,128)(2,1)S(1)}, bf16[512,256]{1,0:T(8,128)(2,1)S(1)}, u32[]{:S(2)}, u32[]{:S(2)}) collective-permute-start(bf16[512,256]{1,0:T(8,128)(2,1)S(1)} %get-tuple-element.91), channel_id=1, source_target_pairs={{0,8},{8,0},{16,24},{24,16},{1,9},{9,1},{17,25},{25,17},{2,10},{10... | collective-permute-start | bytes 786440 | tf_op jit(solution)/shard_map/ppermute | solution.py:23
  36.0 3.6 %collective-permute-start.9 = (bf16[128,768]{1,0:T(8,128)(2,1)S(1)}, bf16[128,768]{1,0:T(8,128)(2,1)S(1)}, u32[]{:S(2)}, u32[]{:S(2)}) collective-permute-start(bf16[128,768]{1,0:T(8,128)(2,1)S(1)} %D1_top.1.refs_0_.refs_5_), channel_id=1, source_target_pairs={{0,1},{1,0},{2,3},{3,2},{4,5},{5,4},{6,7},{7,6},{8,9},{9,8},{10,11... | collective-permute-start | bytes 589832 | tf_op jit(solution)/shard_map/ppermute | solution.py:23
  43.0 13.8 %collective-permute-start.12 = (bf16[256,768]{1,0:T(8,128)(2,1)S(1)}, bf16[256,768]{1,0:T(8,128)(2,1)S(1)}, u32[]{:S(2)}, u32[]{:S(2)}) collective-permute-start(bf16[256,768]{1,0:T(8,128)(2,1)S(1)} %D2_top.1.refs_0_.refs_5_), channel_id=1, source_target_pairs={{0,1},{1,0},{2,3},{3,2},{4,5},{5,4},{6,7},{7,6},{8,9},{9,8},{10,11... | collective-permute-start | bytes 1179656 | tf_op jit(solution)/shard_map/ppermute | solution.py:23
  43.1 12.0 %collective-permute-start.11 = (bf16[512,256]{1,0:T(8,128)(2,1)S(1)}, bf16[512,256]{1,0:T(8,128)(2,1)S(1)}, u32[]{:S(2)}, u32[]{:S(2)}) collective-permute-start(bf16[512,256]{1,0:T(8,128)(2,1)S(1)} %get-tuple-element.97), channel_id=1, source_target_pairs={{0,8},{8,0},{16,24},{24,16},{1,9},{9,1},{17,25},{25,17},{2,10},{10... | collective-permute-start | bytes 786440 | tf_op jit(solution)/shard_map/ppermute | solution.py:23
  44.7 12.7 %collective-permute-start.13 = (bf16[256,256]{1,0:T(8,128)(2,1)S(1)}, bf16[256,256]{1,0:T(8,128)(2,1)S(1)}, u32[]{:S(2)}, u32[]{:S(2)}) collective-permute-start(bf16[256,256]{1,0:T(8,128)(2,1)S(1)} %get-tuple-element.100), channel_id=1, source_target_pairs={{0,16},{8,24},{16,0},{24,8},{1,17},{9,25},{17,1},{25,9},{2,18},{10... | collective-permute-start | bytes 393224 | tf_op jit(solution)/shard_map/ppermute | solution.py:23
  48.0 15.5 %collective-permute-start.14 = (bf16[512,256]{1,0:T(8,128)(2,1)S(1)}, bf16[512,256]{1,0:T(8,128)(2,1)S(1)}, u32[]{:S(2)}, u32[]{:S(2)}) collective-permute-start(bf16[512,256]{1,0:T(8,128)(2,1)S(1)} %get-tuple-element.103), channel_id=1, source_target_pairs={{0,8},{8,0},{16,24},{24,16},{1,9},{9,1},{17,25},{25,17},{2,10},{10... | collective-permute-start | bytes 786440 | tf_op jit(solution)/shard_map/ppermute | solution.py:23
  55.1 9.7 %collective-permute-start.15 = (bf16[256,256]{1,0:T(8,128)(2,1)S(1)}, bf16[256,256]{1,0:T(8,128)(2,1)S(1)}, u32[]{:S(2)}, u32[]{:S(2)}) collective-permute-start(bf16[256,256]{1,0:T(8,128)(2,1)S(1)} %get-tuple-element.105), channel_id=1, source_target_pairs={{0,16},{8,24},{16,0},{24,8},{1,17},{9,25},{17,1},{25,9},{2,18},{10... | collective-permute-start | bytes 393224 | tf_op jit(solution)/shard_map/ppermute | solution.py:23
  58.5 7.8 %collective-permute-start.16 = (bf16[512,128]{1,0:T(8,128)(2,1)S(1)}, bf16[512,128]{1,0:T(8,128)(2,1)S(1)}, u32[]{:S(2)}, u32[]{:S(2)}) collective-permute-start(bf16[512,128]{1,0:T(8,128)(2,1)S(1)} %get-tuple-element.108), channel_id=1, source_target_pairs={{0,8},{8,0},{16,24},{24,16},{1,9},{9,1},{17,25},{25,17},{2,10},{10... | collective-permute-start | bytes 393224 | tf_op jit(solution)/shard_map/ppermute | solution.py:23
  61.9 10.3 %collective-permute-start.17 = (bf16[512,128]{1,0:T(8,128)(2,1)S(1)}, bf16[512,128]{1,0:T(8,128)(2,1)S(1)}, u32[]{:S(2)}, u32[]{:S(2)}) collective-permute-start(bf16[512,128]{1,0:T(8,128)(2,1)S(1)} %get-tuple-element.110), channel_id=1, source_target_pairs={{0,8},{8,0},{16,24},{24,16},{1,9},{9,1},{17,25},{25,17},{2,10},{10... | collective-permute-start | bytes 393224 | tf_op jit(solution)/shard_map/ppermute | solution.py:23
  63.6 9.6 %collective-permute-start.18 = (bf16[256,256]{1,0:T(8,128)(2,1)S(1)}, bf16[256,256]{1,0:T(8,128)(2,1)S(1)}, u32[]{:S(2)}, u32[]{:S(2)}) collective-permute-start(bf16[256,256]{1,0:T(8,128)(2,1)S(1)} %get-tuple-element.112), channel_id=1, source_target_pairs={{0,16},{8,24},{16,0},{24,8},{1,17},{9,25},{17,1},{25,9},{2,18},{10... | collective-permute-start | bytes 393224 | tf_op jit(solution)/shard_map/ppermute | solution.py:23
  66.3 10.1 %collective-permute-start.19 = (bf16[256,128]{1,0:T(8,128)(2,1)S(1)}, bf16[256,128]{1,0:T(8,128)(2,1)S(1)}, u32[]{:S(2)}, u32[]{:S(2)}) collective-permute-start(bf16[256,128]{1,0:T(8,128)(2,1)S(1)} %get-tuple-element.115), channel_id=1, source_target_pairs={{0,16},{8,24},{16,0},{24,8},{1,17},{9,25},{17,1},{25,9},{2,18},{10... | collective-permute-start | bytes 196616 | tf_op jit(solution)/shard_map/ppermute | solution.py:23
  72.3 6.1 %collective-permute-start.20 = (bf16[256,128]{1,0:T(8,128)(2,1)S(1)}, bf16[256,128]{1,0:T(8,128)(2,1)S(1)}, u32[]{:S(2)}, u32[]{:S(2)}) collective-permute-start(bf16[256,128]{1,0:T(8,128)(2,1)S(1)} %get-tuple-element.118), channel_id=1, source_target_pairs={{0,16},{8,24},{16,0},{24,8},{1,17},{9,25},{17,1},{25,9},{2,18},{10... | collective-permute-start | bytes 196616 | tf_op jit(solution)/shard_map/ppermute | solution.py:23
